TPU v7x, 512 devices: a whole 4x8x8 slice. The times are simulated.
512 devices in a mesh: row: 32 (over y, x), col: 16 (over z, core).
Axes of the slice: x: 4, y: 8, z: 8, core: 2. Of those that a mesh axis runs over, the one named last changes fastest.
Arguments:
- tokens: bfloat16 [2048, 4096], P('col', 'row'), may hold values from -6 to 6
- gate_weight: bfloat16 [4096, 16384], P('col', 'row'), may hold values from -0.09375 to 0.09375
- up_weight: bfloat16 [4096, 16384], P('col', 'row'), may hold values from -0.09375 to 0.09375
- gate_keep: int32 [32, 128], P('col', 'row'), may hold values from 0 to 1, as said below
- up_keep: int32 [32, 128], P('col', 'row'), may hold values from 0 to 1, as said below
- cotangent: bfloat16 [2048, 16384], P('col', 'row'), may hold values from -1.5 to 1.5
Outputs:
- hidden: bfloat16 [2048, 16384], P('col', 'row')
- grad_tokens: bfloat16 [2048, 4096], P('row', 'col')
- grad_gate: float32 [4096, 16384], P('col', 'row')
- grad_up: float32 [4096, 16384], P('col', 'row')
Inputs may be any that keep to these rules, and one draw needn't show every extreme that they name: `gate_keep`: 1 keeps a tile of 128 x 128 weights, 0 prunes it; in every tile column, each aligned group of 2 tile rows keeps exactly 1 tiles. `up_keep`: 1 keeps a tile of 128 x 128 weights, 0 prunes it; in every tile column, each aligned group of 2 tile rows keeps exactly 1 tiles.
All inputs are finite; a program needn't handle non-finite values.
Results may differ from a plain program's by a relative error of at most 0.0049.
Values may be sent and summed in bfloat16 or wider, within the bound.
No kernel may reach another device: no remote copies, remote signals or barrier semaphores. Data moves between devices by JAX's collectives and lax.ppermute only.
A program may use at most 64 MiB of HBM per device.

v0:
```python
import jax
import jax.numpy as jnp
from jax import lax
from jax.sharding import PartitionSpec as P

BLOCK = 128


def spread(tile_keep):
    return jnp.repeat(jnp.repeat(tile_keep, BLOCK, 0), BLOCK, 1).astype(jnp.bfloat16)


def shards(tokens, gate_weight, up_weight, gate_keep, up_keep, cotangent):
    gate_mask = spread(gate_keep)
    up_mask = spread(up_keep)
    pruned_gate = gate_weight * gate_mask
    pruned_up = up_weight * up_mask
    contract_last = (((1,), (1,)), ((), ()))
    contract_first = (((0,), (0,)), ((), ()))
    rows_full = lax.all_gather(tokens, "row", axis=1, tiled=True)
    columns_all = lax.all_to_all(rows_full, "col", split_axis=1, concat_axis=0, tiled=True)
    gate = jnp.dot(
        rows_full,
        lax.all_gather(pruned_gate, "col", axis=0, tiled=True),
        preferred_element_type=jnp.float32,
    )
    up = jnp.dot(
        rows_full,
        lax.all_gather(pruned_up, "col", axis=0, tiled=True),
        preferred_element_type=jnp.float32,
    )
    sigmoid_gate = jax.nn.sigmoid(gate)
    activated = gate * sigmoid_gate
    hidden = (activated * up).astype(jnp.bfloat16)
    grad_out = cotangent.astype(jnp.float32)
    d_gate = (grad_out * up * sigmoid_gate * (1.0 + gate * (1.0 - sigmoid_gate))).astype(
        jnp.bfloat16
    )
    d_up = (grad_out * activated).astype(jnp.bfloat16)
    gate_all, up_all = (
        lax.all_gather(d_gate, "col", axis=0, tiled=True),
        lax.all_gather(d_up, "col", axis=0, tiled=True),
    )
    grad_gate = lax.dot_general(
        columns_all, gate_all, contract_first, preferred_element_type=jnp.float32
    )
    grad_up = lax.dot_general(
        columns_all, up_all, contract_first, preferred_element_type=jnp.float32
    )
    rows_term = lax.dot_general(
        gate_all, pruned_gate, contract_last, preferred_element_type=jnp.float32
    )
    grad_sum = lax.psum_scatter(
        rows_term
        + lax.dot_general(up_all, pruned_up, contract_last, preferred_element_type=jnp.float32),
        "row",
        scatter_dimension=0,
        tiled=True,
    )
    grad_gate = grad_gate * gate_mask.astype(jnp.float32)
    grad_up = grad_up * up_mask.astype(jnp.float32)
    return (hidden, grad_sum.astype(jnp.bfloat16), grad_gate, grad_up)


def solution(mesh):
    return jax.shard_map(
        shards,
        mesh=mesh,
        in_specs=(
            P("col", "row"),
            P("col", "row"),
            P("col", "row"),
            P("col", "row"),
            P("col", "row"),
            P("col", "row"),
        ),
        out_specs=(P("col", "row"), P("row", "col"), P("col", "row"), P("col", "row")),
        check_vma=False,
    )
```

profile of v0, /device:TPU:1, one launch (start us, length us, event | category | flops | bytes accessed | tf_op | source)
XLA Modules:
  0.0 524.8 jit_solution(6106721523362518847)
XLA Ops:
  7.2 1.5 copy.28
  8.8 0.0 all-gather.6.cloned.1.call-start
  8.8 1.1 copy.27
  9.9 0.7 convert_element_type.43
  10.6 0.1 copy.26
  10.7 0.1 broadcast_bitcast_fusion.1
  10.8 0.7 bitcast_multiply_fusion.1
  11.6 1.1 copy.30
  12.7 0.7 convert_element_type.46
  13.3 0.1 copy.29
  13.5 0.1 broadcast_bitcast_fusion
  13.5 0.7 bitcast_multiply_fusion
  14.4 0.1 copy.31
  14.5 79.8 %all-gather.8.cloned.1.call-done = bf16[128,4096]{0,1:T(8,128)(2,1)} async-done(((bf16[128,128]{0,1:T(8,128)(2,1)}), bf16[128,4096]{0,1:T(8,128)(2,1)}) %all-gather.8.cloned.1.call-update) | async-done | bytes 1048592 | tf_op jit(solution)/shard_map/all_gather | solution.py:20
  94.3 57.3 %all-gather.6.cloned.1.call-done = bf16[4096,512]{0,1:T(8,128)(2,1)} async-done(((bf16[256,512]{0,1:T(8,128)(2,1)}), bf16[4096,512]{0,1:T(8,128)(2,1)}) %all-gather.6.cloned.1.call-update) | async-done | bytes 4194320 | tf_op jit(solution)/shard_map/all_gather | solution.py:24
  151.6 3.7 convolution_bitcast_fusion.3
  155.4 49.7 %all-gather.10.cloned.1.call-done = bf16[4096,512]{0,1:T(8,128)(2,1)} async-done(((bf16[256,512]{0,1:T(8,128)(2,1)}), bf16[4096,512]{0,1:T(8,128)(2,1)}) %all-gather.10.cloned.1.call-update) | async-done | bytes 4194320 | tf_op jit(solution)/shard_map/all_gather | solution.py:29
  205.1 4.1 fusion.4
  209.3 0.5 all-gather.14.cloned.1.call-update
  209.8 42.7 %all-gather.12.cloned.1.call-done = bf16[2048,512]{0,1:T(8,128)(2,1)} async-done(((bf16[128,512]{0,1:T(8,128)(2,1)}), bf16[2048,512]{0,1:T(8,128)(2,1)}) %all-gather.12.cloned.1.call-update) | async-done | bytes 2097168 | tf_op jit(solution)/shard_map/all_gather | solution.py:41
  252.5 2.3 fusion.7
  254.9 42.6 %all-gather.14.cloned.1.call-done = bf16[2048,512]{0,1:T(8,128)(2,1)} async-done(((bf16[128,512]{0,1:T(8,128)(2,1)}), bf16[2048,512]{0,1:T(8,128)(2,1)}) %all-gather.14.cloned.1.call-update) | async-done | bytes 2097168 | tf_op jit(solution)/shard_map/all_gather | solution.py:42
  297.4 3.7 convolution_add_fusion
  301.1 33.5 %all_to_all.19 = bf16[128,16,256]{0,2,1:T(8,128)(2,1)S(1)} all-to-all(bf16[128,16,256]{0,2,1:T(8,128)(2,1)S(1)} %bitcast.46), channel_id=1, replica_groups=mesh['row'=32,'col'=16] {'col'}, dimensions={1} | all-to-all | bytes 2097152 | tf_op jit(solution)/shard_map/all_to_all | solution.py:21
  334.6 0.5 copy.32
  335.2 0.8 copy.33
  336.0 3.3 fusion.1
  339.2 2.0 copy.34
  341.3 1.5 fusion
  342.8 2.0 copy.35
  344.9 171.6 %reduce-scatter.2.cloned.1.call-done = f32[64,256]{1,0:T(8,128)} async-done(((f32[2048,256]{1,0:T(8,128)}), f32[64,256]{1,0:T(8,128)}) %reduce-scatter.2.cloned.1.call-update) | async-done | bytes 65552 | tf_op jit(solution)/shard_map/reduce_scatter | solution.py:53
  516.5 1.5 convert_element_type.53
  (22 shorter events, 0.4 us)
Async XLA Ops:
  7.2 7.2 %copy-start.3 = (bf16[128,512]{1,0:T(8,128)(2,1)S(1)}, bf16[128,512]{1,0:T(8,128)(2,1)}, u32[]{:S(2)}) copy-start(bf16[128,512]{1,0:T(8,128)(2,1)} %param.11) | copy-start | bytes 393220
  7.2 87.1 %all-gather.8.cloned.1.call-start = ((), (), s32[]{:S(2)}) async-start(), calls=%async_computation.3 | async-start | bytes 1081344 | tf_op jit(solution)/shard_map/all_gather | solution.py:20
  8.8 142.9 %all-gather.6.cloned.1.call-start = ((), (), s32[]{:S(2)}) async-start(), calls=%async_computation.2 | async-start | bytes 4456448 | tf_op jit(solution)/shard_map/all_gather | solution.py:24
  11.5 193.6 %all-gather.10.cloned.1.call-start = ((), (), s32[]{:S(2)}) async-start(), calls=%async_computation.4 | async-start | bytes 4456448 | tf_op jit(solution)/shard_map/all_gather | solution.py:29
  14.3 238.2 %all-gather.12.cloned.1.call-start = ((), (), s32[]{:S(2)}) async-start(), calls=%async_computation.5 | async-start | bytes 2228224 | tf_op jit(solution)/shard_map/all_gather | solution.py:41
  94.3 110.8 %copy-start.1 = (bf16[128,4096]{0,1:T(8,128)(2,1)S(1)}, bf16[128,4096]{0,1:T(8,128)(2,1)}, u32[]{:S(2)}) copy-start(bf16[128,4096]{0,1:T(8,128)(2,1)} %all-gather.8.cloned.1.call-done) | copy-start | bytes 3145732
  155.3 97.2 %copy-start.2 = (bf16[256,512]{0,1:T(8,128)(2,1)S(1)}, bf16[256,512]{0,1:T(8,128)(2,1)}, u32[]{:S(2)}) copy-start(bf16[256,512]{0,1:T(8,128)(2,1)} %bitcast_multiply_fusion.1) | copy-start | bytes 786436
  209.2 88.2 %all-gather.14.cloned.1.call-start = ((), (), s32[]{:S(2)}) async-start(), calls=%async_computation.6 | async-start | bytes 2228224 | tf_op jit(solution)/shard_map/all_gather | solution.py:42
  209.8 306.7 %reduce-scatter.2.cloned.1.call-start = ((), (), s32[]{:S(2)}) async-start(), calls=%async_computation.7 | async-start | bytes 2162688 | tf_op jit(solution)/shard_map/reduce_scatter | solution.py:53
  336.0 5.3 %copy-start = (bf16[2048,512]{0,1:T(8,128)(2,1)S(1)}, bf16[2048,512]{0,1:T(8,128)(2,1)}, u32[]{:S(2)}) copy-start(bf16[2048,512]{0,1:T(8,128)(2,1)} %all-gather.14.cloned.1.call-done) | copy-start | bytes 6291460
Sparse Core Ops, SparseCore 0:
  11.7 82.5 all-gather.7
  96.9 54.6 all-gather.5
  154.2 50.8 all-gather.9
  209.3 43.1 all-gather.11
  254.4 42.9 all-gather.13
  301.7 214.7 reduce-scatter.1
where the time goes:
time: 529 us; the launch traced here: 525 us
  waiting for transfers between devices  444 us (84%)
  blocking collectives  33.5 us (6%)
  matrix products  18.6 us (4%)
  between operations  14.2 us (3%)
  local copies, waits for them, and re-layouts  9.6 us (2%)
    reduce_scatter x1, waiting for transfers between devices, shards(): lax.psum_scatter(rows_term + lax.dot_general(up_all, pruned_up, contract_...  172 us
    all_gather x1, waiting for transfers between devices, shards(): rows_full = lax.all_gather(tokens, 'row', axis=1, tiled=True)  79.8 us
    all_gather x1, waiting for transfers between devices, shards(): lax.all_gather(pruned_gate, 'col', axis=0, tiled=True)  57.3 us
    all_gather x1, waiting for transfers between devices, shards(): lax.all_gather(pruned_up, 'col', axis=0, tiled=True)  49.7 us
    all_gather x1, waiting for transfers between devices, shards(): lax.all_gather(d_gate, 'col', axis=0, tiled=True)  42.7 us
    all_gather x1, waiting for transfers between devices, shards(): lax.all_gather(d_up, 'col', axis=0, tiled=True)  42.6 us
    all_to_all x1, blocking collectives, shards(): lax.all_to_all(rows_full, 'col', split_axis=1, concat_axis=0, tiled=True)  33.5 us
  transfers between devices with their start and end apart: 6, of which 6 were waited for; matrix products, arithmetic and copies ran while one was open for 4% of the time, Pallas kernels for 0%

commit v1 on v0

v1 whole, which is shorter than its diff:
```python
import jax
import jax.numpy as jnp
from jax import lax
from jax.sharding import PartitionSpec as P

BLOCK = 128
bf16 = jnp.bfloat16
f32 = jnp.float32


def kept(weight, keep):
    first = jnp.repeat(keep[0], BLOCK)[None, :] > 0
    return jnp.where(first, weight[:BLOCK], weight[BLOCK:]), first.astype(bf16)


def shards(tokens, gate_weight, up_weight, gate_keep, up_keep, cotangent):
    rows, cols = lax.axis_size("row"), lax.axis_size("col")
    count, width = tokens.shape
    units = cotangent.shape[1]

    gate_tile, gate_first = kept(gate_weight, gate_keep)
    up_tile, up_first = kept(up_weight, up_keep)
    packed = jnp.concatenate(
        [
            gate_tile,
            up_tile,
            jnp.broadcast_to(gate_first, (8, units)),
            jnp.broadcast_to(up_first, (8, units)),
        ],
        axis=0,
    )
    weights = lax.all_gather(packed, "col", axis=0)

    copies = jnp.broadcast_to(tokens[None], (rows, count, width))
    blocks = lax.all_to_all(copies, "row", 0, 0, tiled=True)
    rows_full = blocks.transpose(1, 0, 2).reshape(count, rows * width)

    def spread(tile, first):
        both = jnp.stack([tile * first, tile * (1 - first)], axis=1)
        return both.reshape(cols * 2 * BLOCK, units)

    pruned_gate = spread(weights[:, :BLOCK], weights[:, 2 * BLOCK : 2 * BLOCK + 1])
    pruned_up = spread(weights[:, BLOCK : 2 * BLOCK], weights[:, 2 * BLOCK + 8 : 2 * BLOCK + 9])

    gate = jnp.dot(rows_full, pruned_gate, preferred_element_type=f32)
    up = jnp.dot(rows_full, pruned_up, preferred_element_type=f32)
    sigmoid_gate = jax.nn.sigmoid(gate)
    activated = gate * sigmoid_gate
    hidden = (activated * up).astype(bf16)
    grad_out = cotangent.astype(f32)
    d_gate = (grad_out * up * sigmoid_gate * (1.0 + gate * (1.0 - sigmoid_gate))).astype(bf16)
    d_up = (grad_out * activated).astype(bf16)

    both_all = lax.all_gather(jnp.concatenate([d_gate, d_up], axis=1), "col", axis=0, tiled=True)

    contract_last = (((1,), (1,)), ((), ()))
    share = lax.dot_general(
        d_gate, pruned_gate, contract_last, preferred_element_type=f32
    ) + lax.dot_general(d_up, pruned_up, contract_last, preferred_element_type=f32)
    share = share.astype(bf16).reshape(count, rows, width).transpose(1, 0, 2)
    shares = lax.all_to_all(share, "row", 0, 0, tiled=True)
    total = jnp.sum(shares.astype(f32), axis=0).astype(bf16)
    row = lax.axis_index("row")
    half = count // 2
    odd = row % 2
    pieces = []
    for flip in range(2):
        route = []
        for r in range(rows):
            for c in range(cols):
                to = (2 * c + ((r % 2) ^ flip)) * cols + r // 2
                route.append((r * cols + c, to))
        piece = jnp.where((odd ^ flip) == 1, total[half:], total[:half])
        pieces.append(lax.ppermute(piece, ("row", "col"), route))
    left = jnp.where(odd == 0, pieces[0], pieces[1])
    right = jnp.where(odd == 0, pieces[1], pieces[0])
    grad_tokens = jnp.concatenate([left, right], axis=1)

    by_col = blocks.reshape(cols, rows // cols, count, width)
    columns = lax.all_to_all(by_col, "col", 0, 0, tiled=True)
    columns = columns.transpose(0, 2, 1, 3).reshape(cols * count, (rows // cols) * width)
    grads = lax.dot_general(
        columns, both_all, (((0,), (0,)), ((), ())), preferred_element_type=f32
    )
    gate_mask = jnp.repeat(jnp.repeat(gate_keep, BLOCK, 0), BLOCK, 1).astype(f32)
    up_mask = jnp.repeat(jnp.repeat(up_keep, BLOCK, 0), BLOCK, 1).astype(f32)
    return hidden, grad_tokens, grads[:, :units] * gate_mask, grads[:, units:] * up_mask


def solution(mesh):
    return jax.shard_map(
        shards,
        mesh=mesh,
        in_specs=(P("col", "row"),) * 6,
        out_specs=(P("col", "row"), P("row", "col"), P("col", "row"), P("col", "row")),
        check_vma=False,
    )
```

time: 529 us -> 170 us (0.32)
  waiting for transfers between devices: 444 us -> 58.4 us
  starting transfers between devices: 0.24 us -> 25.1 us
    all_gather x5 -> x2, waiting for transfers between devices: 272 us -> 39 us  [the longest x1 39 us: shards(): weights = lax.all_gather(packed, 'col', axis=0)]
    reduce_scatter x1 -> x0, waiting for transfers between devices: 172 us -> none  [shards(): lax.psum_scatter(rows_term + lax.dot_general(up_all, pruned_up, contract_...]
    all_to_all x0 -> x2, waiting for transfers between devices: none -> 19.3 us  [the longest x1 19.3 us: shards(): columns = lax.all_to_all(by_col, 'col', 0, 0, tiled=True)]
    all_to_all x0 -> x2, starting transfers between devices: none -> 16.9 us  [the longest x1 10.6 us: shards(): blocks = lax.all_to_all(copies, 'row', 0, 0, tiled=True)]
    ppermute x0 -> x2, starting transfers between devices: none -> 8.02 us  [shards(): pieces.append(lax.ppermute(piece, ('row', 'col'), route))]
    dot_general x6 -> x5, matrix products: 18.6 us -> 15.3 us  [the longest x1 3.92 us: shards(): gate = jnp.dot(rows_full, pruned_gate, preferred_element_type=f32)]
  transfers between devices with their start and end apart: 6 -> 6, of which waited for: 6 -> 2; matrix products, arithmetic and copies ran while one was open for 4% -> 12% of each run, Pallas kernels for 0% -> 0%
where the time goes in v1:
time: 170 us
  waiting for transfers between devices  58.4 us (34%)
  blocking collectives  35.9 us (21%)
  starting transfers between devices  25.1 us (15%)
  matrix products  15.3 us (9%)
  between operations  14.3 us (8%)
  local copies, waits for them, and re-layouts  11.4 us (7%)
  other arithmetic  9.32 us (5%)
    all_gather x1, waiting for transfers between devices, shards(): weights = lax.all_gather(packed, 'col', axis=0)  39 us
    all_to_all x1, blocking collectives, shards(): shares = lax.all_to_all(share, 'row', 0, 0, tiled=True)  35.9 us
    all_to_all x1, waiting for transfers between devices, shards(): columns = lax.all_to_all(by_col, 'col', 0, 0, tiled=True)  19.3 us
    all_to_all x1, starting transfers between devices, shards(): blocks = lax.all_to_all(copies, 'row', 0, 0, tiled=True)  10.6 us
    ppermute x2, starting transfers between devices, shards(): pieces.append(lax.ppermute(piece, ('row', 'col'), route))  8.02 us
    all_to_all x1, starting transfers between devices, shards(): columns = lax.all_to_all(by_col, 'col', 0, 0, tiled=True)  6.32 us
    another operation x2, local copies, waits for them, and re-layouts, spread(): both = jnp.stack([tile * first, tile * (1 - first)], axis=1)  5.05 us
    unnamed x21, local copies, waits for them, and re-layouts  3.93 us
  transfers between devices with their start and end apart: 6, of which 2 were waited for; matrix products, arithmetic and copies ran while one was open for 12% of the time, Pallas kernels for 0%

profile of v1, /device:TPU:1, one launch (start us, length us, event | category | flops | bytes accessed | tf_op | source)
XLA Modules:
  0.0 169.6 jit_solution(17203621831127436835)
XLA Ops:
  7.2 0.7 compare_bitcast_fusion
  8.0 0.7 compare_bitcast_fusion.1
  8.8 1.1 slice_select_fusion
  9.9 0.7 pad_maximum_fusion.2
  10.7 0.9 copy.37
  11.5 1.2 broadcast_in_dim.53
  12.8 10.6 %all-to-all-start = ((bf16[32,128,128]{1,2,0:T(8,128)(2,1)}), bf16[32,128,128]{1,2,0:T(8,128)(2,1)}, u32[]{:S(2)}, u32[]{:S(2)}) async-start(bf16[32,128,128]{1,2,0:T(8,128)(2,1)} %broadcast_in_dim.53), calls=%async_computation | async-start | bytes 2097152 | tf_op jit(solution)/shard_map/all_to_all | solution.py:35
  23.6 39.0 %all-gather.6.cloned.1.call-done = bf16[4352,512]{1,0:T(8,128)(2,1)} async-done(((bf16[272,512]{1,0:T(8,128)(2,1)}), bf16[4352,512]{1,0:T(8,128)(2,1)}) %all-gather.6.cloned.1.call-update) | async-done | bytes 4456464 | tf_op jit(solution)/shard_map/all_gather | solution.py:32
  62.6 1.0 fusion.9
  63.7 2.5 %multiply_bitcast_fusion.3 = (bf16[16,1,128,512]{3,2,0,1:T(8,128)(2,1)S(1)}, bf16[16,1,128,512]{3,2,0,1:T(8,128)(2,1)S(1)}, bf16[16,1,128,512]{3,2,0,1:T(8,128)(2,1)S(1)}, bf16[16,1,128,512]{3,2,0,1:T(8,128)(2,1)S(1)}) fusion(bf16[16,272,512]{2,1,0:T(8,128)(2,1)} %bitcast.91, bf16[16,512]{1,0:T(8,128)(2,1)S(1)} %bitcast.93, bf16[16,512]{1,0:T(8,128)(2,1)S(1)} %bitcast.94, ...), kind=kLoop, calls=%fused_computation.7 | loop fusion | flops 4194304 | bytes 12648448 | tf_op jit(solution)/shard_map/stack | solution.py:39
  66.2 0.4 pad_maximum_fusion
  66.6 2.5 %copy.36 = bf16[16,2,128,512]{3,2,1,0:T(8,128)(2,1)} copy(bf16[16,2,128,512]{3,2,0,1:T(8,128)(2,1)S(1)} %pad_maximum_fusion) | data formatting | bytes 8388608 | tf_op jit(solution)/shard_map/stack | solution.py:39
  69.1 0.4 pad_maximum_fusion.1
  69.5 2.6 %copy.38 = bf16[16,2,128,512]{3,2,1,0:T(8,128)(2,1)} copy(bf16[16,2,128,512]{3,2,0,1:T(8,128)(2,1)S(1)} %pad_maximum_fusion.1) | data formatting | bytes 8388608 | tf_op jit(solution)/shard_map/stack | solution.py:39
  72.1 3.9 %convolution_bitcast_fusion.2 = f32[128,512]{0,1:T(8,128)S(1)} fusion(bf16[4096,512]{1,0:T(8,128)(2,1)} %bitcast.84, bf16[128,4096]{0,1:T(8,128)(2,1)} %bitcast.9), kind=kOutput, calls=%fused_computation.11 | convolution fusion | flops 536870912 | bytes 5505024 | tf_op jit(solution)/shard_map/dot_general | solution.py:45
  76.0 2.5 %fusion.6 = (bf16[128,512]{0,1:T(8,128)(2,1)S(1)}, bf16[128,512]{0,1:T(8,128)(2,1)S(1)}, bf16[128,512]{0,1:T(8,128)(2,1)S(1)}) fusion(bf16[128,512]{0,1:T(8,128)(2,1)S(1)} %copy.39, f32[128,512]{0,1:T(8,128)S(1)} %convolution_bitcast_fusion.2, bf16[4096,512]{1,0:T(8,128)(2,1)S(1)} %bitcast.86, bf16[128,4096]{0,1:T(8,128)(2,1)} %bitcast.9), kind=kOutput, calls=%fused_computation.22 | convolution fusion | flops 537919488 | bytes 6029312 | tf_op jit(solution)/shard_map/dot_general | solution.py:46
  78.6 0.7 pad_maximum_fusion.3
  79.3 3.8 %fusion.10 = f32[128,4096]{1,0:T(8,128)S(1)} fusion(bf16[128,512]{0,1:T(8,128)(2,1)S(1)} %get-tuple-element.30, bf16[4096,512]{1,0:T(8,128)(2,1)} %bitcast.85), kind=kOutput, calls=%fused_computation.52 | convolution fusion | flops 536870912 | bytes 6422528 | tf_op jit(solution)/shard_map/dot_general | solution.py:57
  83.2 1.5 fusion.1
  84.7 0.3 copy.66
  85.0 35.9 %all_to_all.15 = bf16[32,128,128]{2,1,0:T(8,128)(2,1)S(1)} all-to-all(bf16[32,128,128]{2,1,0:T(8,128)(2,1)S(1)} %bitcast.89), channel_id=1, replica_groups=mesh['row'=32,'col'=16] {'row'}, dimensions={0} | all-to-all | bytes 2097152 | tf_op jit(solution)/shard_map/all_to_all | solution.py:61
  120.9 6.3 %all-to-all-start.2 = ((bf16[16,2,128,128]{2,3,1,0:T(8,128)(2,1)}), bf16[16,2,128,128]{2,3,1,0:T(8,128)(2,1)S(1)}, u32[]{:S(2)}, u32[]{:S(2)}) async-start(bf16[16,2,128,128]{2,3,1,0:T(8,128)(2,1)} %bitcast.17), calls=%async_computation.2 | async-start | bytes 2097152 | tf_op jit(solution)/shard_map/all_to_all | solution.py:80
  127.6 0.2 reduce_sum.12
  127.8 4.9 %collective-permute-start = (bf16[64,128]{1,0:T(8,128)(2,1)S(1)}, bf16[64,128]{1,0:T(8,128)(2,1)S(1)}, u32[]{:S(2)}, u32[]{:S(2)}) collective-permute-start(bf16[64,128]{1,0:T(8,128)(2,1)S(1)} %get-tuple-element.35), channel_id=1, source_target_pairs={{0,0},{1,32},{2,64},{3,96},{4,128},{5,160},{6,192},{7,224},{8,256}... | collective-permute-start | bytes 49160 | tf_op jit(solution)/shard_map/ppermute | solution.py:74
  132.7 3.1 %collective-permute-start.1 = (bf16[64,128]{1,0:T(8,128)(2,1)S(1)}, bf16[64,128]{1,0:T(8,128)(2,1)S(1)}, u32[]{:S(2)}, u32[]{:S(2)}) collective-permute-start(bf16[64,128]{1,0:T(8,128)(2,1)S(1)} %get-tuple-element.36), channel_id=1, source_target_pairs={{0,16},{1,48},{2,80},{3,112},{4,144},{5,176},{6,208},{7,240},{8,27... | collective-permute-start | bytes 49160 | tf_op jit(solution)/shard_map/ppermute | solution.py:74
  135.8 19.3 %all-to-all-done.2 = bf16[16,2,128,128]{2,3,1,0:T(8,128)(2,1)S(1)} async-done(((bf16[16,2,128,128]{2,3,1,0:T(8,128)(2,1)}), bf16[16,2,128,128]{2,3,1,0:T(8,128)(2,1)S(1)}, u32[]{:S(2)}, u32[]{:S(2)}) %all-to-all-start.2) | async-done | bytes 1048608 | tf_op jit(solution)/shard_map/all_to_all | solution.py:80
  155.1 0.7 copy.41
  155.8 0.8 copy.44
  156.6 0.6 pad_maximum_fusion.4
  157.2 3.5 %convolution_bitcast_fusion = f32[256,1024]{0,1:T(8,128)S(1)} fusion(bf16[2048,1024]{0,1:T(8,128)(2,1)} %all-gather.4.cloned.1.call-done, bf16[32,8,16,128]{3,2,1,0:T(8,128)(2,1)S(1)} %bitcast.92), kind=kOutput, calls=%fused_computation.9 | convolution fusion | flops 1073741824 | bytes 6291456 | tf_op jit(solution)/shard_map/dot_general | solution.py:82
  160.8 1.0 copy.45
  161.8 1.0 copy.46
  (37 shorter events, 0.9 us)
Async XLA Ops:
  7.2 16.3 %copy-start.2 = (bf16[128,512]{1,0:T(8,128)(2,1)S(1)}, bf16[128,512]{1,0:T(8,128)(2,1)}, u32[]{:S(2)}) copy-start(bf16[128,512]{1,0:T(8,128)(2,1)} %param.11) | copy-start | bytes 393220
  7.2 55.5 %all-gather.6.cloned.1.call-start = ((), (), s32[]{:S(2)}) async-start(), calls=%async_computation.4 | async-start | bytes 4734976 | tf_op jit(solution)/shard_map/all_gather | solution.py:32
  12.8 59.3 %all-to-all-start = ((bf16[32,128,128]{1,2,0:T(8,128)(2,1)}), bf16[32,128,128]{1,2,0:T(8,128)(2,1)}, u32[]{:S(2)}, u32[]{:S(2)}) async-start(bf16[32,128,128]{1,2,0:T(8,128)(2,1)} %broadcast_in_dim.53), calls=%async_computation | async-start | bytes 2097152 | tf_op jit(solution)/shard_map/all_to_all | solution.py:35
  23.4 133.8 %all-gather.4.cloned.1.call-start = ((), (), s32[]{:S(2)}) async-start(), calls=%async_computation.3 | async-start | bytes 4456448 | tf_op jit(solution)/shard_map/all_gather | solution.py:54
  72.1 3.9 %copy-start = (bf16[16,2,128,512]{3,2,1,0:T(8,128)(2,1)S(1)}, bf16[16,2,128,512]{3,2,1,0:T(8,128)(2,1)}, u32[]{:S(2)}) copy-start(bf16[16,2,128,512]{3,2,1,0:T(8,128)(2,1)} %copy.38) | copy-start | bytes 12582916
  79.3 3.8 %copy-start.1 = (bf16[16,2,128,512]{3,2,1,0:T(8,128)(2,1)S(1)}, bf16[16,2,128,512]{3,2,1,0:T(8,128)(2,1)}, u32[]{:S(2)}) copy-start(bf16[16,2,128,512]{3,2,1,0:T(8,128)(2,1)} %copy.38) | copy-start | bytes 12582916
  84.7 42.6 %copy-start.3 = (s32[2,4]{1,0:T(2,128)S(1)}, s32[2,4]{1,0:T(2,128)}, u32[]{:S(2)}) copy-start(s32[2,4]{1,0:T(2,128)} %param.10) | copy-start | bytes 100
  84.7 42.6 %copy-start.4 = (s32[2,4]{1,0:T(2,128)S(1)}, s32[2,4]{1,0:T(2,128)}, u32[]{:S(2)}) copy-start(s32[2,4]{1,0:T(2,128)} %param.9) | copy-start | bytes 100
  120.9 34.2 %all-to-all-start.2 = ((bf16[16,2,128,128]{2,3,1,0:T(8,128)(2,1)}), bf16[16,2,128,128]{2,3,1,0:T(8,128)(2,1)S(1)}, u32[]{:S(2)}, u32[]{:S(2)}) async-start(bf16[16,2,128,128]{2,3,1,0:T(8,128)(2,1)} %bitcast.17), calls=%async_computation.2 | async-start | bytes 2097152 | tf_op jit(solution)/shard_map/all_to_all | solution.py:80
  127.8 28.8 %collective-permute-start = (bf16[64,128]{1,0:T(8,128)(2,1)S(1)}, bf16[64,128]{1,0:T(8,128)(2,1)S(1)}, u32[]{:S(2)}, u32[]{:S(2)}) collective-permute-start(bf16[64,128]{1,0:T(8,128)(2,1)S(1)} %get-tuple-element.35), channel_id=1, source_target_pairs={{0,0},{1,32},{2,64},{3,96},{4,128},{5,160},{6,192},{7,224},{8,256}... | collective-permute-start | bytes 49160 | tf_op jit(solution)/shard_map/ppermute | solution.py:74
  132.7 23.9 %collective-permute-start.1 = (bf16[64,128]{1,0:T(8,128)(2,1)S(1)}, bf16[64,128]{1,0:T(8,128)(2,1)S(1)}, u32[]{:S(2)}, u32[]{:S(2)}) collective-permute-start(bf16[64,128]{1,0:T(8,128)(2,1)S(1)} %get-tuple-element.36), channel_id=1, source_target_pairs={{0,16},{1,48},{2,80},{3,112},{4,144},{5,176},{6,208},{7,240},{8,27... | collective-permute-start | bytes 49160 | tf_op jit(solution)/shard_map/ppermute | solution.py:74
Sparse Core Ops, SparseCore 0:
  10.8 51.7 all-gather.5
  79.4 49.8 all-gather.3

commit v2 on v1

v2 whole, which is shorter than its diff:
```python
import jax
import jax.numpy as jnp
from jax import lax
from jax.experimental import pallas as pl
from jax.experimental.pallas import tpu as pltpu
from jax.sharding import PartitionSpec as P

BLOCK = 128
EXTRA = 16
bf16 = jnp.bfloat16
f16 = jnp.float16
f32 = jnp.float32


def exponent(largest):
    return jnp.floor(14.0 - jnp.log2(jnp.maximum(largest, 2.0**-100)))


def kept(weight, first):
    return jnp.where(first, weight[:BLOCK], weight[BLOCK:]).astype(f32)


def forward(x_ref, w_ref, grad_ref, hidden_ref, both_ref, share_ref, rows, full):
    groups, units = w_ref.shape[0], w_ref.shape[2]
    for tile in range(x_ref.shape[0]):
        rows[:, tile * BLOCK : (tile + 1) * BLOCK] = x_ref[tile]

    def expand(g, carry):
        at = pl.ds(pl.multiple_of(g * 2 * BLOCK, BLOCK), BLOCK)
        after = pl.ds(pl.multiple_of(g * 2 * BLOCK + BLOCK, BLOCK), BLOCK)
        marks = w_ref[g, 2 * BLOCK : 2 * BLOCK + EXTRA, :]
        for part in range(2):
            columns = pl.ds(part * units, units)
            tile = w_ref[g, part * BLOCK : (part + 1) * BLOCK, :]
            first = marks[part : part + 1]
            full[at, columns] = tile * first
            full[after, columns] = tile * (1 - first)
        return carry

    lax.fori_loop(0, groups, expand, 0)
    step = 256
    for n in range(0, units, step):
        gate = jnp.dot(rows[...], full[:, n : n + step], preferred_element_type=f32)
        up = jnp.dot(rows[...], full[:, units + n : units + n + step], preferred_element_type=f32)
        sigmoid_gate = jax.nn.sigmoid(gate)
        activated = gate * sigmoid_gate
        hidden_ref[:, n : n + step] = (activated * up).astype(bf16)
        grad_out = grad_ref[:, n : n + step].astype(f32)
        d_gate = grad_out * up * sigmoid_gate * (1.0 + gate * (1.0 - sigmoid_gate))
        both_ref[:, n : n + step] = d_gate.astype(bf16)
        both_ref[:, units + n : units + n + step] = (grad_out * activated).astype(bf16)

    def back(g, carry):
        at = pl.ds(pl.multiple_of(g * 2 * BLOCK, BLOCK), 2 * BLOCK)
        pair = lax.dot_general(
            both_ref[...], full[at, :], (((1,), (1,)), ((), ())), preferred_element_type=f32
        ).astype(bf16)
        share_ref[2 * g] = pair[:, :BLOCK]
        share_ref[2 * g + 1] = pair[:, BLOCK:]
        return carry

    lax.fori_loop(0, groups, back, 0)


def shards(tokens, gate_weight, up_weight, gate_keep, up_keep, cotangent):
    rows, cols = lax.axis_size("row"), lax.axis_size("col")
    count, width = tokens.shape
    units = cotangent.shape[1]

    copies = jnp.broadcast_to(tokens[None], (rows, count, width))
    blocks = lax.all_to_all(copies, "row", 0, 0, tiled=True)

    gate_first = (jnp.repeat(gate_keep[0], BLOCK) > 0)[None, :]
    up_first = (jnp.repeat(up_keep[0], BLOCK) > 0)[None, :]
    gate_tile, up_tile = kept(gate_weight, gate_first), kept(up_weight, up_first)
    power = exponent(jnp.maximum(jnp.max(jnp.abs(gate_tile)), jnp.max(jnp.abs(up_tile))))
    scale = jnp.exp2(power)
    line = lax.broadcasted_iota(jnp.int32, (EXTRA, units), 0)
    marks = jnp.where(
        line == 0,
        gate_first.astype(f32),
        jnp.where(line == 1, up_first.astype(f32), jnp.where(line == 2, power, 0.0)),
    )
    packed = jnp.concatenate([gate_tile * scale, up_tile * scale, marks], axis=0).astype(f16)
    weights = lax.all_gather(packed, "col", axis=0)
    back = jnp.exp2(-weights[:, 2 * BLOCK + 2, :1].astype(f32))[:, :, None]
    is_mark = lax.broadcasted_iota(jnp.int32, (1, 2 * BLOCK + EXTRA, 1), 1) >= 2 * BLOCK
    weights = (weights.astype(f32) * jnp.where(is_mark, 1.0, back)).astype(bf16)

    hidden, both, share = pl.pallas_call(
        forward,
        out_shape=(
            jax.ShapeDtypeStruct((count, units), bf16),
            jax.ShapeDtypeStruct((count, 2 * units), bf16),
            jax.ShapeDtypeStruct((rows, count, width), bf16),
        ),
        in_specs=[pl.BlockSpec(memory_space=pltpu.VMEM)] * 3,
        out_specs=[pl.BlockSpec(memory_space=pltpu.VMEM)] * 3,
        scratch_shapes=[
            pltpu.VMEM((count, rows * width), bf16),
            pltpu.VMEM((rows * width, 2 * units), bf16),
        ],
        compiler_params=pltpu.CompilerParams(vmem_limit_bytes=40 * 2**20),
        cost_estimate=pl.CostEstimate(
            flops=8 * count * rows * width * units, bytes_accessed=8 * 2**20, transcendentals=count * units
        ),
    )(blocks, weights, cotangent)

    by_col = blocks.reshape(cols, rows // cols, count, width)
    columns = lax.all_to_all(by_col, "col", 0, 0, tiled=True)

    shares = lax.all_to_all(share, "row", 0, 0, tiled=True)

    both = both.astype(f32)
    power = exponent(jnp.max(jnp.abs(both)))
    sent = jnp.concatenate([both * jnp.exp2(power), jnp.full((8, 2 * units), power)], axis=0)
    both_all = lax.all_gather(sent.astype(f16), "col", axis=0)
    back = jnp.exp2(-both_all[:, count, :1].astype(f32))[:, :, None]
    both_all = (both_all[:, :count].astype(f32) * back).astype(bf16)

    total = jnp.sum(shares.astype(f32), axis=0).astype(bf16)
    row = lax.axis_index("row")
    half = count // 2
    odd = row % 2
    pieces = []
    for flip in range(2):
        route = []
        for r in range(rows):
            for c in range(cols):
                to = (2 * c + ((r % 2) ^ flip)) * cols + r // 2
                route.append((r * cols + c, to))
        piece = jnp.where((odd ^ flip) == 1, total[half:], total[:half])
        pieces.append(lax.ppermute(piece, ("row", "col"), route))
    left = jnp.where(odd == 0, pieces[0], pieces[1])
    right = jnp.where(odd == 0, pieces[1], pieces[0])
    grad_tokens = jnp.concatenate([left, right], axis=1)

    columns = columns.transpose(0, 2, 1, 3).reshape(cols * count, (rows // cols) * width)
    both_all = both_all.reshape(cols * count, 2 * units)
    contract_first = (((0,), (0,)), ((), ()))
    masks = [jnp.repeat(jnp.repeat(k, BLOCK, 0), BLOCK, 1).astype(f32) for k in (gate_keep, up_keep)]
    grads = [
        lax.dot_general(
            columns, both_all[:, i * units : (i + 1) * units], contract_first, preferred_element_type=f32
        ) * masks[i]
        for i in range(2)
    ]
    return hidden, grad_tokens, grads[0], grads[1]


def solution(mesh):
    return jax.shard_map(
        shards,
        mesh=mesh,
        in_specs=(P("col", "row"),) * 6,
        out_specs=(P("col", "row"), P("row", "col"), P("col", "row"), P("col", "row")),
        check_vma=False,
    )
```

time: 170 us -> 171 us (level)
  the two profiles are of different devices: /device:TPU:1 before, /device:TPU:257 now
where the time goes in v2:
time: 171 us; the launch traced here: 170 us
  blocking collectives  64.8 us (38%)
  starting transfers between devices  45.6 us (27%)
  waiting for transfers between devices  19.3 us (11%)
  other arithmetic  13.9 us (8%)
  local copies, waits for them, and re-layouts  12.1 us (7%)
  Pallas kernels  8.27 us (5%)
  matrix products  3.13 us (2%)
  between operations  3.01 us (2%)
    all_gather x1, blocking collectives, shards(): both_all = lax.all_gather(sent.astype(f16), 'col', axis=0)  33.3 us
    all_gather x1, blocking collectives, shards(): weights = lax.all_gather(packed, 'col', axis=0)  31.5 us
    ppermute x2, starting transfers between devices, shards(): pieces.append(lax.ppermute(piece, ('row', 'col'), route))  17.6 us
    all_to_all x1, waiting for transfers between devices, shards(): columns = lax.all_to_all(by_col, 'col', 0, 0, tiled=True)  11.1 us
    all_to_all x1, starting transfers between devices, shards(): blocks = lax.all_to_all(copies, 'row', 0, 0, tiled=True)  9.67 us
    all_to_all x1, starting transfers between devices, shards(): shares = lax.all_to_all(share, 'row', 0, 0, tiled=True)  9.5 us
    all_to_all x1, starting transfers between devices, shards(): columns = lax.all_to_all(by_col, 'col', 0, 0, tiled=True)  8.79 us
    pallas_call x1, Pallas kernels, shards(): pl.pallas_call(forward, out_shape=(jax.ShapeDtypeStruct((count, units), b...  8.27 us
  transfers between devices with their start and end apart: 5, of which 2 were waited for; matrix products, arithmetic and copies ran while one was open for 12% of the time, Pallas kernels for 5%

profile of v2, /device:TPU:257, one launch (start us, length us, event | category | flops | bytes accessed | tf_op | source)
XLA Modules:
  0.0 170.1 jit_solution(6024736389371405151)
XLA Ops:
  0.7 2.0 %broadcast_in_dim.85 = bf16[32,128,128]{2,1,0:T(8,128)(2,1)} broadcast(bf16[128,128]{1,0:T(8,128)(2,1)} %param.6), dimensions={1,2} | broadcast | bytes 1081344 | tf_op jit(solution)/shard_map/broadcast_in_dim | solution.py:70
  2.7 9.7 %all-to-all-start = ((bf16[32,128,128]{2,1,0:T(8,128)(2,1)}), bf16[32,128,128]{2,1,0:T(8,128)(2,1)S(1)}, u32[]{:S(2)}, u32[]{:S(2)}) async-start(bf16[32,128,128]{2,1,0:T(8,128)(2,1)} %broadcast_in_dim.85), calls=%async_computation | async-start | bytes 2097152 | tf_op jit(solution)/shard_map/all_to_all | solution.py:71
  12.4 0.7 compare_bitcast_fusion.1
  13.1 0.7 compare_bitcast_fusion
  13.9 1.8 %fusion.22 = (f32[]{:T(128)}, f32[]{:T(128)}) fusion(bf16[256,512]{1,0:T(8,128)(2,1)} %param.7, pred[512]{0:T(512)(128)(4,1)S(1)} %get-tuple-element.31, bf16[256,512]{1,0:T(8,128)(2,1)} %param.8, pred[512]{0:T(512)(128)(4,1)S(1)} %get-tuple-element.33), kind=kLoop, calls=%fused_computation.23 | loop fusion | flops 524286 | bytes 525320 | tf_op jit(solution)/shard_map/reduce_max | solution.py:76
  17.0 1.0 fusion.26
  18.1 1.0 fusion.27
  19.3 31.5 %all-gather.3 = f16[16,272,512]{2,1,0:T(8,128)(2,1)S(1)} all-gather(f16[1,272,512]{2,1,0:T(8,128)(2,1)S(1)} %pad_maximum_fusion), channel_id=1, replica_groups=mesh['row'=32,'col'=16] {'col'}, dimensions={0}, use_global_device_ids=true | all-gather | bytes 4734976 | tf_op jit(solution)/shard_map/all_gather | solution.py:85
  50.8 2.0 %copy-done.1 = f16[16,272,512]{2,1,0:T(8,128)(2,1)} copy-done((f16[16,272,512]{2,1,0:T(8,128)(2,1)}, f16[16,272,512]{2,1,0:T(8,128)(2,1)S(1)}, u32[]{:S(2)}) %copy-start.1) | copy-done | bytes 4456472
  52.9 0.1 copy.33
  53.1 1.3 copy.27
  54.4 8.8 %all-to-all-start.2 = ((bf16[16,2,128,128]{2,3,1,0:T(8,128)(2,1)}), bf16[16,2,128,128]{2,3,1,0:T(8,128)(2,1)S(1)}, u32[]{:S(2)}, u32[]{:S(2)}) async-start(bf16[16,2,128,128]{2,3,1,0:T(8,128)(2,1)} %copy.27), calls=%async_computation.2 | async-start | bytes 2097152 | tf_op jit(solution)/shard_map/all_to_all | solution.py:110
  63.5 2.9 %multiply_convert_fusion.w_ref = bf16[16,272,512]{2,1,0:T(8,128)(2,1)S(1)} fusion(f16[16,272,512]{2,1,0:T(8,128)(2,1)} %copy-done.1, f32[16,272]{1,0:T(8,128)S(1)} %broadcast_select_fusion.4), kind=kLoop, calls=%fused_computation | loop fusion | flops 6684672 | bytes 8930304 | tf_op jit(solution)/shard_map/convert_element_type | solution.py:88
  66.4 8.3 %shard_map.93 = (bf16[128,512]{1,0:T(8,128)(2,1)}, bf16[128,1024]{1,0:T(8,128)(2,1)S(1)}, bf16[32,128,128]{2,1,0:T(8,128)(2,1)}) custom-call(bf16[32,128,128]{2,1,0:T(8,128)(2,1)S(1)} %all-to-all-done.x_ref, bf16[16,272,512]{2,1,0:T(8,128)(2,1)S(1)} %multiply_convert_fusion.w_ref, bf16[128,512]{1,0:T(8,128)(2,1)S(1)} %copy-done), custom_call_target="tpu_custom_call" | custom-call | flops 2147483648 | bytes 8388608 | tf_op jit(solution)/shard_map/pallas_call | solution.py:90
  74.7 0.6 fusion.20
  76.2 11.1 %all-to-all-done.2 = bf16[16,2,128,128]{2,3,1,0:T(8,128)(2,1)S(1)} async-done(((bf16[16,2,128,128]{2,3,1,0:T(8,128)(2,1)}), bf16[16,2,128,128]{2,3,1,0:T(8,128)(2,1)S(1)}, u32[]{:S(2)}, u32[]{:S(2)}) %all-to-all-start.2) | async-done | bytes 1048608 | tf_op jit(solution)/shard_map/all_to_all | solution.py:110
  87.3 9.5 %all-to-all-start.1 = ((bf16[32,128,128]{2,1,0:T(8,128)(2,1)}), bf16[32,128,128]{2,1,0:T(8,128)(2,1)S(1)}, u32[]{:S(2)}, u32[]{:S(2)}) async-start(bf16[32,128,128]{2,1,0:T(8,128)(2,1)} %get-tuple-element.8), calls=%async_computation.1 | async-start | bytes 2097152 | tf_op jit(solution)/shard_map/all_to_all | solution.py:112
  96.9 33.3 %all-gather.4 = f16[2176,1024]{1,0:T(8,128)(2,1)S(1)} all-gather(f16[136,1024]{1,0:T(8,128)(2,1)S(1)} %concatenate.28), channel_id=2, replica_groups=mesh['row'=32,'col'=16] {'col'}, dimensions={0}, use_global_device_ids=true | all-gather | bytes 4734976 | tf_op jit(solution)/shard_map/all_gather | solution.py:117
  130.2 2.1 %copy-done.2 = f16[2176,1024]{1,0:T(8,128)(2,1)} copy-done((f16[2176,1024]{1,0:T(8,128)(2,1)}, f16[2176,1024]{1,0:T(8,128)(2,1)S(1)}, u32[]{:S(2)}) %copy-start.2) | copy-done | bytes 4456472
  132.3 0.1 copy.34
  132.4 3.9 %multiply_convert_fusion.1 = bf16[16,128,1024]{2,1,0:T(8,128)(2,1)S(1)} fusion(f16[16,136,1024]{2,1,0:T(8,128)(2,1)} %bitcast.59, f32[16]{0:T(128)S(1)} %exponential_bitcast_fusion), kind=kLoop, calls=%fused_computation.1 | loop fusion | flops 6291456 | bytes 8388672 | tf_op jit(solution)/shard_map/convert_element_type | solution.py:119
  136.3 0.7 copy.28
  137.0 1.2 copy-done.3
  138.2 0.8 fusion.7
  139.1 0.2 reduce_sum.12
  139.2 14.3 %collective-permute-start = (bf16[64,128]{1,0:T(8,128)(2,1)S(1)}, bf16[64,128]{1,0:T(8,128)(2,1)S(1)}, u32[]{:S(2)}, u32[]{:S(2)}) collective-permute-start(bf16[64,128]{1,0:T(8,128)(2,1)S(1)} %get-tuple-element.28), channel_id=1, source_target_pairs={{0,0},{1,32},{2,64},{3,96},{4,128},{5,160},{6,192},{7,224},{8,256}... | collective-permute-start | bytes 49160 | tf_op jit(solution)/shard_map/ppermute | solution.py:133
  153.6 3.3 %collective-permute-start.1 = (bf16[64,128]{1,0:T(8,128)(2,1)S(1)}, bf16[64,128]{1,0:T(8,128)(2,1)S(1)}, u32[]{:S(2)}, u32[]{:S(2)}) collective-permute-start(bf16[64,128]{1,0:T(8,128)(2,1)S(1)} %get-tuple-element.29), channel_id=1, source_target_pairs={{0,16},{1,48},{2,80},{3,112},{4,144},{5,176},{6,208},{7,240},{8,27... | collective-permute-start | bytes 49160 | tf_op jit(solution)/shard_map/ppermute | solution.py:133
  156.9 2.3 %fusion.13 = f32[256,512]{0,1:T(8,128)S(1)} fusion(f32[256,512]{0,1:T(8,128)S(1)} %bitcast.65, bf16[2048,1024]{1,0:T(8,128)(2,1)} %bitcast.61, bf16[32,8,16,128]{3,2,1,0:T(8,128)(2,1)S(1)} %bitcast.64), kind=kOutput, calls=%fused_computation.9 | convolution fusion | flops 537001984 | bytes 4194304 | tf_op jit(solution)/shard_map/dot_general | solution.py:143
  159.3 1.0 copy.31
  160.2 1.0 copy.32
  161.2 8.2 %collective-permute-done.1 = bf16[64,128]{1,0:T(8,128)(2,1)S(1)} collective-permute-done((bf16[64,128]{1,0:T(8,128)(2,1)S(1)}, bf16[64,128]{1,0:T(8,128)(2,1)S(1)}, u32[]{:S(2)}, u32[]{:S(2)}) %collective-permute-start.1) | collective-permute-done | bytes 16416 | tf_op jit(solution)/shard_map/ppermute | solution.py:133
  169.4 0.6 pad_maximum_fusion.1
  (38 shorter events, 1.0 us)
Async XLA Ops:
  0.6 18.5 %copy-start.4 = (s32[2,4]{1,0:T(2,128)S(1)}, s32[2,4]{1,0:T(2,128)}, u32[]{:S(2)}) copy-start(s32[2,4]{1,0:T(2,128)} %param.9) | copy-start | bytes 100
  0.6 18.5 %copy-start.5 = (s32[2,4]{1,0:T(2,128)S(1)}, s32[2,4]{1,0:T(2,128)}, u32[]{:S(2)}) copy-start(s32[2,4]{1,0:T(2,128)} %param.10) | copy-start | bytes 100
  2.7 50.4 %all-to-all-start = ((bf16[32,128,128]{2,1,0:T(8,128)(2,1)}), bf16[32,128,128]{2,1,0:T(8,128)(2,1)S(1)}, u32[]{:S(2)}, u32[]{:S(2)}) async-start(bf16[32,128,128]{2,1,0:T(8,128)(2,1)} %broadcast_in_dim.85), calls=%async_computation | async-start | bytes 2097152 | tf_op jit(solution)/shard_map/all_to_all | solution.py:71
  50.8 2.0 %copy-start.1 = (f16[16,272,512]{2,1,0:T(8,128)(2,1)}, f16[16,272,512]{2,1,0:T(8,128)(2,1)S(1)}, u32[]{:S(2)}) copy-start(f16[16,272,512]{2,1,0:T(8,128)(2,1)S(1)} %all-gather.3) | copy-start | bytes 13369348
  54.4 33.0 %all-to-all-start.2 = ((bf16[16,2,128,128]{2,3,1,0:T(8,128)(2,1)}), bf16[16,2,128,128]{2,3,1,0:T(8,128)(2,1)S(1)}, u32[]{:S(2)}, u32[]{:S(2)}) async-start(bf16[16,2,128,128]{2,3,1,0:T(8,128)(2,1)} %copy.27), calls=%async_computation.2 | async-start | bytes 2097152 | tf_op jit(solution)/shard_map/all_to_all | solution.py:110
  63.5 2.9 %copy-start = (bf16[128,512]{1,0:T(8,128)(2,1)S(1)}, bf16[128,512]{1,0:T(8,128)(2,1)}, u32[]{:S(2)}) copy-start(bf16[128,512]{1,0:T(8,128)(2,1)} %grad_ref.1) | copy-start | bytes 393220
  87.3 51.7 %all-to-all-start.1 = ((bf16[32,128,128]{2,1,0:T(8,128)(2,1)}), bf16[32,128,128]{2,1,0:T(8,128)(2,1)S(1)}, u32[]{:S(2)}, u32[]{:S(2)}) async-start(bf16[32,128,128]{2,1,0:T(8,128)(2,1)} %get-tuple-element.8), calls=%async_computation.1 | async-start | bytes 2097152 | tf_op jit(solution)/shard_map/all_to_all | solution.py:112
  130.1 2.1 %copy-start.2 = (f16[2176,1024]{1,0:T(8,128)(2,1)}, f16[2176,1024]{1,0:T(8,128)(2,1)S(1)}, u32[]{:S(2)}) copy-start(f16[2176,1024]{1,0:T(8,128)(2,1)S(1)} %all-gather.4) | copy-start | bytes 13369348
  136.3 2.0 %copy-start.3 = (bf16[16,128,1024]{2,1,0:T(8,128)(2,1)}, bf16[16,128,1024]{2,1,0:T(8,128)(2,1)S(1)}, u32[]{:S(2)}) copy-start(bf16[16,128,1024]{2,1,0:T(8,128)(2,1)S(1)} %multiply_convert_fusion.1) | copy-start | bytes 12582916
  139.2 22.0 %collective-permute-start = (bf16[64,128]{1,0:T(8,128)(2,1)S(1)}, bf16[64,128]{1,0:T(8,128)(2,1)S(1)}, u32[]{:S(2)}, u32[]{:S(2)}) collective-permute-start(bf16[64,128]{1,0:T(8,128)(2,1)S(1)} %get-tuple-element.28), channel_id=1, source_target_pairs={{0,0},{1,32},{2,64},{3,96},{4,128},{5,160},{6,192},{7,224},{8,256}... | collective-permute-start | bytes 49160 | tf_op jit(solution)/shard_map/ppermute | solution.py:133
  153.6 15.9 %collective-permute-start.1 = (bf16[64,128]{1,0:T(8,128)(2,1)S(1)}, bf16[64,128]{1,0:T(8,128)(2,1)S(1)}, u32[]{:S(2)}, u32[]{:S(2)}) collective-permute-start(bf16[64,128]{1,0:T(8,128)(2,1)S(1)} %get-tuple-element.29), channel_id=1, source_target_pairs={{0,16},{1,48},{2,80},{3,112},{4,144},{5,176},{6,208},{7,240},{8,27... | collective-permute-start | bytes 49160 | tf_op jit(solution)/shard_map/ppermute | solution.py:133

commit v3 on v2

v3 whole, which is shorter than its diff:
```python
import functools

import jax
import jax.numpy as jnp
from jax import lax
from jax.experimental import pallas as pl
from jax.experimental.pallas import tpu as pltpu
from jax.sharding import PartitionSpec as P

BLOCK = 128
EXTRA = 16
SPLIT = 64
bf16 = jnp.bfloat16
f16 = jnp.float16
f32 = jnp.float32


def exponent(largest):
    return jnp.floor(14.0 - jnp.log2(jnp.maximum(largest, 2.0**-100)))


def peak(values):
    return jnp.max(jnp.max(jnp.abs(values), axis=0, keepdims=True), axis=1, keepdims=True)


def pack(gate_ref, up_ref, gate_keep, up_keep, packed_ref):
    units = gate_ref.shape[1]
    line = lax.broadcasted_iota(jnp.int32, (EXTRA, BLOCK), 0)
    tiles, marks = [], []
    for ref, keep in ((gate_ref, gate_keep), (up_ref, up_keep)):
        for j in range(units // BLOCK):
            at = slice(j * BLOCK, (j + 1) * BLOCK)
            first = keep[0, j]
            tiles.append(jnp.where(first > 0, ref[:BLOCK, at], ref[BLOCK:, at]).astype(f32))
            marks.append(first.astype(f32))
    largest = functools.reduce(jnp.maximum, [peak(tile) for tile in tiles])
    power = exponent(largest)
    scale = jnp.exp2(power)
    count = units // BLOCK
    for j in range(count):
        at = slice(j * BLOCK, (j + 1) * BLOCK)
        packed_ref[:BLOCK, at] = (tiles[j] * scale).astype(bf16)
        packed_ref[BLOCK : 2 * BLOCK, at] = (tiles[count + j] * scale).astype(bf16)
        lines = jnp.where(line == 0, marks[j], jnp.where(line == 1, marks[count + j], 0.0))
        packed_ref[2 * BLOCK :, at] = jnp.where(line == 2, power, lines).astype(bf16)


def forward(got_ref, w_ref, grad_ref, block_ref, hidden_ref, sent_ref, share_ref, rows, full, both):
    groups, units = w_ref.shape[0], w_ref.shape[2]
    count = grad_ref.shape[0]

    def expand(g, carry):
        at = pl.ds(pl.multiple_of(g * 2 * BLOCK, BLOCK), BLOCK)
        after = pl.ds(pl.multiple_of(g * 2 * BLOCK + BLOCK, BLOCK), BLOCK)
        marks = w_ref[g, 2 * BLOCK : 2 * BLOCK + EXTRA, :]
        back = jnp.exp2(-marks[2:3, :BLOCK].astype(f32)).astype(bf16)
        rows[:, at] = got_ref[2 * g, :count, :] * back
        rows[:, after] = got_ref[2 * g + 1, :count, :] * back
        for part in range(2):
            columns = pl.ds(part * units, units)
            tile = w_ref[g, part * BLOCK : (part + 1) * BLOCK, :]
            first = marks[part : part + 1]
            full[at, columns] = tile * first
            full[after, columns] = tile * (1 - first)
        return carry

    lax.fori_loop(0, groups, expand, 0)
    step = 256
    largest = jnp.zeros((1, 1), f32)
    for n in range(0, units, step):
        gate = jnp.dot(rows[...], full[:, n : n + step], preferred_element_type=f32)
        up = jnp.dot(rows[...], full[:, units + n : units + n + step], preferred_element_type=f32)
        sigmoid_gate = jax.nn.sigmoid(gate)
        activated = gate * sigmoid_gate
        hidden_ref[:, n : n + step] = (activated * up).astype(bf16)
        grad_out = grad_ref[:, n : n + step].astype(f32)
        d_gate = grad_out * up * sigmoid_gate * (1.0 + gate * (1.0 - sigmoid_gate))
        d_up = grad_out * activated
        largest = jnp.maximum(largest, jnp.maximum(peak(d_gate), peak(d_up)))
        both[:, n : n + step] = d_gate.astype(bf16)
        both[:, units + n : units + n + step] = d_up.astype(bf16)

    power = exponent(largest)
    sent_ref[:count, :] = (both[...].astype(f32) * jnp.exp2(power)).astype(bf16)
    sent_ref[count:, :] = jnp.broadcast_to(power, (EXTRA, 2 * units)).astype(bf16)

    def backward(g, carry):
        at = pl.ds(pl.multiple_of(g * 2 * BLOCK, BLOCK), 2 * BLOCK)
        back = jnp.exp2(-w_ref[g, 2 * BLOCK + 2 : 2 * BLOCK + 3, : 2 * BLOCK].astype(f32))
        pair = lax.dot_general(
            both[...], full[at, :], (((1,), (1,)), ((), ())), preferred_element_type=f32
        )
        pair = (pair * back).astype(bf16)
        share_ref[2 * g, :count, :] = pair[:, :BLOCK]
        share_ref[2 * g + 1, :count, :] = pair[:, BLOCK:]
        share_ref[2 * g, count:, :] = block_ref[SPLIT:, :]
        share_ref[2 * g + 1, count:, :] = block_ref[SPLIT:, :]
        return carry

    lax.fori_loop(0, groups, backward, 0)


def weight_gradients(both_ref, got_ref, shares_ref, gate_keep, up_keep, gate_ref, up_ref, columns):
    sources, count, units = both_ref.shape[0], both_ref.shape[1] - EXTRA, gate_ref.shape[1]
    for c in range(sources):
        back = jnp.exp2(-both_ref[c, count : count + 1, :BLOCK].astype(f32)).astype(bf16)
        for h in range(2):
            tile = jnp.concatenate(
                [got_ref[2 * c + h, count:, :], shares_ref[2 * c + h, count:, :]], axis=0
            )
            columns[h * BLOCK : (h + 1) * BLOCK, c * count : (c + 1) * count] = (tile * back).T
    step = 256
    for ref, keep, start in ((gate_ref, gate_keep, 0), (up_ref, up_keep, units)):
        for n in range(0, units, step):
            at = slice(start + n, start + n + step)
            right = jnp.concatenate([both_ref[c, :count, at] for c in range(sources)], axis=0)
            grad = jnp.dot(columns[...], right, preferred_element_type=f32)
            for h in range(2):
                for j in range(step // BLOCK):
                    tile = grad[h * BLOCK : (h + 1) * BLOCK, j * BLOCK : (j + 1) * BLOCK]
                    mask = keep[h, n // BLOCK + j].astype(f32)
                    ref[h * BLOCK : (h + 1) * BLOCK, n + j * BLOCK : n + (j + 1) * BLOCK] = tile * mask


def kernel(body, outs, specs, scratch, megabytes, flops):
    vmem = pl.BlockSpec(memory_space=pltpu.VMEM)
    smem = pl.BlockSpec(memory_space=pltpu.SMEM)
    return pl.pallas_call(
        body,
        out_shape=[jax.ShapeDtypeStruct(shape, dtype) for shape, dtype in outs],
        in_specs=[smem if s == "s" else vmem for s in specs],
        out_specs=[vmem] * len(outs),
        scratch_shapes=[pltpu.VMEM(shape, bf16) for shape in scratch],
        compiler_params=pltpu.CompilerParams(vmem_limit_bytes=megabytes * 2**20),
        cost_estimate=pl.CostEstimate(flops=flops, bytes_accessed=4 * 2**20, transcendentals=0),
    )


def shards(tokens, gate_weight, up_weight, gate_keep, up_keep, cotangent):
    rows, cols = lax.axis_size("row"), lax.axis_size("col")
    count, width = tokens.shape
    units = cotangent.shape[1]
    row = lax.axis_index("row")
    half = count // 2
    odd = row % 2

    route = [
        (r * cols + c, (2 * c + r % 2) * cols + r // 2) for r in range(rows) for c in range(cols)
    ]
    block = lax.ppermute(tokens, ("row", "col"), route)

    (packed,) = kernel(
        pack, [((2 * BLOCK + EXTRA, units), bf16)], "vvss", [], 8, 4 * BLOCK * units
    )(gate_weight, up_weight, gate_keep, up_keep)
    packed = packed.astype(f16)

    copies = jnp.concatenate([tokens, block[:SPLIT]], axis=0)
    copies = jnp.broadcast_to(copies[None], (rows, count + SPLIT, width))
    copies, packed = lax.optimization_barrier((copies, packed))
    got = lax.all_to_all(copies, "row", 0, 0, tiled=True)

    weights = lax.all_gather(packed, "col", axis=0).astype(bf16)

    hidden, sent, share = kernel(
        forward,
        [
            ((count, units), bf16),
            ((count + EXTRA, 2 * units), bf16),
            ((rows, 2 * count - SPLIT, width), bf16),
        ],
        "vvvv",
        [(count, rows * width), (rows * width, 2 * units), (count, 2 * units)],
        28,
        8 * count * rows * width * units,
    )(got, weights, cotangent, block)

    shares = lax.all_to_all(share, "row", 0, 0, tiled=True)

    both_all = lax.all_gather(sent.astype(f16), "col", axis=0).astype(bf16)

    total = jnp.sum(shares[:, :count].astype(f32), axis=0).astype(bf16)
    pieces = []
    for flip in range(2):
        route = []
        for r in range(rows):
            for c in range(cols):
                to = (2 * c + ((r % 2) ^ flip)) * cols + r // 2
                route.append((r * cols + c, to))
        piece = jnp.where((odd ^ flip) == 1, total[half:], total[:half])
        pieces.append(lax.ppermute(piece, ("row", "col"), route))
    left = jnp.where(odd == 0, pieces[0], pieces[1])
    right = jnp.where(odd == 0, pieces[1], pieces[0])
    grad_tokens = jnp.concatenate([left, right], axis=1)

    grad_gate, grad_up = kernel(
        weight_gradients,
        [((2 * BLOCK, units), f32)] * 2,
        "vvvss",
        [(2 * BLOCK, cols * count)],
        28,
        8 * BLOCK * cols * count * units,
    )(both_all, got, shares, gate_keep, up_keep)
    return hidden, grad_tokens, grad_gate, grad_up


def solution(mesh):
    return jax.shard_map(
        shards,
        mesh=mesh,
        in_specs=(P("col", "row"),) * 6,
        out_specs=(P("col", "row"), P("row", "col"), P("col", "row"), P("col", "row")),
        check_vma=False,
    )
```

time: 171 us -> 154 us (0.901)
  the two profiles are of different devices: /device:TPU:257 before, /device:TPU:33 now
where the time goes in v3:
time: 154 us; the launch traced here: 153 us
  blocking collectives  74.8 us (49%)
  starting transfers between devices  46.8 us (30%)
  local copies, waits for them, and re-layouts  11.5 us (7%)
  Pallas kernels  11.4 us (7%)
  other arithmetic  8.08 us (5%)
    all_gather x1, blocking collectives, shards(): weights = lax.all_gather(packed, 'col', axis=0).astype(bf16)  40.4 us
    all_gather x1, blocking collectives, shards(): both_all = lax.all_gather(sent.astype(f16), 'col', axis=0).astype(bf16)  34.4 us
    ppermute x2, starting transfers between devices, shards(): pieces.append(lax.ppermute(piece, ('row', 'col'), route))  17.3 us
    ppermute x1, starting transfers between devices, shards(): block = lax.ppermute(tokens, ('row', 'col'), route)  13.2 us
    unnamed x20, local copies, waits for them, and re-layouts  9.96 us
    all_to_all x1, starting transfers between devices, shards(): shares = lax.all_to_all(share, 'row', 0, 0, tiled=True)  9.22 us
    pallas_call x1, Pallas kernels, shards(): kernel(forward, [((count, units), bf16), ((count + EXTRA, 2 * units), bf1...  7.98 us
    all_to_all x1, starting transfers between devices, shards(): got = lax.all_to_all(copies, 'row', 0, 0, tiled=True)  7.05 us
  transfers between devices with their start and end apart: 5, of which 0 were waited for; matrix products, arithmetic and copies ran while one was open for 4% of the time, Pallas kernels for 2%

profile of v3, /device:TPU:33, one launch (start us, length us, event | category | flops | bytes accessed | tf_op | source)
XLA Modules:
  0.0 153.3 jit_solution(17059409319206778547)
XLA Ops:
  0.6 13.2 %collective-permute-start = (bf16[128,128]{1,0:T(8,128)(2,1)}, bf16[128,128]{1,0:T(8,128)(2,1)S(1)}, u32[]{:S(2)}, u32[]{:S(2)}) collective-permute-start(bf16[128,128]{1,0:T(8,128)(2,1)} %param.6), channel_id=1, source_target_pairs={{0,0},{1,32},{2,64},{3,96},{4,128},{5,160},{6,192},{7,224},{8,256}... | collective-permute-start | bytes 98312 | tf_op jit(solution)/shard_map/ppermute | solution.py:150
  13.9 0.9 copy-done.3
  14.8 0.9 copy-done.4
  15.7 0.7 copy-done.5
  16.4 0.7 copy-done.7
  17.1 0.8 shard_map.93
  17.9 0.0 collective-permute-done.block_ref
  17.9 0.8 pad_maximum_fusion
  18.7 1.5 broadcast_in_dim.2
  20.2 7.1 %all-to-all-start = ((bf16[32,192,128]{2,1,0:T(8,128)(2,1)}), bf16[32,192,128]{2,1,0:T(8,128)(2,1)S(1)}, u32[]{:S(2)}, u32[]{:S(2)}) async-start(bf16[32,192,128]{2,1,0:T(8,128)(2,1)} %broadcast_in_dim.2), calls=%async_computation | async-start | bytes 3145728 | tf_op jit(solution)/shard_map/all_to_all | solution.py:160
  27.3 40.4 %all-gather.4 = f16[4352,512]{1,0:T(8,128)(2,1)S(1)} all-gather(f16[272,512]{1,0:T(8,128)(2,1)S(1)} %convert_element_type.14), channel_id=2, replica_groups=mesh['row'=32,'col'=16] {'col'}, dimensions={0}, use_global_device_ids=true | all-gather | bytes 4734976 | tf_op jit(solution)/shard_map/all_gather | solution.py:162
  67.7 2.9 %convert_element_type.18 = bf16[4352,512]{1,0:T(8,128)(2,1)} convert(f16[4352,512]{1,0:T(8,128)(2,1)S(1)} %all-gather.4) | non-fusion elementwise | flops 2228224 | bytes 8912896 | tf_op jit(solution)/shard_map/convert_element_type | solution.py:162
  70.6 0.0 all-to-all-done.got_ref
  70.6 2.3 %copy-done.1 = bf16[4352,512]{1,0:T(8,128)(2,1)S(1)} copy-done((bf16[4352,512]{1,0:T(8,128)(2,1)S(1)}, bf16[4352,512]{1,0:T(8,128)(2,1)}, u32[]{:S(2)}) %copy-start.1) | copy-done | bytes 4456472
  72.9 0.9 copy-done.9
  73.8 8.0 %shard_map.94 = (bf16[128,512]{1,0:T(8,128)(2,1)}, bf16[144,1024]{1,0:T(8,128)(2,1)S(1)}, bf16[32,192,128]{2,1,0:T(8,128)(2,1)S(1)}) custom-call(bf16[32,192,128]{2,1,0:T(8,128)(2,1)S(1)} %all-to-all-done.got_ref, bf16[16,272,512]{2,1,0:T(8,128)(2,1)S(1)} %bitcast.3, bf16[128,512]{1,0:T(8,128)(2,1)S(1)} %copy-done.9, ...), custom_call_target="tpu_custom_call" | custom-call | flops 2147483648 | bytes 4194304 | tf_op jit(solution)/shard_map/pallas_call | solution.py:164
  81.7 1.2 copy-done.2
  82.9 9.2 %all-to-all-start.1 = ((bf16[32,192,128]{2,1,0:T(8,128)(2,1)}), bf16[32,192,128]{2,1,0:T(8,128)(2,1)S(1)}, u32[]{:S(2)}, u32[]{:S(2)}) async-start(bf16[32,192,128]{2,1,0:T(8,128)(2,1)} %copy-done.2), calls=%async_computation.1 | async-start | bytes 3145728 | tf_op jit(solution)/shard_map/all_to_all | solution.py:177
  92.2 0.1 convert_element_type.16
  92.2 34.4 %all-gather.5 = f16[2304,1024]{1,0:T(8,128)(2,1)S(1)} all-gather(f16[144,1024]{1,0:T(8,128)(2,1)S(1)} %convert_element_type.16), channel_id=3, replica_groups=mesh['row'=32,'col'=16] {'col'}, dimensions={0}, use_global_device_ids=true | all-gather | bytes 5013504 | tf_op jit(solution)/shard_map/all_gather | solution.py:179
  126.7 3.5 %convert_element_type.19 = bf16[2304,1024]{1,0:T(8,128)(2,1)} convert(f16[2304,1024]{1,0:T(8,128)(2,1)S(1)} %all-gather.5) | non-fusion elementwise | flops 2359296 | bytes 9437184 | tf_op jit(solution)/shard_map/convert_element_type | solution.py:179
  130.2 0.0 all-to-all-done.1.shares_ref
  130.2 0.2 slice_reduce_fusion
  130.3 5.3 %collective-permute-start.1 = (bf16[64,128]{1,0:T(8,128)(2,1)S(1)}, bf16[64,128]{1,0:T(8,128)(2,1)S(1)}, u32[]{:S(2)}, u32[]{:S(2)}) collective-permute-start(bf16[64,128]{1,0:T(8,128)(2,1)S(1)} %get-tuple-element.20), channel_id=1, source_target_pairs={{0,0},{1,32},{2,64},{3,96},{4,128},{5,160},{6,192},{7,224},{8,256}... | collective-permute-start | bytes 49160 | tf_op jit(solution)/shard_map/ppermute | solution.py:190
  135.7 12.0 %collective-permute-start.2 = (bf16[64,128]{1,0:T(8,128)(2,1)S(1)}, bf16[64,128]{1,0:T(8,128)(2,1)S(1)}, u32[]{:S(2)}, u32[]{:S(2)}) collective-permute-start(bf16[64,128]{1,0:T(8,128)(2,1)S(1)} %get-tuple-element.21), channel_id=1, source_target_pairs={{0,16},{1,48},{2,80},{3,112},{4,144},{5,176},{6,208},{7,240},{8,27... | collective-permute-start | bytes 49160 | tf_op jit(solution)/shard_map/ppermute | solution.py:190
  147.6 0.0 copy-done.6
  147.6 0.0 copy-done.8
  147.7 2.3 %copy-done = bf16[2304,1024]{1,0:T(8,128)(2,1)S(1)} copy-done((bf16[2304,1024]{1,0:T(8,128)(2,1)S(1)}, bf16[2304,1024]{1,0:T(8,128)(2,1)}, u32[]{:S(2)}) %copy-start) | copy-done | bytes 4718616
  150.0 2.7 %shard_map.95 = (f32[256,512]{1,0:T(8,128)}, f32[256,512]{1,0:T(8,128)}) custom-call(bf16[16,144,1024]{2,1,0:T(8,128)(2,1)S(1)} %bitcast.2, bf16[32,192,128]{2,1,0:T(8,128)(2,1)S(1)} %all-to-all-done.got_ref, bf16[32,192,128]{2,1,0:T(8,128)(2,1)S(1)} %all-to-all-done.1.shares_ref, s32[2,4]{1,0:T(2,128)S(1)} %copy-done.6, s32[2,4]{1,0:T(2,128)S(1)} %copy-done.8), custom_call_target="tpu_custom_call" | custom-call | flops 1073741824 | bytes 4194304 | tf_op jit(solution)/shard_map/pallas_call | solution.py:195
  152.7 0.0 collective-permute-done.1
  152.7 0.0 collective-permute-done.2
  152.7 0.6 pad_maximum_fusion.1
  (14 shorter events, 0.1 us)
Async XLA Ops:
  0.6 17.3 %collective-permute-start = (bf16[128,128]{1,0:T(8,128)(2,1)}, bf16[128,128]{1,0:T(8,128)(2,1)S(1)}, u32[]{:S(2)}, u32[]{:S(2)}) collective-permute-start(bf16[128,128]{1,0:T(8,128)(2,1)} %param.6), channel_id=1, source_target_pairs={{0,0},{1,32},{2,64},{3,96},{4,128},{5,160},{6,192},{7,224},{8,256}... | collective-permute-start | bytes 98312 | tf_op jit(solution)/shard_map/ppermute | solution.py:150
  13.8 1.0 copy-start.3
  14.8 0.9 copy-start.4
  15.7 0.7 copy-start.5
  16.4 0.7 copy-start.7
  20.2 50.4 %all-to-all-start = ((bf16[32,192,128]{2,1,0:T(8,128)(2,1)}), bf16[32,192,128]{2,1,0:T(8,128)(2,1)S(1)}, u32[]{:S(2)}, u32[]{:S(2)}) async-start(bf16[32,192,128]{2,1,0:T(8,128)(2,1)} %broadcast_in_dim.2), calls=%async_computation | async-start | bytes 3145728 | tf_op jit(solution)/shard_map/all_to_all | solution.py:160
  70.6 2.3 %copy-start.1 = (bf16[4352,512]{1,0:T(8,128)(2,1)S(1)}, bf16[4352,512]{1,0:T(8,128)(2,1)}, u32[]{:S(2)}) copy-start(bf16[4352,512]{1,0:T(8,128)(2,1)} %convert_element_type.18) | copy-start | bytes 13369348
  72.9 0.9 copy-start.9
  81.7 1.2 copy-start.2
  82.9 47.2 %all-to-all-start.1 = ((bf16[32,192,128]{2,1,0:T(8,128)(2,1)}), bf16[32,192,128]{2,1,0:T(8,128)(2,1)S(1)}, u32[]{:S(2)}, u32[]{:S(2)}) async-start(bf16[32,192,128]{2,1,0:T(8,128)(2,1)} %copy-done.2), calls=%async_computation.1 | async-start | bytes 3145728 | tf_op jit(solution)/shard_map/all_to_all | solution.py:177
  126.7 21.0 %copy-start.6 = (s32[2,4]{1,0:T(2,128)S(1)}, s32[2,4]{1,0:T(2,128)}, u32[]{:S(2)}) copy-start(s32[2,4]{1,0:T(2,128)} %gate_keep.3) | copy-start | bytes 100
  126.7 21.0 %copy-start.8 = (s32[2,4]{1,0:T(2,128)S(1)}, s32[2,4]{1,0:T(2,128)}, u32[]{:S(2)}) copy-start(s32[2,4]{1,0:T(2,128)} %up_keep.3) | copy-start | bytes 100
  130.3 22.3 %collective-permute-start.1 = (bf16[64,128]{1,0:T(8,128)(2,1)S(1)}, bf16[64,128]{1,0:T(8,128)(2,1)S(1)}, u32[]{:S(2)}, u32[]{:S(2)}) collective-permute-start(bf16[64,128]{1,0:T(8,128)(2,1)S(1)} %get-tuple-element.20), channel_id=1, source_target_pairs={{0,0},{1,32},{2,64},{3,96},{4,128},{5,160},{6,192},{7,224},{8,256}... | collective-permute-start | bytes 49160 | tf_op jit(solution)/shard_map/ppermute | solution.py:190
  135.7 17.0 %collective-permute-start.2 = (bf16[64,128]{1,0:T(8,128)(2,1)S(1)}, bf16[64,128]{1,0:T(8,128)(2,1)S(1)}, u32[]{:S(2)}, u32[]{:S(2)}) collective-permute-start(bf16[64,128]{1,0:T(8,128)(2,1)S(1)} %get-tuple-element.21), channel_id=1, source_target_pairs={{0,16},{1,48},{2,80},{3,112},{4,144},{5,176},{6,208},{7,240},{8,27... | collective-permute-start | bytes 49160 | tf_op jit(solution)/shard_map/ppermute | solution.py:190
  147.7 2.3 %copy-start = (bf16[2304,1024]{1,0:T(8,128)(2,1)S(1)}, bf16[2304,1024]{1,0:T(8,128)(2,1)}, u32[]{:S(2)}) copy-start(bf16[2304,1024]{1,0:T(8,128)(2,1)} %convert_element_type.19) | copy-start | bytes 14155780

commit v4 on v3

--- a/solution.py
+++ b/solution.py
@@ -9,6 +9,7 @@
 
 BLOCK = 128
 EXTRA = 16
+MARKS = 8
 SPLIT = 64
 bf16 = jnp.bfloat16
 f16 = jnp.float16
@@ -45,14 +46,29 @@
         packed_ref[2 * BLOCK :, at] = jnp.where(line == 2, power, lines).astype(bf16)
 
 
-def forward(got_ref, w_ref, grad_ref, block_ref, hidden_ref, sent_ref, share_ref, rows, full, both):
-    groups, units = w_ref.shape[0], w_ref.shape[2]
+def forward(
+    got_ref, weights_ref, grad_ref, block_ref, hidden_ref, sent_ref, shares_ref,
+    rows, full, both, w_ref, share_ref, in_sems, out_sems,
+):
+    groups, units = weights_ref.shape[0], weights_ref.shape[2]
     count = grad_ref.shape[0]
+
+    def fetch(g):
+        return pltpu.make_async_copy(weights_ref.at[g], w_ref.at[g], in_sems.at[g])
+
+    def deliver(g):
+        at = pl.ds(2 * g, 2)
+        return pltpu.make_async_copy(share_ref.at[at], shares_ref.at[at], out_sems.at[g])
+
+    def begin(g, carry):
+        fetch(g).start()
+        return carry
 
     def expand(g, carry):
         at = pl.ds(pl.multiple_of(g * 2 * BLOCK, BLOCK), BLOCK)
         after = pl.ds(pl.multiple_of(g * 2 * BLOCK + BLOCK, BLOCK), BLOCK)
-        marks = w_ref[g, 2 * BLOCK : 2 * BLOCK + EXTRA, :]
+        fetch(g).wait()
+        marks = w_ref[g, 2 * BLOCK :, :]
         back = jnp.exp2(-marks[2:3, :BLOCK].astype(f32)).astype(bf16)
         rows[:, at] = got_ref[2 * g, :count, :] * back
         rows[:, after] = got_ref[2 * g + 1, :count, :] * back
@@ -64,6 +80,7 @@
             full[after, columns] = tile * (1 - first)
         return carry
 
+    lax.fori_loop(0, groups, begin, 0)
     lax.fori_loop(0, groups, expand, 0)
     step = 256
     largest = jnp.zeros((1, 1), f32)
@@ -95,15 +112,31 @@
         share_ref[2 * g + 1, :count, :] = pair[:, BLOCK:]
         share_ref[2 * g, count:, :] = block_ref[SPLIT:, :]
         share_ref[2 * g + 1, count:, :] = block_ref[SPLIT:, :]
+        deliver(g).start()
+        return carry
+
+    def finish(g, carry):
+        deliver(g).wait()
         return carry
 
     lax.fori_loop(0, groups, backward, 0)
-
-
-def weight_gradients(both_ref, got_ref, shares_ref, gate_keep, up_keep, gate_ref, up_ref, columns):
-    sources, count, units = both_ref.shape[0], both_ref.shape[1] - EXTRA, gate_ref.shape[1]
+    lax.fori_loop(0, groups, finish, 0)
+
+
+def weight_gradients(
+    both_ref, got_ref, shares_ref, gate_keep, up_keep, gate_ref, up_ref, columns, both, sems
+):
+    sources, units = both_ref.shape[0], gate_ref.shape[1]
+    count = columns.shape[1] // sources
+
+    def fetch(c):
+        return pltpu.make_async_copy(both_ref.at[c], both.at[c], sems.at[c])
+
     for c in range(sources):
-        back = jnp.exp2(-both_ref[c, count : count + 1, :BLOCK].astype(f32)).astype(bf16)
+        fetch(c).start()
+    for c in range(sources):
+        fetch(c).wait()
+        back = jnp.exp2(-both[c, count : count + 1, :BLOCK].astype(f32)).astype(bf16)
         for h in range(2):
             tile = jnp.concatenate(
                 [got_ref[2 * c + h, count:, :], shares_ref[2 * c + h, count:, :]], axis=0
@@ -113,7 +146,7 @@
     for ref, keep, start in ((gate_ref, gate_keep, 0), (up_ref, up_keep, units)):
         for n in range(0, units, step):
             at = slice(start + n, start + n + step)
-            right = jnp.concatenate([both_ref[c, :count, at] for c in range(sources)], axis=0)
+            right = jnp.concatenate([both[c, :count, at] for c in range(sources)], axis=0)
             grad = jnp.dot(columns[...], right, preferred_element_type=f32)
             for h in range(2):
                 for j in range(step // BLOCK):
@@ -122,15 +155,16 @@
                     ref[h * BLOCK : (h + 1) * BLOCK, n + j * BLOCK : n + (j + 1) * BLOCK] = tile * mask
 
 
-def kernel(body, outs, specs, scratch, megabytes, flops):
-    vmem = pl.BlockSpec(memory_space=pltpu.VMEM)
-    smem = pl.BlockSpec(memory_space=pltpu.SMEM)
+def kernel(body, outs, specs, scratch, sems, megabytes, flops):
+    spaces = {"v": pltpu.VMEM, "s": pltpu.SMEM, "h": pltpu.HBM}
+    places = [pl.BlockSpec(memory_space=spaces[s]) for s in specs]
     return pl.pallas_call(
         body,
         out_shape=[jax.ShapeDtypeStruct(shape, dtype) for shape, dtype in outs],
-        in_specs=[smem if s == "s" else vmem for s in specs],
-        out_specs=[vmem] * len(outs),
-        scratch_shapes=[pltpu.VMEM(shape, bf16) for shape in scratch],
+        in_specs=places[: -len(outs)],
+        out_specs=places[-len(outs) :],
+        scratch_shapes=[pltpu.VMEM(shape, bf16) for shape in scratch]
+        + [pltpu.SemaphoreType.DMA((n,)) for n in sems],
         compiler_params=pltpu.CompilerParams(vmem_limit_bytes=megabytes * 2**20),
         cost_estimate=pl.CostEstimate(flops=flops, bytes_accessed=4 * 2**20, transcendentals=0),
     )
@@ -150,9 +184,9 @@
     block = lax.ppermute(tokens, ("row", "col"), route)
 
     (packed,) = kernel(
-        pack, [((2 * BLOCK + EXTRA, units), bf16)], "vvss", [], 8, 4 * BLOCK * units
+        pack, [((2 * BLOCK + EXTRA, units), bf16)], "vvssv", [], [], 8, 4 * BLOCK * units
     )(gate_weight, up_weight, gate_keep, up_keep)
-    packed = packed.astype(f16)
+    packed = packed[: 2 * BLOCK + MARKS].astype(f16)
 
     copies = jnp.concatenate([tokens, block[:SPLIT]], axis=0)
     copies = jnp.broadcast_to(copies[None], (rows, count + SPLIT, width))
@@ -168,15 +202,22 @@
             ((count + EXTRA, 2 * units), bf16),
             ((rows, 2 * count - SPLIT, width), bf16),
         ],
-        "vvvv",
-        [(count, rows * width), (rows * width, 2 * units), (count, 2 * units)],
-        28,
+        "vhvvvvh",
+        [
+            (count, rows * width),
+            (rows * width, 2 * units),
+            (count, 2 * units),
+            (cols, 2 * BLOCK + MARKS, units),
+            (rows, 2 * count - SPLIT, width),
+        ],
+        [cols, cols],
+        48,
         8 * count * rows * width * units,
     )(got, weights, cotangent, block)
 
     shares = lax.all_to_all(share, "row", 0, 0, tiled=True)
 
-    both_all = lax.all_gather(sent.astype(f16), "col", axis=0).astype(bf16)
+    both_all = lax.all_gather(sent[: count + MARKS].astype(f16), "col", axis=0).astype(bf16)
 
     total = jnp.sum(shares[:, :count].astype(f32), axis=0).astype(bf16)
     pieces = []
@@ -195,9 +236,10 @@
     grad_gate, grad_up = kernel(
         weight_gradients,
         [((2 * BLOCK, units), f32)] * 2,
-        "vvvss",
-        [(2 * BLOCK, cols * count)],
-        28,
+        "hvvssvv",
+        [(2 * BLOCK, cols * count), (cols, count + MARKS, 2 * units)],
+        [cols],
+        48,
         8 * BLOCK * cols * count * units,
     )(both_all, got, shares, gate_keep, up_keep)
     return hidden, grad_tokens, grad_gate, grad_up

time: 154 us -> 154 us (level)
  the two profiles are of different devices: /device:TPU:33 before, /device:TPU:105 now
where the time goes in v4:
time: 154 us; the launch traced here: 153 us
  blocking collectives  70.4 us (46%)
  starting transfers between devices  46.2 us (30%)
  Pallas kernels  17.6 us (11%)
  other arithmetic  7.83 us (5%)
  local copies, waits for them, and re-layouts  6.86 us (4%)
  waiting for transfers between devices  3.79 us (2%)
    all_gather x1, blocking collectives, shards(): weights = lax.all_gather(packed, 'col', axis=0).astype(bf16)  38.4 us
    all_gather x1, blocking collectives, shards(): lax.all_gather(sent[:count + MARKS].astype(f16), 'col', axis=0).astype(bf16)  31.9 us
    ppermute x2, starting transfers between devices, shards(): pieces.append(lax.ppermute(piece, ('row', 'col'), route))  17.3 us
    ppermute x1, starting transfers between devices, shards(): block = lax.ppermute(tokens, ('row', 'col'), route)  13.2 us
    pallas_call x1, Pallas kernels, shards(): kernel(forward, [((count, units), bf16), ((count + EXTRA, 2 * units), bf1...  11.8 us
    all_to_all x1, starting transfers between devices, shards(): shares = lax.all_to_all(share, 'row', 0, 0, tiled=True)  9.22 us
    all_to_all x1, starting transfers between devices, shards(): got = lax.all_to_all(copies, 'row', 0, 0, tiled=True)  6.49 us
    unnamed x16, local copies, waits for them, and re-layouts  5.32 us
  transfers between devices with their start and end apart: 5, of which 1 were waited for; matrix products, arithmetic and copies ran while one was open for 4% of the time, Pallas kernels for 4%

profile of v4, /device:TPU:105, one launch (start us, length us, event | category | flops | bytes accessed | tf_op | source)
XLA Modules:
  0.0 153.4 jit_solution(4520558409082017807)
XLA Ops:
  0.6 13.2 %collective-permute-start = (bf16[128,128]{1,0:T(8,128)(2,1)}, bf16[128,128]{1,0:T(8,128)(2,1)S(1)}, u32[]{:S(2)}, u32[]{:S(2)}) collective-permute-start(bf16[128,128]{1,0:T(8,128)(2,1)} %param.6), channel_id=1, source_target_pairs={{0,0},{1,32},{2,64},{3,96},{4,128},{5,160},{6,192},{7,224},{8,256}... | collective-permute-start | bytes 98312 | tf_op jit(solution)/shard_map/ppermute | solution.py:184
  13.8 0.0 copy-start.1
  13.9 0.9 copy-done.1
  14.8 0.0 copy-start.2
  14.8 0.9 copy-done.2
  15.7 0.7 copy-done.3
  16.4 0.7 copy-done.5
  17.1 0.8 shard_map.93
  17.9 0.0 collective-permute-done.block_ref
  17.9 0.8 pad_maximum_fusion
  18.7 1.5 broadcast_in_dim.2
  20.2 6.5 %all-to-all-start = ((bf16[32,192,128]{2,1,0:T(8,128)(2,1)}), bf16[32,192,128]{2,1,0:T(8,128)(2,1)S(1)}, u32[]{:S(2)}, u32[]{:S(2)}) async-start(bf16[32,192,128]{2,1,0:T(8,128)(2,1)} %broadcast_in_dim.2), calls=%async_computation | async-start | bytes 3145728 | tf_op jit(solution)/shard_map/all_to_all | solution.py:194
  26.7 38.4 %all-gather.4 = f16[4224,512]{1,0:T(8,128)(2,1)S(1)} all-gather(f16[264,512]{1,0:T(8,128)(2,1)S(1)} %slice_convert_fusion.1), channel_id=2, replica_groups=mesh['row'=32,'col'=16] {'col'}, dimensions={0}, use_global_device_ids=true | all-gather | bytes 4595712 | tf_op jit(solution)/shard_map/all_gather | solution.py:196
  65.2 2.8 %convert_element_type.18 = bf16[4224,512]{1,0:T(8,128)(2,1)} convert(f16[4224,512]{1,0:T(8,128)(2,1)S(1)} %all-gather.4) | non-fusion elementwise | flops 2162688 | bytes 8650752 | tf_op jit(solution)/shard_map/convert_element_type | solution.py:196
  68.0 0.0 all-to-all-done.got_ref
  68.0 0.9 copy-done.7
  68.9 11.8 %shard_map.94 = (bf16[128,512]{1,0:T(8,128)(2,1)}, bf16[144,1024]{1,0:T(8,128)(2,1)S(1)}, bf16[32,192,128]{2,1,0:T(8,128)(2,1)S(1)}) custom-call(bf16[32,192,128]{2,1,0:T(8,128)(2,1)S(1)} %all-to-all-done.got_ref, bf16[16,264,512]{2,1,0:T(8,128)(2,1)} %bitcast.3, bf16[128,512]{1,0:T(8,128)(2,1)S(1)} %copy-done.7, ...), custom_call_target="tpu_custom_call" | custom-call | flops 2147483648 | bytes 4194304 | tf_op jit(solution)/shard_map/pallas_call | solution.py:198
  80.8 0.0 copy-start
  80.8 1.2 copy-done
  81.9 9.2 %all-to-all-start.1 = ((bf16[32,192,128]{2,1,0:T(8,128)(2,1)}), bf16[32,192,128]{2,1,0:T(8,128)(2,1)S(1)}, u32[]{:S(2)}, u32[]{:S(2)}) async-start(bf16[32,192,128]{2,1,0:T(8,128)(2,1)} %copy-done), calls=%async_computation.1 | async-start | bytes 3145728 | tf_op jit(solution)/shard_map/all_to_all | solution.py:218
  91.2 31.9 %all-gather.5 = f16[2176,1024]{1,0:T(8,128)(2,1)S(1)} all-gather(f16[136,1024]{1,0:T(8,128)(2,1)S(1)} %slice_convert_fusion), channel_id=3, replica_groups=mesh['row'=32,'col'=16] {'col'}, dimensions={0}, use_global_device_ids=true | all-gather | bytes 4734976 | tf_op jit(solution)/shard_map/all_gather | solution.py:220
  123.2 3.3 %convert_element_type.19 = bf16[2176,1024]{1,0:T(8,128)(2,1)} convert(f16[2176,1024]{1,0:T(8,128)(2,1)S(1)} %all-gather.5) | non-fusion elementwise | flops 2228224 | bytes 8912896 | tf_op jit(solution)/shard_map/convert_element_type | solution.py:220
  126.5 0.0 all-to-all-done.1.shares_ref
  126.5 0.2 slice_reduce_fusion
  126.7 10.2 %collective-permute-start.1 = (bf16[64,128]{1,0:T(8,128)(2,1)S(1)}, bf16[64,128]{1,0:T(8,128)(2,1)S(1)}, u32[]{:S(2)}, u32[]{:S(2)}) collective-permute-start(bf16[64,128]{1,0:T(8,128)(2,1)S(1)} %get-tuple-element.20), channel_id=1, source_target_pairs={{0,0},{1,32},{2,64},{3,96},{4,128},{5,160},{6,192},{7,224},{8,256}... | collective-permute-start | bytes 49160 | tf_op jit(solution)/shard_map/ppermute | solution.py:231
  136.9 7.1 %collective-permute-start.2 = (bf16[64,128]{1,0:T(8,128)(2,1)S(1)}, bf16[64,128]{1,0:T(8,128)(2,1)S(1)}, u32[]{:S(2)}, u32[]{:S(2)}) collective-permute-start(bf16[64,128]{1,0:T(8,128)(2,1)S(1)} %get-tuple-element.21), channel_id=1, source_target_pairs={{0,16},{1,48},{2,80},{3,112},{4,144},{5,176},{6,208},{7,240},{8,27... | collective-permute-start | bytes 49160 | tf_op jit(solution)/shard_map/ppermute | solution.py:231
  144.0 0.0 copy-done.4
  144.0 0.0 copy-done.6
  144.0 5.0 %shard_map.95 = (f32[256,512]{1,0:T(8,128)}, f32[256,512]{1,0:T(8,128)}) custom-call(bf16[16,136,1024]{2,1,0:T(8,128)(2,1)} %bitcast.2, bf16[32,192,128]{2,1,0:T(8,128)(2,1)S(1)} %all-to-all-done.got_ref, bf16[32,192,128]{2,1,0:T(8,128)(2,1)S(1)} %all-to-all-done.1.shares_ref, s32[2,4]{1,0:T(2,128)S(1)} %copy-done.4, s32[2,4]{1,0:T(2,128)S(1)} %copy-done.6), custom_call_target="tpu_custom_call" | custom-call | flops 1073741824 | bytes 4194304 | tf_op jit(solution)/shard_map/pallas_call | solution.py:236
  149.0 0.0 collective-permute-done.1
  149.0 3.7 %collective-permute-done.2 = bf16[64,128]{1,0:T(8,128)(2,1)S(1)} collective-permute-done((bf16[64,128]{1,0:T(8,128)(2,1)S(1)}, bf16[64,128]{1,0:T(8,128)(2,1)S(1)}, u32[]{:S(2)}, u32[]{:S(2)}) %collective-permute-start.2) | collective-permute-done | bytes 16416 | tf_op jit(solution)/shard_map/ppermute | solution.py:231
  152.8 0.6 pad_maximum_fusion.1
  (10 shorter events, 0.1 us)
Async XLA Ops:
  0.6 17.3 %collective-permute-start = (bf16[128,128]{1,0:T(8,128)(2,1)}, bf16[128,128]{1,0:T(8,128)(2,1)S(1)}, u32[]{:S(2)}, u32[]{:S(2)}) collective-permute-start(bf16[128,128]{1,0:T(8,128)(2,1)} %param.6), channel_id=1, source_target_pairs={{0,0},{1,32},{2,64},{3,96},{4,128},{5,160},{6,192},{7,224},{8,256}... | collective-permute-start | bytes 98312 | tf_op jit(solution)/shard_map/ppermute | solution.py:184
  13.8 1.0 copy-start.1
  14.8 0.9 copy-start.2
  15.7 0.7 copy-start.3
  16.4 0.7 copy-start.5
  20.2 47.7 %all-to-all-start = ((bf16[32,192,128]{2,1,0:T(8,128)(2,1)}), bf16[32,192,128]{2,1,0:T(8,128)(2,1)S(1)}, u32[]{:S(2)}, u32[]{:S(2)}) async-start(bf16[32,192,128]{2,1,0:T(8,128)(2,1)} %broadcast_in_dim.2), calls=%async_computation | async-start | bytes 3145728 | tf_op jit(solution)/shard_map/all_to_all | solution.py:194
  68.0 0.9 copy-start.7
  80.8 1.2 copy-start
  81.9 44.6 %all-to-all-start.1 = ((bf16[32,192,128]{2,1,0:T(8,128)(2,1)}), bf16[32,192,128]{2,1,0:T(8,128)(2,1)S(1)}, u32[]{:S(2)}, u32[]{:S(2)}) async-start(bf16[32,192,128]{2,1,0:T(8,128)(2,1)} %copy-done), calls=%async_computation.1 | async-start | bytes 3145728 | tf_op jit(solution)/shard_map/all_to_all | solution.py:218
  123.2 20.8 %copy-start.4 = (s32[2,4]{1,0:T(2,128)S(1)}, s32[2,4]{1,0:T(2,128)}, u32[]{:S(2)}) copy-start(s32[2,4]{1,0:T(2,128)} %gate_keep.3) | copy-start | bytes 100
  123.2 20.8 %copy-start.6 = (s32[2,4]{1,0:T(2,128)S(1)}, s32[2,4]{1,0:T(2,128)}, u32[]{:S(2)}) copy-start(s32[2,4]{1,0:T(2,128)} %up_keep.3) | copy-start | bytes 100
  126.7 22.3 %collective-permute-start.1 = (bf16[64,128]{1,0:T(8,128)(2,1)S(1)}, bf16[64,128]{1,0:T(8,128)(2,1)S(1)}, u32[]{:S(2)}, u32[]{:S(2)}) collective-permute-start(bf16[64,128]{1,0:T(8,128)(2,1)S(1)} %get-tuple-element.20), channel_id=1, source_target_pairs={{0,0},{1,32},{2,64},{3,96},{4,128},{5,160},{6,192},{7,224},{8,256}... | collective-permute-start | bytes 49160 | tf_op jit(solution)/shard_map/ppermute | solution.py:231
  136.9 15.9 %collective-permute-start.2 = (bf16[64,128]{1,0:T(8,128)(2,1)S(1)}, bf16[64,128]{1,0:T(8,128)(2,1)S(1)}, u32[]{:S(2)}, u32[]{:S(2)}) collective-permute-start(bf16[64,128]{1,0:T(8,128)(2,1)S(1)} %get-tuple-element.21), channel_id=1, source_target_pairs={{0,16},{1,48},{2,80},{3,112},{4,144},{5,176},{6,208},{7,240},{8,27... | collective-permute-start | bytes 49160 | tf_op jit(solution)/shard_map/ppermute | solution.py:231

commit v5 on v4

--- a/solution.py
+++ b/solution.py
@@ -10,6 +10,7 @@
 BLOCK = 128
 EXTRA = 16
 MARKS = 8
+PARTS = 4
 SPLIT = 64
 bf16 = jnp.bfloat16
 f16 = jnp.float16
@@ -46,12 +47,26 @@
         packed_ref[2 * BLOCK :, at] = jnp.where(line == 2, power, lines).astype(bf16)
 
 
+def spread(tokens_ref, block_ref, copies_ref, one, sems):
+    count = tokens_ref.shape[0]
+    one[:count] = tokens_ref[...]
+    one[count:] = block_ref[:SPLIT]
+    copies = [
+        pltpu.make_async_copy(one, copies_ref.at[i], sems.at[i]) for i in range(copies_ref.shape[0])
+    ]
+    for copy in copies:
+        copy.start()
+    for copy in copies:
+        copy.wait()
+
+
 def forward(
     got_ref, weights_ref, grad_ref, block_ref, hidden_ref, sent_ref, shares_ref,
-    rows, full, both, w_ref, share_ref, in_sems, out_sems,
+    rows, full, both, w_ref, share_ref, total, in_sems, out_sems,
 ):
     groups, units = weights_ref.shape[0], weights_ref.shape[2]
     count = grad_ref.shape[0]
+    half, rest = count // 2, (count - SPLIT) // 2
 
     def fetch(g):
         return pltpu.make_async_copy(weights_ref.at[g], w_ref.at[g], in_sems.at[g])
@@ -81,12 +96,18 @@
         return carry
 
     lax.fori_loop(0, groups, begin, 0)
-    lax.fori_loop(0, groups, expand, 0)
-    step = 256
+    part, step = groups // PARTS, 256
+    for p in range(PARTS):
+        lax.fori_loop(p * part, (p + 1) * part, expand, 0)
+        inner = slice(p * part * 2 * BLOCK, (p + 1) * part * 2 * BLOCK)
+        for n in range(0, 2 * units, step):
+            at = slice(n, n + step)
+            term = jnp.dot(rows[:, inner], full[inner, at], preferred_element_type=f32)
+            total[:, at] = term if p == 0 else total[:, at] + term
+
     largest = jnp.zeros((1, 1), f32)
     for n in range(0, units, step):
-        gate = jnp.dot(rows[...], full[:, n : n + step], preferred_element_type=f32)
-        up = jnp.dot(rows[...], full[:, units + n : units + n + step], preferred_element_type=f32)
+        gate, up = total[:, n : n + step], total[:, units + n : units + n + step]
         sigmoid_gate = jax.nn.sigmoid(gate)
         activated = gate * sigmoid_gate
         hidden_ref[:, n : n + step] = (activated * up).astype(bf16)
@@ -108,10 +129,10 @@
             both[...], full[at, :], (((1,), (1,)), ((), ())), preferred_element_type=f32
         )
         pair = (pair * back).astype(bf16)
-        share_ref[2 * g, :count, :] = pair[:, :BLOCK]
-        share_ref[2 * g + 1, :count, :] = pair[:, BLOCK:]
-        share_ref[2 * g, count:, :] = block_ref[SPLIT:, :]
-        share_ref[2 * g + 1, count:, :] = block_ref[SPLIT:, :]
+        for i in range(2):
+            share_ref[2 * g + i, :half, :] = pair[i * half : (i + 1) * half]
+            share_ref[2 * g + i, half:, :BLOCK] = block_ref[SPLIT : SPLIT + rest, :]
+            share_ref[2 * g + i, half:, BLOCK:] = block_ref[SPLIT + rest :, :]
         deliver(g).start()
         return carry
 
@@ -139,7 +160,12 @@
         back = jnp.exp2(-both[c, count : count + 1, :BLOCK].astype(f32)).astype(bf16)
         for h in range(2):
             tile = jnp.concatenate(
-                [got_ref[2 * c + h, count:, :], shares_ref[2 * c + h, count:, :]], axis=0
+                [
+                    got_ref[2 * c + h, count:, :],
+                    shares_ref[2 * c + h, count // 2 :, :BLOCK],
+                    shares_ref[2 * c + h, count // 2 :, BLOCK:],
+                ],
+                axis=0,
             )
             columns[h * BLOCK : (h + 1) * BLOCK, c * count : (c + 1) * count] = (tile * back).T
     step = 256
@@ -163,7 +189,10 @@
         out_shape=[jax.ShapeDtypeStruct(shape, dtype) for shape, dtype in outs],
         in_specs=places[: -len(outs)],
         out_specs=places[-len(outs) :],
-        scratch_shapes=[pltpu.VMEM(shape, bf16) for shape in scratch]
+        scratch_shapes=[
+            pltpu.VMEM(shape[1:], f32) if shape[0] is f32 else pltpu.VMEM(shape, bf16)
+            for shape in scratch
+        ]
         + [pltpu.SemaphoreType.DMA((n,)) for n in sems],
         compiler_params=pltpu.CompilerParams(vmem_limit_bytes=megabytes * 2**20),
         cost_estimate=pl.CostEstimate(flops=flops, bytes_accessed=4 * 2**20, transcendentals=0),
@@ -174,9 +203,6 @@
     rows, cols = lax.axis_size("row"), lax.axis_size("col")
     count, width = tokens.shape
     units = cotangent.shape[1]
-    row = lax.axis_index("row")
-    half = count // 2
-    odd = row % 2
 
     route = [
         (r * cols + c, (2 * c + r % 2) * cols + r // 2) for r in range(rows) for c in range(cols)
@@ -188,8 +214,9 @@
     )(gate_weight, up_weight, gate_keep, up_keep)
     packed = packed[: 2 * BLOCK + MARKS].astype(f16)
 
-    copies = jnp.concatenate([tokens, block[:SPLIT]], axis=0)
-    copies = jnp.broadcast_to(copies[None], (rows, count + SPLIT, width))
+    (copies,) = kernel(
+        spread, [((rows, count + SPLIT, width), bf16)], "vvh", [(count + SPLIT, width)], [rows], 48, 1
+    )(tokens, block)
     copies, packed = lax.optimization_barrier((copies, packed))
     got = lax.all_to_all(copies, "row", 0, 0, tiled=True)
 
@@ -200,7 +227,7 @@
         [
             ((count, units), bf16),
             ((count + EXTRA, 2 * units), bf16),
-            ((rows, 2 * count - SPLIT, width), bf16),
+            ((rows, count - SPLIT // 2, 2 * width), bf16),
         ],
         "vhvvvvh",
         [
@@ -208,7 +235,8 @@
             (rows * width, 2 * units),
             (count, 2 * units),
             (cols, 2 * BLOCK + MARKS, units),
-            (rows, 2 * count - SPLIT, width),
+            (rows, count - SPLIT // 2, 2 * width),
+            (f32, count, 2 * units),
         ],
         [cols, cols],
         48,
@@ -219,19 +247,8 @@
 
     both_all = lax.all_gather(sent[: count + MARKS].astype(f16), "col", axis=0).astype(bf16)
 
-    total = jnp.sum(shares[:, :count].astype(f32), axis=0).astype(bf16)
-    pieces = []
-    for flip in range(2):
-        route = []
-        for r in range(rows):
-            for c in range(cols):
-                to = (2 * c + ((r % 2) ^ flip)) * cols + r // 2
-                route.append((r * cols + c, to))
-        piece = jnp.where((odd ^ flip) == 1, total[half:], total[:half])
-        pieces.append(lax.ppermute(piece, ("row", "col"), route))
-    left = jnp.where(odd == 0, pieces[0], pieces[1])
-    right = jnp.where(odd == 0, pieces[1], pieces[0])
-    grad_tokens = jnp.concatenate([left, right], axis=1)
+    total = jnp.sum(shares[:, : count // 2].astype(f32), axis=0).astype(bf16)
+    grad_tokens = lax.ppermute(total, ("row", "col"), route)
 
     grad_gate, grad_up = kernel(
         weight_gradients,

time: 154 us -> 146 us (0.948)
  the two profiles are of different devices: /device:TPU:105 before, /device:TPU:1 now
where the time goes in v5:
time: 146 us; the launch traced here: 143 us
  blocking collectives  72.1 us (49%)
  starting transfers between devices  37.3 us (26%)
  Pallas kernels  19.1 us (13%)
  other arithmetic  6.4 us (4%)
  local copies, waits for them, and re-layouts  5.79 us (4%)
  waiting for transfers between devices  1.88 us (1%)
    all_gather x1, blocking collectives, shards(): weights = lax.all_gather(packed, 'col', axis=0).astype(bf16)  39.4 us
    all_gather x1, blocking collectives, shards(): lax.all_gather(sent[:count + MARKS].astype(f16), 'col', axis=0).astype(bf16)  32.7 us
    all_to_all x1, starting transfers between devices, shards(): got = lax.all_to_all(copies, 'row', 0, 0, tiled=True)  15.5 us
    pallas_call x1, Pallas kernels, shards(): kernel(forward, [((count, units), bf16), ((count + EXTRA, 2 * units), bf1...  11.9 us
    all_to_all x1, starting transfers between devices, shards(): shares = lax.all_to_all(share, 'row', 0, 0, tiled=True)  9.49 us
    ppermute x1, starting transfers between devices, shards(): grad_tokens = lax.ppermute(total, ('row', 'col'), route)  6.34 us
    ppermute x1, starting transfers between devices, shards(): block = lax.ppermute(tokens, ('row', 'col'), route)  6.04 us
    unnamed x19, local copies, waits for them, and re-layouts  5.79 us
  transfers between devices with their start and end apart: 4, of which 1 were waited for; matrix products, arithmetic and copies ran while one was open for 4% of the time, Pallas kernels for 4%

profile of v5, /device:TPU:1, one launch (start us, length us, event | category | flops | bytes accessed | tf_op | source)
XLA Modules:
  0.0 143.4 jit_solution(16334717659995408893)
XLA Ops:
  0.6 6.0 %collective-permute-start = (bf16[128,128]{1,0:T(8,128)(2,1)}, bf16[128,128]{1,0:T(8,128)(2,1)S(1)}, u32[]{:S(2)}, u32[]{:S(2)}) collective-permute-start(bf16[128,128]{1,0:T(8,128)(2,1)} %tokens_ref.1), channel_id=1, source_target_pairs={{0,0},{1,32},{2,64},{3,96},{4,128},{5,160},{6,192},{7,224},{8,256}... | collective-permute-start | bytes 98312 | tf_op jit(solution)/shard_map/ppermute | solution.py:210
  6.7 0.0 copy-start.1
  6.7 0.9 copy-done.1
  7.6 0.0 copy-start.2
  7.6 0.9 copy-done.2
  8.6 0.0 copy-start.4
  8.6 0.7 copy-done.4
  9.3 0.7 copy-done.6
  9.9 0.8 shard_map.94
  10.8 0.0 collective-permute-done.block_ref
  10.8 0.0 copy-start.3
  10.8 0.7 copy-done.3
  11.5 1.5 %shard_map.93 = bf16[32,192,128]{2,1,0:T(8,128)(2,1)} custom-call(bf16[128,128]{1,0:T(8,128)(2,1)S(1)} %copy-done.3, bf16[128,128]{1,0:T(8,128)(2,1)S(1)} %collective-permute-done.block_ref), custom_call_target="tpu_custom_call" | custom-call | flops 1 | bytes 4194304 | tf_op jit(solution)/shard_map/pallas_call | solution.py:217
  13.0 15.5 %all-to-all-start = ((bf16[32,192,128]{2,1,0:T(8,128)(2,1)}), bf16[32,192,128]{2,1,0:T(8,128)(2,1)S(1)}, u32[]{:S(2)}, u32[]{:S(2)}) async-start(bf16[32,192,128]{2,1,0:T(8,128)(2,1)} %shard_map.93), calls=%async_computation | async-start | bytes 3145728 | tf_op jit(solution)/shard_map/all_to_all | solution.py:221
  28.5 39.4 %all-gather.4 = f16[4224,512]{1,0:T(8,128)(2,1)S(1)} all-gather(f16[264,512]{1,0:T(8,128)(2,1)S(1)} %slice_convert_fusion.1), channel_id=2, replica_groups=mesh['row'=32,'col'=16] {'col'}, dimensions={0}, use_global_device_ids=true | all-gather | bytes 4595712 | tf_op jit(solution)/shard_map/all_gather | solution.py:223
  67.9 2.8 %convert_element_type.18 = bf16[4224,512]{1,0:T(8,128)(2,1)} convert(f16[4224,512]{1,0:T(8,128)(2,1)S(1)} %all-gather.4) | non-fusion elementwise | flops 2162688 | bytes 8650752 | tf_op jit(solution)/shard_map/convert_element_type | solution.py:223
  70.7 0.0 all-to-all-done.got_ref
  70.7 0.0 copy-done.8
  70.7 11.9 %shard_map.95 = (bf16[128,512]{1,0:T(8,128)(2,1)}, bf16[144,1024]{1,0:T(8,128)(2,1)S(1)}, bf16[32,96,256]{2,1,0:T(8,128)(2,1)S(1)}) custom-call(bf16[32,192,128]{2,1,0:T(8,128)(2,1)S(1)} %all-to-all-done.got_ref, bf16[16,264,512]{2,1,0:T(8,128)(2,1)} %bitcast.3, bf16[128,512]{1,0:T(8,128)(2,1)S(1)} %copy-done.8, ...), custom_call_target="tpu_custom_call" | custom-call | flops 2147483648 | bytes 4194304 | tf_op jit(solution)/shard_map/pallas_call | solution.py:225
  82.6 0.0 copy-start
  82.6 1.2 copy-done
  83.8 9.5 %all-to-all-start.1 = ((bf16[32,96,256]{2,1,0:T(8,128)(2,1)}), bf16[32,96,256]{2,1,0:T(8,128)(2,1)S(1)}, u32[]{:S(2)}, u32[]{:S(2)}) async-start(bf16[32,96,256]{2,1,0:T(8,128)(2,1)} %copy-done), calls=%async_computation.1 | async-start | bytes 3145728 | tf_op jit(solution)/shard_map/all_to_all | solution.py:246
  93.3 32.7 %all-gather.5 = f16[2176,1024]{1,0:T(8,128)(2,1)S(1)} all-gather(f16[136,1024]{1,0:T(8,128)(2,1)S(1)} %slice_convert_fusion), channel_id=3, replica_groups=mesh['row'=32,'col'=16] {'col'}, dimensions={0}, use_global_device_ids=true | all-gather | bytes 4734976 | tf_op jit(solution)/shard_map/all_gather | solution.py:248
  126.0 3.3 %convert_element_type.19 = bf16[2176,1024]{1,0:T(8,128)(2,1)} convert(f16[2176,1024]{1,0:T(8,128)(2,1)S(1)} %all-gather.5) | non-fusion elementwise | flops 2228224 | bytes 8912896 | tf_op jit(solution)/shard_map/convert_element_type | solution.py:248
  129.4 1.9 %all-to-all-done.1.shares_ref = bf16[32,96,256]{2,1,0:T(8,128)(2,1)S(1)} async-done(((bf16[32,96,256]{2,1,0:T(8,128)(2,1)}), bf16[32,96,256]{2,1,0:T(8,128)(2,1)S(1)}, u32[]{:S(2)}, u32[]{:S(2)}) %all-to-all-start.1) | async-done | bytes 1572896 | tf_op jit(solution)/shard_map/all_to_all | solution.py:246
  131.2 0.1 slice_reduce_fusion
  131.4 6.3 %collective-permute-start.1 = (bf16[64,256]{1,0:T(8,128)(2,1)S(1)}, bf16[64,256]{1,0:T(8,128)(2,1)S(1)}, u32[]{:S(2)}, u32[]{:S(2)}) collective-permute-start(bf16[64,256]{1,0:T(8,128)(2,1)S(1)} %slice_reduce_fusion), channel_id=1, source_target_pairs={{0,0},{1,32},{2,64},{3,96},{4,128},{5,160},{6,192},{7,224},{8,256}... | collective-permute-start | bytes 98312 | tf_op jit(solution)/shard_map/ppermute | solution.py:251
  137.7 0.0 copy-done.5
  137.7 0.0 copy-done.7
  137.8 5.0 %shard_map.96 = (f32[256,512]{1,0:T(8,128)}, f32[256,512]{1,0:T(8,128)}) custom-call(bf16[16,136,1024]{2,1,0:T(8,128)(2,1)} %bitcast.2, bf16[32,192,128]{2,1,0:T(8,128)(2,1)S(1)} %all-to-all-done.got_ref, bf16[32,96,256]{2,1,0:T(8,128)(2,1)S(1)} %all-to-all-done.1.shares_ref, s32[2,4]{1,0:T(2,128)S(1)} %copy-done.5, s32[2,4]{1,0:T(2,128)S(1)} %copy-done.7), custom_call_target="tpu_custom_call" | custom-call | flops 1073741824 | bytes 4194304 | tf_op jit(solution)/shard_map/pallas_call | solution.py:253
  142.8 0.0 collective-permute-done.1
  142.8 0.6 copy.11
  (6 shorter events, 0.1 us)
Async XLA Ops:
  0.6 10.1 %collective-permute-start = (bf16[128,128]{1,0:T(8,128)(2,1)}, bf16[128,128]{1,0:T(8,128)(2,1)S(1)}, u32[]{:S(2)}, u32[]{:S(2)}) collective-permute-start(bf16[128,128]{1,0:T(8,128)(2,1)} %tokens_ref.1), channel_id=1, source_target_pairs={{0,0},{1,32},{2,64},{3,96},{4,128},{5,160},{6,192},{7,224},{8,256}... | collective-permute-start | bytes 98312 | tf_op jit(solution)/shard_map/ppermute | solution.py:210
  6.7 1.0 copy-start.1
  7.6 0.9 copy-start.2
  8.6 0.7 copy-start.4
  9.3 0.7 copy-start.6
  10.8 0.8 copy-start.3
  13.0 57.7 %all-to-all-start = ((bf16[32,192,128]{2,1,0:T(8,128)(2,1)}), bf16[32,192,128]{2,1,0:T(8,128)(2,1)S(1)}, u32[]{:S(2)}, u32[]{:S(2)}) async-start(bf16[32,192,128]{2,1,0:T(8,128)(2,1)} %shard_map.93), calls=%async_computation | async-start | bytes 3145728 | tf_op jit(solution)/shard_map/all_to_all | solution.py:221
  67.9 2.8 %copy-start.8 = (bf16[128,512]{1,0:T(8,128)(2,1)S(1)}, bf16[128,512]{1,0:T(8,128)(2,1)}, u32[]{:S(2)}) copy-start(bf16[128,512]{1,0:T(8,128)(2,1)} %grad_ref.1) | copy-start | bytes 393220
  82.6 1.2 copy-start
  83.8 47.5 %all-to-all-start.1 = ((bf16[32,96,256]{2,1,0:T(8,128)(2,1)}), bf16[32,96,256]{2,1,0:T(8,128)(2,1)S(1)}, u32[]{:S(2)}, u32[]{:S(2)}) async-start(bf16[32,96,256]{2,1,0:T(8,128)(2,1)} %copy-done), calls=%async_computation.1 | async-start | bytes 3145728 | tf_op jit(solution)/shard_map/all_to_all | solution.py:246
  126.0 11.7 %copy-start.5 = (s32[2,4]{1,0:T(2,128)S(1)}, s32[2,4]{1,0:T(2,128)}, u32[]{:S(2)}) copy-start(s32[2,4]{1,0:T(2,128)} %gate_keep.3) | copy-start | bytes 100
  126.0 11.7 %copy-start.7 = (s32[2,4]{1,0:T(2,128)S(1)}, s32[2,4]{1,0:T(2,128)}, u32[]{:S(2)}) copy-start(s32[2,4]{1,0:T(2,128)} %up_keep.3) | copy-start | bytes 100
  131.4 11.4 %collective-permute-start.1 = (bf16[64,256]{1,0:T(8,128)(2,1)S(1)}, bf16[64,256]{1,0:T(8,128)(2,1)S(1)}, u32[]{:S(2)}, u32[]{:S(2)}) collective-permute-start(bf16[64,256]{1,0:T(8,128)(2,1)S(1)} %slice_reduce_fusion), channel_id=1, source_target_pairs={{0,0},{1,32},{2,64},{3,96},{4,128},{5,160},{6,192},{7,224},{8,256}... | collective-permute-start | bytes 98312 | tf_op jit(solution)/shard_map/ppermute | solution.py:251

commit v6 on v5

--- a/solution.py
+++ b/solution.py
@@ -61,19 +61,15 @@
 
 
 def forward(
-    got_ref, weights_ref, grad_ref, block_ref, hidden_ref, sent_ref, shares_ref,
-    rows, full, both, w_ref, share_ref, total, in_sems, out_sems,
+    got_ref, weights_ref, grad_ref, block_ref, hidden_ref, sent_ref, share_ref,
+    rows, full, both, w_ref, turned, total, sems,
 ):
     groups, units = weights_ref.shape[0], weights_ref.shape[2]
     count = grad_ref.shape[0]
-    half, rest = count // 2, (count - SPLIT) // 2
+    half = count // 2
 
     def fetch(g):
-        return pltpu.make_async_copy(weights_ref.at[g], w_ref.at[g], in_sems.at[g])
-
-    def deliver(g):
-        at = pl.ds(2 * g, 2)
-        return pltpu.make_async_copy(share_ref.at[at], shares_ref.at[at], out_sems.at[g])
+        return pltpu.make_async_copy(weights_ref.at[g], w_ref.at[g], sems.at[g])
 
     def begin(g, carry):
         fetch(g).start()
@@ -98,7 +94,7 @@
     lax.fori_loop(0, groups, begin, 0)
     part, step = groups // PARTS, 256
     for p in range(PARTS):
-        lax.fori_loop(p * part, (p + 1) * part, expand, 0)
+        lax.fori_loop(p * part, (p + 1) * part, expand, 0, unroll=part)
         inner = slice(p * part * 2 * BLOCK, (p + 1) * part * 2 * BLOCK)
         for n in range(0, 2 * units, step):
             at = slice(n, n + step)
@@ -122,30 +118,37 @@
     sent_ref[:count, :] = (both[...].astype(f32) * jnp.exp2(power)).astype(bf16)
     sent_ref[count:, :] = jnp.broadcast_to(power, (EXTRA, 2 * units)).astype(bf16)
 
+    turned[...] = both[...].T
+    left = lax.broadcasted_iota(jnp.int32, (BLOCK, count), 1) < half
+
     def backward(g, carry):
         at = pl.ds(pl.multiple_of(g * 2 * BLOCK, BLOCK), 2 * BLOCK)
-        back = jnp.exp2(-w_ref[g, 2 * BLOCK + 2 : 2 * BLOCK + 3, : 2 * BLOCK].astype(f32))
-        pair = lax.dot_general(
-            both[...], full[at, :], (((1,), (1,)), ((), ())), preferred_element_type=f32
-        )
-        pair = (pair * back).astype(bf16)
-        for i in range(2):
-            share_ref[2 * g + i, :half, :] = pair[i * half : (i + 1) * half]
-            share_ref[2 * g + i, half:, :BLOCK] = block_ref[SPLIT : SPLIT + rest, :]
-            share_ref[2 * g + i, half:, BLOCK:] = block_ref[SPLIT + rest :, :]
-        deliver(g).start()
+        back = jnp.exp2(-w_ref[g, 2 * BLOCK + 2 : 2 * BLOCK + 3, :count].astype(f32))
+        pair = jnp.dot(full[at, :], turned[...], preferred_element_type=f32) * back
+        upper, lower = pair[:BLOCK], pair[BLOCK:]
+        first = jnp.where(left, upper, pltpu.roll(lower, half, 1))
+        second = jnp.where(left, pltpu.roll(upper, half, 1), lower)
+        share_ref[2 * g, :BLOCK, :] = first.astype(bf16)
+        share_ref[2 * g + 1, :BLOCK, :] = second.astype(bf16)
+        share_ref[2 * g, BLOCK:, :] = block_ref[SPLIT:, :]
+        share_ref[2 * g + 1, BLOCK:, :] = block_ref[SPLIT:, :]
         return carry
 
-    def finish(g, carry):
-        deliver(g).wait()
-        return carry
-
-    lax.fori_loop(0, groups, backward, 0)
-    lax.fori_loop(0, groups, finish, 0)
+    lax.fori_loop(0, groups, backward, 0, unroll=groups)
+
+
+def add_up(shares_ref, out_ref):
+    half = out_ref.shape[0]
+    total = shares_ref[0, :BLOCK, :].astype(f32)
+    for i in range(1, shares_ref.shape[0]):
+        total = total + shares_ref[i, :BLOCK, :].astype(f32)
+    total = total.T
+    out_ref[:, :BLOCK] = total[:half].astype(bf16)
+    out_ref[:, BLOCK:] = total[half:].astype(bf16)
 
 
 def weight_gradients(
-    both_ref, got_ref, shares_ref, gate_keep, up_keep, gate_ref, up_ref, columns, both, sems
+    both_ref, got_ref, shares_ref, gate_keep, up_keep, gate_ref, up_ref, columns, both, total, sems
 ):
     sources, units = both_ref.shape[0], gate_ref.shape[1]
     count = columns.shape[1] // sources
@@ -155,30 +158,35 @@
 
     for c in range(sources):
         fetch(c).start()
-    for c in range(sources):
-        fetch(c).wait()
-        back = jnp.exp2(-both[c, count : count + 1, :BLOCK].astype(f32)).astype(bf16)
-        for h in range(2):
-            tile = jnp.concatenate(
-                [
-                    got_ref[2 * c + h, count:, :],
-                    shares_ref[2 * c + h, count // 2 :, :BLOCK],
-                    shares_ref[2 * c + h, count // 2 :, BLOCK:],
-                ],
-                axis=0,
+    part, step = sources // PARTS, 256
+    for p in range(PARTS):
+        for c in range(p * part, (p + 1) * part):
+            fetch(c).wait()
+            back = jnp.exp2(-both[c, count : count + 1, :BLOCK].astype(f32)).astype(bf16)
+            for h in range(2):
+                tile = jnp.concatenate(
+                    [got_ref[2 * c + h, count:, :], shares_ref[2 * c + h, BLOCK:, :]], axis=0
+                )
+                columns[h * BLOCK : (h + 1) * BLOCK, c * count : (c + 1) * count] = (tile * back).T
+        inner = slice(p * part * count, (p + 1) * part * count)
+        for n in range(0, 2 * units, step):
+            at = slice(n, n + step)
+            right = jnp.concatenate(
+                [both[c, :count, at] for c in range(p * part, (p + 1) * part)], axis=0
             )
-            columns[h * BLOCK : (h + 1) * BLOCK, c * count : (c + 1) * count] = (tile * back).T
-    step = 256
-    for ref, keep, start in ((gate_ref, gate_keep, 0), (up_ref, up_keep, units)):
-        for n in range(0, units, step):
-            at = slice(start + n, start + n + step)
-            right = jnp.concatenate([both[c, :count, at] for c in range(sources)], axis=0)
-            grad = jnp.dot(columns[...], right, preferred_element_type=f32)
+            term = jnp.dot(columns[:, inner], right, preferred_element_type=f32)
+            if p > 0:
+                term = total[:, at] + term
+            if p < PARTS - 1:
+                total[:, at] = term
+                continue
+            ref, keep = (gate_ref, gate_keep) if n < units else (up_ref, up_keep)
             for h in range(2):
                 for j in range(step // BLOCK):
-                    tile = grad[h * BLOCK : (h + 1) * BLOCK, j * BLOCK : (j + 1) * BLOCK]
-                    mask = keep[h, n // BLOCK + j].astype(f32)
-                    ref[h * BLOCK : (h + 1) * BLOCK, n + j * BLOCK : n + (j + 1) * BLOCK] = tile * mask
+                    tile = term[h * BLOCK : (h + 1) * BLOCK, j * BLOCK : (j + 1) * BLOCK]
+                    start = n % units + j * BLOCK
+                    mask = keep[h, start // BLOCK].astype(f32)
+                    ref[h * BLOCK : (h + 1) * BLOCK, start : start + BLOCK] = tile * mask
 
 
 def kernel(body, outs, specs, scratch, sems, megabytes, flops):
@@ -227,18 +235,18 @@
         [
             ((count, units), bf16),
             ((count + EXTRA, 2 * units), bf16),
-            ((rows, count - SPLIT // 2, 2 * width), bf16),
+            ((rows, BLOCK + count - SPLIT, count), bf16),
         ],
-        "vhvvvvh",
+        "vhvvvvv",
         [
             (count, rows * width),
             (rows * width, 2 * units),
             (count, 2 * units),
             (cols, 2 * BLOCK + MARKS, units),
-            (rows, count - SPLIT // 2, 2 * width),
+            (2 * units, count),
             (f32, count, 2 * units),
         ],
-        [cols, cols],
+        [cols],
         48,
         8 * count * rows * width * units,
     )(got, weights, cotangent, block)
@@ -247,14 +255,14 @@
 
     both_all = lax.all_gather(sent[: count + MARKS].astype(f16), "col", axis=0).astype(bf16)
 
-    total = jnp.sum(shares[:, : count // 2].astype(f32), axis=0).astype(bf16)
+    (total,) = kernel(add_up, [((count // 2, 2 * width), bf16)], "vv", [], [], 48, 10**6)(shares)
     grad_tokens = lax.ppermute(total, ("row", "col"), route)
 
     grad_gate, grad_up = kernel(
         weight_gradients,
         [((2 * BLOCK, units), f32)] * 2,
         "hvvssvv",
-        [(2 * BLOCK, cols * count), (cols, count + MARKS, 2 * units)],
+        [(2 * BLOCK, cols * count), (cols, count + MARKS, 2 * units), (f32, 2 * BLOCK, 2 * units)],
         [cols],
         48,
         8 * BLOCK * cols * count * units,

time: 146 us -> 140 us (0.959)
  Pallas kernels: 19.1 us -> 13.4 us
    pallas_call x1, Pallas kernels: 11.9 us -> 5.95 us  [shards(): kernel(forward, [((count, units), bf16), ((count + EXTRA, 2 * units), bf1...]
  transfers between devices with their start and end apart: 4 -> 4, of which waited for: 1 -> 1; matrix products, arithmetic and copies ran while one was open for 4% -> 5% of each run, Pallas kernels for 4% -> 4%
where the time goes in v6:
time: 140 us; the launch traced here: 137 us
  blocking collectives  72.1 us (51%)
  starting transfers between devices  37.3 us (27%)
  Pallas kernels  13.4 us (10%)
  other arithmetic  6.27 us (4%)
  local copies, waits for them, and re-layouts  5.79 us (4%)
  waiting for transfers between devices  1.87 us (1%)
    all_gather x1, blocking collectives, shards(): weights = lax.all_gather(packed, 'col', axis=0).astype(bf16)  39.4 us
    all_gather x1, blocking collectives, shards(): lax.all_gather(sent[:count + MARKS].astype(f16), 'col', axis=0).astype(bf16)  32.7 us
    all_to_all x1, starting transfers between devices, shards(): got = lax.all_to_all(copies, 'row', 0, 0, tiled=True)  15.5 us
    all_to_all x1, starting transfers between devices, shards(): shares = lax.all_to_all(share, 'row', 0, 0, tiled=True)  9.49 us
    ppermute x1, starting transfers between devices, shards(): grad_tokens = lax.ppermute(total, ('row', 'col'), route)  6.34 us
    ppermute x1, starting transfers between devices, shards(): block = lax.ppermute(tokens, ('row', 'col'), route)  6.04 us
    pallas_call x1, Pallas kernels, shards(): kernel(forward, [((count, units), bf16), ((count + EXTRA, 2 * units), bf1...  5.95 us
    unnamed x19, local copies, waits for them, and re-layouts  5.79 us
  transfers between devices with their start and end apart: 4, of which 1 were waited for; matrix products, arithmetic and copies ran while one was open for 5% of the time, Pallas kernels for 4%

profile of v6, /device:TPU:1, one launch (start us, length us, event | category | flops | bytes accessed | tf_op | source)
XLA Modules:
  0.0 137.5 jit_solution(12822183743353355051)
XLA Ops:
  0.6 6.0 %collective-permute-start = (bf16[128,128]{1,0:T(8,128)(2,1)}, bf16[128,128]{1,0:T(8,128)(2,1)S(1)}, u32[]{:S(2)}, u32[]{:S(2)}) collective-permute-start(bf16[128,128]{1,0:T(8,128)(2,1)} %tokens_ref.1), channel_id=1, source_target_pairs={{0,0},{1,32},{2,64},{3,96},{4,128},{5,160},{6,192},{7,224},{8,256}... | collective-permute-start | bytes 98312 | tf_op jit(solution)/shard_map/ppermute | solution.py:218
  6.7 0.0 copy-start.1
  6.7 0.9 copy-done.1
  7.6 0.0 copy-start.2
  7.6 0.9 copy-done.2
  8.6 0.0 copy-start.4
  8.6 0.7 copy-done.4
  9.3 0.7 copy-done.6
  9.9 0.8 shard_map.94
  10.8 0.0 collective-permute-done.block_ref
  10.8 0.0 copy-start.3
  10.8 0.7 copy-done.3
  11.5 1.5 %shard_map.93 = bf16[32,192,128]{2,1,0:T(8,128)(2,1)} custom-call(bf16[128,128]{1,0:T(8,128)(2,1)S(1)} %copy-done.3, bf16[128,128]{1,0:T(8,128)(2,1)S(1)} %collective-permute-done.block_ref), custom_call_target="tpu_custom_call" | custom-call | flops 1 | bytes 4194304 | tf_op jit(solution)/shard_map/pallas_call | solution.py:225
  13.0 15.5 %all-to-all-start = ((bf16[32,192,128]{2,1,0:T(8,128)(2,1)}), bf16[32,192,128]{2,1,0:T(8,128)(2,1)S(1)}, u32[]{:S(2)}, u32[]{:S(2)}) async-start(bf16[32,192,128]{2,1,0:T(8,128)(2,1)} %shard_map.93), calls=%async_computation | async-start | bytes 3145728 | tf_op jit(solution)/shard_map/all_to_all | solution.py:229
  28.5 39.4 %all-gather.4 = f16[4224,512]{1,0:T(8,128)(2,1)S(1)} all-gather(f16[264,512]{1,0:T(8,128)(2,1)S(1)} %slice_convert_fusion.1), channel_id=2, replica_groups=mesh['row'=32,'col'=16] {'col'}, dimensions={0}, use_global_device_ids=true | all-gather | bytes 4595712 | tf_op jit(solution)/shard_map/all_gather | solution.py:231
  67.9 2.8 %convert_element_type.16 = bf16[4224,512]{1,0:T(8,128)(2,1)} convert(f16[4224,512]{1,0:T(8,128)(2,1)S(1)} %all-gather.4) | non-fusion elementwise | flops 2162688 | bytes 8650752 | tf_op jit(solution)/shard_map/convert_element_type | solution.py:231
  70.7 0.0 all-to-all-done.got_ref
  70.7 0.0 copy-done.8
  70.7 5.9 %shard_map.95 = (bf16[128,512]{1,0:T(8,128)(2,1)}, bf16[144,1024]{1,0:T(8,128)(2,1)S(1)}, bf16[32,192,128]{2,1,0:T(8,128)(2,1)S(1)}) custom-call(bf16[32,192,128]{2,1,0:T(8,128)(2,1)S(1)} %all-to-all-done.got_ref, bf16[16,264,512]{2,1,0:T(8,128)(2,1)} %bitcast.3, bf16[128,512]{1,0:T(8,128)(2,1)S(1)} %copy-done.8, ...), custom_call_target="tpu_custom_call" | custom-call | flops 2147483648 | bytes 4194304 | tf_op jit(solution)/shard_map/pallas_call | solution.py:233
  76.7 0.0 copy-start
  76.7 1.2 copy-done
  77.8 9.5 %all-to-all-start.1 = ((bf16[32,192,128]{2,1,0:T(8,128)(2,1)}), bf16[32,192,128]{2,1,0:T(8,128)(2,1)S(1)}, u32[]{:S(2)}, u32[]{:S(2)}) async-start(bf16[32,192,128]{2,1,0:T(8,128)(2,1)} %copy-done), calls=%async_computation.1 | async-start | bytes 3145728 | tf_op jit(solution)/shard_map/all_to_all | solution.py:254
  87.4 32.7 %all-gather.5 = f16[2176,1024]{1,0:T(8,128)(2,1)S(1)} all-gather(f16[136,1024]{1,0:T(8,128)(2,1)S(1)} %slice_convert_fusion), channel_id=3, replica_groups=mesh['row'=32,'col'=16] {'col'}, dimensions={0}, use_global_device_ids=true | all-gather | bytes 4734976 | tf_op jit(solution)/shard_map/all_gather | solution.py:256
  120.1 3.3 %convert_element_type.17 = bf16[2176,1024]{1,0:T(8,128)(2,1)} convert(f16[2176,1024]{1,0:T(8,128)(2,1)S(1)} %all-gather.5) | non-fusion elementwise | flops 2228224 | bytes 8912896 | tf_op jit(solution)/shard_map/convert_element_type | solution.py:256
  123.4 1.9 %all-to-all-done.1.shares_ref = bf16[32,192,128]{2,1,0:T(8,128)(2,1)S(1)} async-done(((bf16[32,192,128]{2,1,0:T(8,128)(2,1)}), bf16[32,192,128]{2,1,0:T(8,128)(2,1)S(1)}, u32[]{:S(2)}, u32[]{:S(2)}) %all-to-all-start.1) | async-done | bytes 1572896 | tf_op jit(solution)/shard_map/all_to_all | solution.py:254
  125.3 0.2 shard_map.96
  125.5 6.3 %collective-permute-start.1 = (bf16[64,256]{1,0:T(8,128)(2,1)S(1)}, bf16[64,256]{1,0:T(8,128)(2,1)S(1)}, u32[]{:S(2)}, u32[]{:S(2)}) collective-permute-start(bf16[64,256]{1,0:T(8,128)(2,1)S(1)} %shard_map.96), channel_id=1, source_target_pairs={{0,0},{1,32},{2,64},{3,96},{4,128},{5,160},{6,192},{7,224},{8,256}... | collective-permute-start | bytes 98312 | tf_op jit(solution)/shard_map/ppermute | solution.py:259
  131.9 0.0 copy-done.5
  131.9 0.0 copy-done.7
  131.9 5.0 %shard_map.97 = (f32[256,512]{1,0:T(8,128)}, f32[256,512]{1,0:T(8,128)}) custom-call(bf16[16,136,1024]{2,1,0:T(8,128)(2,1)} %bitcast.2, bf16[32,192,128]{2,1,0:T(8,128)(2,1)S(1)} %all-to-all-done.got_ref, bf16[32,192,128]{2,1,0:T(8,128)(2,1)S(1)} %all-to-all-done.1.shares_ref, s32[2,4]{1,0:T(2,128)S(1)} %copy-done.5, s32[2,4]{1,0:T(2,128)S(1)} %copy-done.7), custom_call_target="tpu_custom_call" | custom-call | flops 1073741824 | bytes 4194304 | tf_op jit(solution)/shard_map/pallas_call | solution.py:261
  136.9 0.0 collective-permute-done.1
  136.9 0.6 copy.11
  (6 shorter events, 0.1 us)
Async XLA Ops:
  0.6 10.1 %collective-permute-start = (bf16[128,128]{1,0:T(8,128)(2,1)}, bf16[128,128]{1,0:T(8,128)(2,1)S(1)}, u32[]{:S(2)}, u32[]{:S(2)}) collective-permute-start(bf16[128,128]{1,0:T(8,128)(2,1)} %tokens_ref.1), channel_id=1, source_target_pairs={{0,0},{1,32},{2,64},{3,96},{4,128},{5,160},{6,192},{7,224},{8,256}... | collective-permute-start | bytes 98312 | tf_op jit(solution)/shard_map/ppermute | solution.py:218
  6.7 1.0 copy-start.1
  7.6 0.9 copy-start.2
  8.6 0.7 copy-start.4
  9.3 0.7 copy-start.6
  10.8 0.8 copy-start.3
  13.0 57.7 %all-to-all-start = ((bf16[32,192,128]{2,1,0:T(8,128)(2,1)}), bf16[32,192,128]{2,1,0:T(8,128)(2,1)S(1)}, u32[]{:S(2)}, u32[]{:S(2)}) async-start(bf16[32,192,128]{2,1,0:T(8,128)(2,1)} %shard_map.93), calls=%async_computation | async-start | bytes 3145728 | tf_op jit(solution)/shard_map/all_to_all | solution.py:229
  67.9 2.8 %copy-start.8 = (bf16[128,512]{1,0:T(8,128)(2,1)S(1)}, bf16[128,512]{1,0:T(8,128)(2,1)}, u32[]{:S(2)}) copy-start(bf16[128,512]{1,0:T(8,128)(2,1)} %grad_ref.1) | copy-start | bytes 393220
  76.7 1.2 copy-start
  77.8 47.5 %all-to-all-start.1 = ((bf16[32,192,128]{2,1,0:T(8,128)(2,1)}), bf16[32,192,128]{2,1,0:T(8,128)(2,1)S(1)}, u32[]{:S(2)}, u32[]{:S(2)}) async-start(bf16[32,192,128]{2,1,0:T(8,128)(2,1)} %copy-done), calls=%async_computation.1 | async-start | bytes 3145728 | tf_op jit(solution)/shard_map/all_to_all | solution.py:254
  120.1 11.8 %copy-start.5 = (s32[2,4]{1,0:T(2,128)S(1)}, s32[2,4]{1,0:T(2,128)}, u32[]{:S(2)}) copy-start(s32[2,4]{1,0:T(2,128)} %gate_keep.3) | copy-start | bytes 100
  120.1 11.8 %copy-start.7 = (s32[2,4]{1,0:T(2,128)S(1)}, s32[2,4]{1,0:T(2,128)}, u32[]{:S(2)}) copy-start(s32[2,4]{1,0:T(2,128)} %up_keep.3) | copy-start | bytes 100
  125.5 11.4 %collective-permute-start.1 = (bf16[64,256]{1,0:T(8,128)(2,1)S(1)}, bf16[64,256]{1,0:T(8,128)(2,1)S(1)}, u32[]{:S(2)}, u32[]{:S(2)}) collective-permute-start(bf16[64,256]{1,0:T(8,128)(2,1)S(1)} %shard_map.96), channel_id=1, source_target_pairs={{0,0},{1,32},{2,64},{3,96},{4,128},{5,160},{6,192},{7,224},{8,256}... | collective-permute-start | bytes 98312 | tf_op jit(solution)/shard_map/ppermute | solution.py:259

commit v7 on v6

--- a/solution.py
+++ b/solution.py
@@ -25,8 +25,9 @@
     return jnp.max(jnp.max(jnp.abs(values), axis=0, keepdims=True), axis=1, keepdims=True)
 
 
-def pack(gate_ref, up_ref, gate_keep, up_keep, packed_ref):
+def pack(gate_ref, up_ref, tokens_ref, gate_keep, up_keep, packed_ref, same_ref):
     units = gate_ref.shape[1]
+    same_ref[...] = tokens_ref[...]
     line = lax.broadcasted_iota(jnp.int32, (EXTRA, BLOCK), 0)
     tiles, marks = [], []
     for ref, keep in ((gate_ref, gate_keep), (up_ref, up_keep)):
@@ -115,8 +116,10 @@
         both[:, units + n : units + n + step] = d_up.astype(bf16)
 
     power = exponent(largest)
-    sent_ref[:count, :] = (both[...].astype(f32) * jnp.exp2(power)).astype(bf16)
-    sent_ref[count:, :] = jnp.broadcast_to(power, (EXTRA, 2 * units)).astype(bf16)
+    scaled = (both[...].astype(f32) * jnp.exp2(power)).astype(bf16)
+    sent_ref[:count, :] = scaled[:, :units]
+    sent_ref[count : 2 * count, :] = scaled[:, units:]
+    sent_ref[2 * count :, :] = jnp.broadcast_to(power, (EXTRA, units)).astype(bf16)
 
     turned[...] = both[...].T
     left = lax.broadcasted_iota(jnp.int32, (BLOCK, count), 1) < half
@@ -148,7 +151,7 @@
 
 
 def weight_gradients(
-    both_ref, got_ref, shares_ref, gate_keep, up_keep, gate_ref, up_ref, columns, both, total, sems
+    both_ref, got_ref, shares_ref, gate_keep, up_keep, gate_ref, up_ref, columns, both, total, sems, out_sems
 ):
     sources, units = both_ref.shape[0], gate_ref.shape[1]
     count = columns.shape[1] // sources
@@ -159,10 +162,11 @@
     for c in range(sources):
         fetch(c).start()
     part, step = sources // PARTS, 256
+    copies = []
     for p in range(PARTS):
         for c in range(p * part, (p + 1) * part):
             fetch(c).wait()
-            back = jnp.exp2(-both[c, count : count + 1, :BLOCK].astype(f32)).astype(bf16)
+            back = jnp.exp2(-both[c, 2 * count : 2 * count + 1, :BLOCK].astype(f32)).astype(bf16)
             for h in range(2):
                 tile = jnp.concatenate(
                     [got_ref[2 * c + h, count:, :], shares_ref[2 * c + h, BLOCK:, :]], axis=0
@@ -170,9 +174,11 @@
                 columns[h * BLOCK : (h + 1) * BLOCK, c * count : (c + 1) * count] = (tile * back).T
         inner = slice(p * part * count, (p + 1) * part * count)
         for n in range(0, 2 * units, step):
-            at = slice(n, n + step)
+            at, start = slice(n, n + step), n % units
+            lines = slice(0, count) if n < units else slice(count, 2 * count)
             right = jnp.concatenate(
-                [both[c, :count, at] for c in range(p * part, (p + 1) * part)], axis=0
+                [both[c, lines, start : start + step] for c in range(p * part, (p + 1) * part)],
+                axis=0,
             )
             term = jnp.dot(columns[:, inner], right, preferred_element_type=f32)
             if p > 0:
@@ -184,9 +190,16 @@
             for h in range(2):
                 for j in range(step // BLOCK):
                     tile = term[h * BLOCK : (h + 1) * BLOCK, j * BLOCK : (j + 1) * BLOCK]
-                    start = n % units + j * BLOCK
-                    mask = keep[h, start // BLOCK].astype(f32)
-                    ref[h * BLOCK : (h + 1) * BLOCK, start : start + BLOCK] = tile * mask
+                    mask = keep[h, start // BLOCK + j].astype(f32)
+                    column = n + j * BLOCK
+                    total[h * BLOCK : (h + 1) * BLOCK, column : column + BLOCK] = tile * mask
+            copy = pltpu.make_async_copy(
+                total.at[:, pl.ds(n, step)], ref.at[:, pl.ds(start, step)], out_sems.at[n // step]
+            )
+            copy.start()
+            copies.append(copy)
+    for copy in copies:
+        copy.wait()
 
 
 def kernel(body, outs, specs, scratch, sems, megabytes, flops):
@@ -217,14 +230,20 @@
     ]
     block = lax.ppermute(tokens, ("row", "col"), route)
 
-    (packed,) = kernel(
-        pack, [((2 * BLOCK + EXTRA, units), bf16)], "vvssv", [], [], 8, 4 * BLOCK * units
-    )(gate_weight, up_weight, gate_keep, up_keep)
+    packed, same = kernel(
+        pack,
+        [((2 * BLOCK + EXTRA, units), bf16), ((count, width), bf16)],
+        "vvvssvv",
+        [],
+        [],
+        8,
+        4 * BLOCK * units,
+    )(gate_weight, up_weight, tokens, gate_keep, up_keep)
     packed = packed[: 2 * BLOCK + MARKS].astype(f16)
 
     (copies,) = kernel(
         spread, [((rows, count + SPLIT, width), bf16)], "vvh", [(count + SPLIT, width)], [rows], 48, 1
-    )(tokens, block)
+    )(same, block)
     copies, packed = lax.optimization_barrier((copies, packed))
     got = lax.all_to_all(copies, "row", 0, 0, tiled=True)
 
@@ -234,7 +253,7 @@
         forward,
         [
             ((count, units), bf16),
-            ((count + EXTRA, 2 * units), bf16),
+            ((2 * count + EXTRA, units), bf16),
             ((rows, BLOCK + count - SPLIT, count), bf16),
         ],
         "vhvvvvv",
@@ -253,7 +272,7 @@
 
     shares = lax.all_to_all(share, "row", 0, 0, tiled=True)
 
-    both_all = lax.all_gather(sent[: count + MARKS].astype(f16), "col", axis=0).astype(bf16)
+    both_all = lax.all_gather(sent[: 2 * count + MARKS].astype(f16), "col", axis=0).astype(bf16)
 
     (total,) = kernel(add_up, [((count // 2, 2 * width), bf16)], "vv", [], [], 48, 10**6)(shares)
     grad_tokens = lax.ppermute(total, ("row", "col"), route)
@@ -261,9 +280,9 @@
     grad_gate, grad_up = kernel(
         weight_gradients,
         [((2 * BLOCK, units), f32)] * 2,
-        "hvvssvv",
-        [(2 * BLOCK, cols * count), (cols, count + MARKS, 2 * units), (f32, 2 * BLOCK, 2 * units)],
-        [cols],
+        "hvvsshh",
+        [(2 * BLOCK, cols * count), (cols, 2 * count + MARKS, units), (f32, 2 * BLOCK, 2 * units)],
+        [cols, 4],
         48,
         8 * BLOCK * cols * count * units,
     )(both_all, got, shares, gate_keep, up_keep)

time: 140 us -> 139 us (level)
  transfers between devices with their start and end apart: 4 -> 4, of which waited for: 1 -> 1; matrix products, arithmetic and copies ran while one was open for 5% -> 4% of each run, Pallas kernels for 4% -> 4%
where the time goes in v7:
time: 139 us; the launch traced here: 138 us
  blocking collectives  70.8 us (51%)
  starting transfers between devices  37.9 us (27%)
  Pallas kernels  13.5 us (10%)
  local copies, waits for them, and re-layouts  5.8 us (4%)
  other arithmetic  5.74 us (4%)
  waiting for transfers between devices  3.14 us (2%)
    all_gather x1, blocking collectives, shards(): weights = lax.all_gather(packed, 'col', axis=0).astype(bf16)  38.9 us
    all_gather x1, blocking collectives, shards(): lax.all_gather(sent[:2 * count + MARKS].astype(f16), 'col', axis=0)  31.9 us
    all_to_all x1, starting transfers between devices, shards(): got = lax.all_to_all(copies, 'row', 0, 0, tiled=True)  15.2 us
    all_to_all x1, starting transfers between devices, shards(): shares = lax.all_to_all(share, 'row', 0, 0, tiled=True)  9.49 us
    ppermute x1, starting transfers between devices, shards(): grad_tokens = lax.ppermute(total, ('row', 'col'), route)  7.11 us
    ppermute x1, starting transfers between devices, shards(): block = lax.ppermute(tokens, ('row', 'col'), route)  6.04 us
    pallas_call x1, Pallas kernels, shards(): kernel(forward, [((count, units), bf16), ((2 * count + EXTRA, units), bf1...  5.94 us
    unnamed x19, local copies, waits for them, and re-layouts  5.8 us
  transfers between devices with their start and end apart: 4, of which 1 were waited for; matrix products, arithmetic and copies ran while one was open for 4% of the time, Pallas kernels for 4%

profile of v7, /device:TPU:1, one launch (start us, length us, event | category | flops | bytes accessed | tf_op | source)
XLA Modules:
  0.0 137.6 jit_solution(1054628276087046783)
XLA Ops:
  0.6 6.0 %collective-permute-start = (bf16[128,128]{1,0:T(8,128)(2,1)}, bf16[128,128]{1,0:T(8,128)(2,1)S(1)}, u32[]{:S(2)}, u32[]{:S(2)}) collective-permute-start(bf16[128,128]{1,0:T(8,128)(2,1)} %tokens_ref.1), channel_id=1, source_target_pairs={{0,0},{1,32},{2,64},{3,96},{4,128},{5,160},{6,192},{7,224},{8,256}... | collective-permute-start | bytes 98312 | tf_op jit(solution)/shard_map/ppermute | solution.py:231
  6.7 0.0 copy-start.1
  6.7 0.9 copy-done.1
  7.6 0.0 copy-start.2
  7.6 0.9 copy-done.2
  8.6 0.0 copy-start.3
  8.6 0.8 copy-done.3
  9.3 0.0 copy-start.4
  9.3 0.7 copy-done.4
  10.0 0.7 copy-done.6
  10.7 0.8 shard_map.93
  11.5 0.0 collective-permute-done.block_ref
  11.5 1.5 %shard_map.94 = bf16[32,192,128]{2,1,0:T(8,128)(2,1)} custom-call(bf16[128,128]{1,0:T(8,128)(2,1)S(1)} %get-tuple-element.13.tokens_ref, bf16[128,128]{1,0:T(8,128)(2,1)S(1)} %collective-permute-done.block_ref), custom_call_target="tpu_custom_call" | custom-call | flops 1 | bytes 4194304 | tf_op jit(solution)/shard_map/pallas_call | solution.py:244
  13.0 15.2 %all-to-all-start = ((bf16[32,192,128]{2,1,0:T(8,128)(2,1)}), bf16[32,192,128]{2,1,0:T(8,128)(2,1)S(1)}, u32[]{:S(2)}, u32[]{:S(2)}) async-start(bf16[32,192,128]{2,1,0:T(8,128)(2,1)} %shard_map.94), calls=%async_computation | async-start | bytes 3145728 | tf_op jit(solution)/shard_map/all_to_all | solution.py:248
  28.3 38.9 %all-gather.4 = f16[4224,512]{1,0:T(8,128)(2,1)S(1)} all-gather(f16[264,512]{1,0:T(8,128)(2,1)S(1)} %slice_convert_fusion.1), channel_id=2, replica_groups=mesh['row'=32,'col'=16] {'col'}, dimensions={0}, use_global_device_ids=true | all-gather | bytes 4595712 | tf_op jit(solution)/shard_map/all_gather | solution.py:250
  67.1 2.8 %convert_element_type.16 = bf16[4224,512]{1,0:T(8,128)(2,1)} convert(f16[4224,512]{1,0:T(8,128)(2,1)S(1)} %all-gather.4) | non-fusion elementwise | flops 2162688 | bytes 8650752 | tf_op jit(solution)/shard_map/convert_element_type | solution.py:250
  69.9 0.0 all-to-all-done.got_ref
  69.9 0.0 copy-done.8
  69.9 5.9 %shard_map.95 = (bf16[128,512]{1,0:T(8,128)(2,1)}, bf16[272,512]{1,0:T(8,128)(2,1)S(1)}, bf16[32,192,128]{2,1,0:T(8,128)(2,1)S(1)}) custom-call(bf16[32,192,128]{2,1,0:T(8,128)(2,1)S(1)} %all-to-all-done.got_ref, bf16[16,264,512]{2,1,0:T(8,128)(2,1)} %bitcast.3, bf16[128,512]{1,0:T(8,128)(2,1)S(1)} %copy-done.8, ...), custom_call_target="tpu_custom_call" | custom-call | flops 2147483648 | bytes 4194304 | tf_op jit(solution)/shard_map/pallas_call | solution.py:252
  75.9 0.0 copy-start
  75.9 1.2 copy-done
  77.1 9.5 %all-to-all-start.1 = ((bf16[32,192,128]{2,1,0:T(8,128)(2,1)}), bf16[32,192,128]{2,1,0:T(8,128)(2,1)S(1)}, u32[]{:S(2)}, u32[]{:S(2)}) async-start(bf16[32,192,128]{2,1,0:T(8,128)(2,1)} %copy-done), calls=%async_computation.1 | async-start | bytes 3145728 | tf_op jit(solution)/shard_map/all_to_all | solution.py:273
  86.6 31.9 %all-gather.5 = f16[4224,512]{1,0:T(8,128)(2,1)S(1)} all-gather(f16[264,512]{1,0:T(8,128)(2,1)S(1)} %slice_convert_fusion), channel_id=3, replica_groups=mesh['row'=32,'col'=16] {'col'}, dimensions={0}, use_global_device_ids=true | all-gather | bytes 4595712 | tf_op jit(solution)/shard_map/all_gather | solution.py:275
  118.6 2.8 %convert_element_type.17 = bf16[4224,512]{1,0:T(8,128)(2,1)} convert(f16[4224,512]{1,0:T(8,128)(2,1)S(1)} %all-gather.5) | non-fusion elementwise | flops 2162688 | bytes 8650752 | tf_op jit(solution)/shard_map/convert_element_type | solution.py:275
  121.4 3.1 %all-to-all-done.1.shares_ref = bf16[32,192,128]{2,1,0:T(8,128)(2,1)S(1)} async-done(((bf16[32,192,128]{2,1,0:T(8,128)(2,1)}), bf16[32,192,128]{2,1,0:T(8,128)(2,1)S(1)}, u32[]{:S(2)}, u32[]{:S(2)}) %all-to-all-start.1) | async-done | bytes 1572896 | tf_op jit(solution)/shard_map/all_to_all | solution.py:273
  124.5 0.2 shard_map.96
  124.7 7.1 %collective-permute-start.1 = (bf16[64,256]{1,0:T(8,128)(2,1)S(1)}, bf16[64,256]{1,0:T(8,128)(2,1)S(1)}, u32[]{:S(2)}, u32[]{:S(2)}) collective-permute-start(bf16[64,256]{1,0:T(8,128)(2,1)S(1)} %shard_map.96), channel_id=1, source_target_pairs={{0,0},{1,32},{2,64},{3,96},{4,128},{5,160},{6,192},{7,224},{8,256}... | collective-permute-start | bytes 98312 | tf_op jit(solution)/shard_map/ppermute | solution.py:278
  131.9 0.0 copy-done.5
  131.9 0.0 copy-done.7
  131.9 5.1 %shard_map.97 = (f32[256,512]{1,0:T(8,128)}, f32[256,512]{1,0:T(8,128)}) custom-call(bf16[16,264,512]{2,1,0:T(8,128)(2,1)} %bitcast.2, bf16[32,192,128]{2,1,0:T(8,128)(2,1)S(1)} %all-to-all-done.got_ref, bf16[32,192,128]{2,1,0:T(8,128)(2,1)S(1)} %all-to-all-done.1.shares_ref, s32[2,4]{1,0:T(2,128)S(1)} %copy-done.5, s32[2,4]{1,0:T(2,128)S(1)} %copy-done.7), custom_call_target="tpu_custom_call" | custom-call | flops 1073741824 | bytes 4194304 | tf_op jit(solution)/shard_map/pallas_call | solution.py:280
  137.0 0.0 collective-permute-done.1
  137.0 0.6 copy.11
  (6 shorter events, 0.1 us)
Async XLA Ops:
  0.6 10.9 %collective-permute-start = (bf16[128,128]{1,0:T(8,128)(2,1)}, bf16[128,128]{1,0:T(8,128)(2,1)S(1)}, u32[]{:S(2)}, u32[]{:S(2)}) collective-permute-start(bf16[128,128]{1,0:T(8,128)(2,1)} %tokens_ref.1), channel_id=1, source_target_pairs={{0,0},{1,32},{2,64},{3,96},{4,128},{5,160},{6,192},{7,224},{8,256}... | collective-permute-start | bytes 98312 | tf_op jit(solution)/shard_map/ppermute | solution.py:231
  6.7 1.0 copy-start.1
  7.6 0.9 copy-start.2
  8.6 0.8 copy-start.3
  9.3 0.7 copy-start.4
  10.0 0.7 copy-start.6
  13.0 56.9 %all-to-all-start = ((bf16[32,192,128]{2,1,0:T(8,128)(2,1)}), bf16[32,192,128]{2,1,0:T(8,128)(2,1)S(1)}, u32[]{:S(2)}, u32[]{:S(2)}) async-start(bf16[32,192,128]{2,1,0:T(8,128)(2,1)} %shard_map.94), calls=%async_computation | async-start | bytes 3145728 | tf_op jit(solution)/shard_map/all_to_all | solution.py:248
  67.1 2.8 %copy-start.8 = (bf16[128,512]{1,0:T(8,128)(2,1)S(1)}, bf16[128,512]{1,0:T(8,128)(2,1)}, u32[]{:S(2)}) copy-start(bf16[128,512]{1,0:T(8,128)(2,1)} %grad_ref.1) | copy-start | bytes 393220
  75.9 1.2 copy-start
  77.1 47.5 %all-to-all-start.1 = ((bf16[32,192,128]{2,1,0:T(8,128)(2,1)}), bf16[32,192,128]{2,1,0:T(8,128)(2,1)S(1)}, u32[]{:S(2)}, u32[]{:S(2)}) async-start(bf16[32,192,128]{2,1,0:T(8,128)(2,1)} %copy-done), calls=%async_computation.1 | async-start | bytes 3145728 | tf_op jit(solution)/shard_map/all_to_all | solution.py:273
  118.6 13.3 %copy-start.5 = (s32[2,4]{1,0:T(2,128)S(1)}, s32[2,4]{1,0:T(2,128)}, u32[]{:S(2)}) copy-start(s32[2,4]{1,0:T(2,128)} %gate_keep.3) | copy-start | bytes 100
  118.6 13.3 %copy-start.7 = (s32[2,4]{1,0:T(2,128)S(1)}, s32[2,4]{1,0:T(2,128)}, u32[]{:S(2)}) copy-start(s32[2,4]{1,0:T(2,128)} %up_keep.3) | copy-start | bytes 100
  124.7 12.3 %collective-permute-start.1 = (bf16[64,256]{1,0:T(8,128)(2,1)S(1)}, bf16[64,256]{1,0:T(8,128)(2,1)S(1)}, u32[]{:S(2)}, u32[]{:S(2)}) collective-permute-start(bf16[64,256]{1,0:T(8,128)(2,1)S(1)} %shard_map.96), channel_id=1, source_target_pairs={{0,0},{1,32},{2,64},{3,96},{4,128},{5,160},{6,192},{7,224},{8,256}... | collective-permute-start | bytes 98312 | tf_op jit(solution)/shard_map/ppermute | solution.py:278

commit v8 on v7

--- a/solution.py
+++ b/solution.py
@@ -62,8 +62,8 @@
 
 
 def forward(
-    got_ref, weights_ref, grad_ref, block_ref, hidden_ref, sent_ref, share_ref,
-    rows, full, both, w_ref, turned, total, sems,
+    got_ref, weights_ref, grad_ref, block_ref, hidden_ref, sent_ref, shares_ref,
+    rows, full, both, w_ref, share_ref, turned, total, sems, out_sems,
 ):
     groups, units = weights_ref.shape[0], weights_ref.shape[2]
     count = grad_ref.shape[0]
@@ -71,6 +71,10 @@
 
     def fetch(g):
         return pltpu.make_async_copy(weights_ref.at[g], w_ref.at[g], sems.at[g])
+
+    def deliver(g):
+        at = pl.ds(2 * g, 2)
+        return pltpu.make_async_copy(share_ref.at[at], shares_ref.at[at], out_sems.at[g])
 
     def begin(g, carry):
         fetch(g).start()
@@ -135,9 +139,15 @@
         share_ref[2 * g + 1, :BLOCK, :] = second.astype(bf16)
         share_ref[2 * g, BLOCK:, :] = block_ref[SPLIT:, :]
         share_ref[2 * g + 1, BLOCK:, :] = block_ref[SPLIT:, :]
+        deliver(g).start()
         return carry
 
+    def finish(g, carry):
+        deliver(g).wait()
+        return carry
+
     lax.fori_loop(0, groups, backward, 0, unroll=groups)
+    lax.fori_loop(0, groups, finish, 0)
 
 
 def add_up(shares_ref, out_ref):
@@ -207,7 +217,10 @@
     places = [pl.BlockSpec(memory_space=spaces[s]) for s in specs]
     return pl.pallas_call(
         body,
-        out_shape=[jax.ShapeDtypeStruct(shape, dtype) for shape, dtype in outs],
+        out_shape=[
+            pltpu.HBM(shape, dtype) if s == "h" else jax.ShapeDtypeStruct(shape, dtype)
+            for s, (shape, dtype) in zip(specs[-len(outs) :], outs)
+        ],
         in_specs=places[: -len(outs)],
         out_specs=places[-len(outs) :],
         scratch_shapes=[
@@ -256,16 +269,17 @@
             ((2 * count + EXTRA, units), bf16),
             ((rows, BLOCK + count - SPLIT, count), bf16),
         ],
-        "vhvvvvv",
+        "vhvvvvh",
         [
             (count, rows * width),
             (rows * width, 2 * units),
             (count, 2 * units),
             (cols, 2 * BLOCK + MARKS, units),
+            (rows, BLOCK + count - SPLIT, count),
             (2 * units, count),
             (f32, count, 2 * units),
         ],
-        [cols],
+        [cols, cols],
         48,
         8 * count * rows * width * units,
     )(got, weights, cotangent, block)

time: 139 us -> 139 us (level)
  Pallas kernels: 13.5 us -> 14.9 us
    unnamed x19 -> x17, local copies, waits for them, and re-layouts: 5.8 us -> 4.64 us
where the time goes in v8:
time: 139 us; the launch traced here: 138 us
  blocking collectives  70.8 us (51%)
  starting transfers between devices  37.9 us (27%)
  Pallas kernels  14.9 us (11%)
  other arithmetic  5.75 us (4%)
  local copies, waits for them, and re-layouts  4.64 us (3%)
  waiting for transfers between devices  3.13 us (2%)
    all_gather x1, blocking collectives, shards(): weights = lax.all_gather(packed, 'col', axis=0).astype(bf16)  38.9 us
    all_gather x1, blocking collectives, shards(): lax.all_gather(sent[:2 * count + MARKS].astype(f16), 'col', axis=0)  31.9 us
    all_to_all x1, starting transfers between devices, shards(): got = lax.all_to_all(copies, 'row', 0, 0, tiled=True)  15.2 us
    all_to_all x1, starting transfers between devices, shards(): shares = lax.all_to_all(share, 'row', 0, 0, tiled=True)  9.51 us
    pallas_call x1, Pallas kernels, shards(): kernel(forward, [((count, units), bf16), ((2 * count + EXTRA, units), bf1...  7.33 us
    ppermute x1, starting transfers between devices, shards(): grad_tokens = lax.ppermute(total, ('row', 'col'), route)  7.11 us
    ppermute x1, starting transfers between devices, shards(): block = lax.ppermute(tokens, ('row', 'col'), route)  6.04 us
    pallas_call x1, Pallas kernels, shards(): kernel(weight_gradients, [((2 * BLOCK, units), f32)] * 2, 'hvvsshh', [(2...  5.13 us
  transfers between devices with their start and end apart: 4, of which 1 were waited for; matrix products, arithmetic and copies ran while one was open for 4% of the time, Pallas kernels for 4%

profile of v8, /device:TPU:1, one launch (start us, length us, event | category | flops | bytes accessed | tf_op | source)
XLA Modules:
  0.0 137.9 jit_solution(14843345985258852271)
XLA Ops:
  0.6 6.0 %collective-permute-start = (bf16[128,128]{1,0:T(8,128)(2,1)}, bf16[128,128]{1,0:T(8,128)(2,1)S(1)}, u32[]{:S(2)}, u32[]{:S(2)}) collective-permute-start(bf16[128,128]{1,0:T(8,128)(2,1)} %tokens_ref.1), channel_id=1, source_target_pairs={{0,0},{1,32},{2,64},{3,96},{4,128},{5,160},{6,192},{7,224},{8,256}... | collective-permute-start | bytes 98312 | tf_op jit(solution)/shard_map/ppermute | solution.py:244
  6.7 0.0 copy-start
  6.7 0.9 copy-done
  7.6 0.0 copy-start.1
  7.6 0.9 copy-done.1
  8.6 0.0 copy-start.2
  8.6 0.8 copy-done.2
  9.3 0.0 copy-start.3
  9.3 0.7 copy-done.3
  10.0 0.0 copy-start.5
  10.0 0.7 copy-done.5
  10.7 0.8 shard_map.93
  11.5 0.0 collective-permute-done.block_ref
  11.5 1.5 %shard_map.94 = bf16[32,192,128]{2,1,0:T(8,128)(2,1)} custom-call(bf16[128,128]{1,0:T(8,128)(2,1)S(1)} %get-tuple-element.13.tokens_ref, bf16[128,128]{1,0:T(8,128)(2,1)S(1)} %collective-permute-done.block_ref), custom_call_target="tpu_custom_call" | custom-call | flops 1 | bytes 4194304 | tf_op jit(solution)/shard_map/pallas_call | solution.py:257
  13.0 15.2 %all-to-all-start = ((bf16[32,192,128]{2,1,0:T(8,128)(2,1)}), bf16[32,192,128]{2,1,0:T(8,128)(2,1)S(1)}, u32[]{:S(2)}, u32[]{:S(2)}) async-start(bf16[32,192,128]{2,1,0:T(8,128)(2,1)} %shard_map.94), calls=%async_computation | async-start | bytes 3145728 | tf_op jit(solution)/shard_map/all_to_all | solution.py:261
  28.3 38.9 %all-gather.4 = f16[4224,512]{1,0:T(8,128)(2,1)S(1)} all-gather(f16[264,512]{1,0:T(8,128)(2,1)S(1)} %slice_convert_fusion.1), channel_id=2, replica_groups=mesh['row'=32,'col'=16] {'col'}, dimensions={0}, use_global_device_ids=true | all-gather | bytes 4595712 | tf_op jit(solution)/shard_map/all_gather | solution.py:263
  67.1 0.0 copy-start.7
  67.1 2.8 %convert_element_type.16 = bf16[4224,512]{1,0:T(8,128)(2,1)} convert(f16[4224,512]{1,0:T(8,128)(2,1)S(1)} %all-gather.4) | non-fusion elementwise | flops 2162688 | bytes 8650752 | tf_op jit(solution)/shard_map/convert_element_type | solution.py:263
  69.9 0.0 all-to-all-done.got_ref
  69.9 0.0 copy-done.7
  69.9 7.3 %shard_map.95 = (bf16[128,512]{1,0:T(8,128)(2,1)}, bf16[272,512]{1,0:T(8,128)(2,1)S(1)}, bf16[32,192,128]{2,1,0:T(8,128)(2,1)}) custom-call(bf16[32,192,128]{2,1,0:T(8,128)(2,1)S(1)} %all-to-all-done.got_ref, bf16[16,264,512]{2,1,0:T(8,128)(2,1)} %bitcast.3, bf16[128,512]{1,0:T(8,128)(2,1)S(1)} %copy-done.7, bf16[128,128]{1,0:T(8,128)(2,1)S(1)} %collective-permute-done.block_ref), custom_call_target="tpu_custom_call" | custom-call | flops 2147483648 | bytes 4194304 | tf_op jit(solution)/shard_map/pallas_call | solution.py:265
  77.3 9.5 %all-to-all-start.1 = ((bf16[32,192,128]{2,1,0:T(8,128)(2,1)}), bf16[32,192,128]{2,1,0:T(8,128)(2,1)S(1)}, u32[]{:S(2)}, u32[]{:S(2)}) async-start(bf16[32,192,128]{2,1,0:T(8,128)(2,1)} %get-tuple-element.18), calls=%async_computation.1 | async-start | bytes 3145728 | tf_op jit(solution)/shard_map/all_to_all | solution.py:287
  86.9 31.9 %all-gather.5 = f16[4224,512]{1,0:T(8,128)(2,1)S(1)} all-gather(f16[264,512]{1,0:T(8,128)(2,1)S(1)} %slice_convert_fusion), channel_id=3, replica_groups=mesh['row'=32,'col'=16] {'col'}, dimensions={0}, use_global_device_ids=true | all-gather | bytes 4595712 | tf_op jit(solution)/shard_map/all_gather | solution.py:289
  118.8 2.8 %convert_element_type.17 = bf16[4224,512]{1,0:T(8,128)(2,1)} convert(f16[4224,512]{1,0:T(8,128)(2,1)S(1)} %all-gather.5) | non-fusion elementwise | flops 2162688 | bytes 8650752 | tf_op jit(solution)/shard_map/convert_element_type | solution.py:289
  121.6 3.1 %all-to-all-done.1.shares_ref = bf16[32,192,128]{2,1,0:T(8,128)(2,1)S(1)} async-done(((bf16[32,192,128]{2,1,0:T(8,128)(2,1)}), bf16[32,192,128]{2,1,0:T(8,128)(2,1)S(1)}, u32[]{:S(2)}, u32[]{:S(2)}) %all-to-all-start.1) | async-done | bytes 1572896 | tf_op jit(solution)/shard_map/all_to_all | solution.py:287
  124.8 0.2 shard_map.96
  125.0 7.1 %collective-permute-start.1 = (bf16[64,256]{1,0:T(8,128)(2,1)S(1)}, bf16[64,256]{1,0:T(8,128)(2,1)S(1)}, u32[]{:S(2)}, u32[]{:S(2)}) collective-permute-start(bf16[64,256]{1,0:T(8,128)(2,1)S(1)} %shard_map.96), channel_id=1, source_target_pairs={{0,0},{1,32},{2,64},{3,96},{4,128},{5,160},{6,192},{7,224},{8,256}... | collective-permute-start | bytes 98312 | tf_op jit(solution)/shard_map/ppermute | solution.py:292
  132.1 0.0 copy-done.4
  132.1 0.0 copy-done.6
  132.1 5.1 %shard_map.97 = (f32[256,512]{1,0:T(8,128)}, f32[256,512]{1,0:T(8,128)}) custom-call(bf16[16,264,512]{2,1,0:T(8,128)(2,1)} %bitcast.2, bf16[32,192,128]{2,1,0:T(8,128)(2,1)S(1)} %all-to-all-done.got_ref, bf16[32,192,128]{2,1,0:T(8,128)(2,1)S(1)} %all-to-all-done.1.shares_ref, s32[2,4]{1,0:T(2,128)S(1)} %copy-done.4, s32[2,4]{1,0:T(2,128)S(1)} %copy-done.6), custom_call_target="tpu_custom_call" | custom-call | flops 1073741824 | bytes 4194304 | tf_op jit(solution)/shard_map/pallas_call | solution.py:294
  137.3 0.0 collective-permute-done.1
  137.3 0.6 copy.11
  (4 shorter events, 0.1 us)
Async XLA Ops:
  0.6 10.9 %collective-permute-start = (bf16[128,128]{1,0:T(8,128)(2,1)}, bf16[128,128]{1,0:T(8,128)(2,1)S(1)}, u32[]{:S(2)}, u32[]{:S(2)}) collective-permute-start(bf16[128,128]{1,0:T(8,128)(2,1)} %tokens_ref.1), channel_id=1, source_target_pairs={{0,0},{1,32},{2,64},{3,96},{4,128},{5,160},{6,192},{7,224},{8,256}... | collective-permute-start | bytes 98312 | tf_op jit(solution)/shard_map/ppermute | solution.py:244
  6.7 1.0 copy-start
  7.6 0.9 copy-start.1
  8.6 0.8 copy-start.2
  9.3 0.7 copy-start.3
  10.0 0.7 copy-start.5
  13.0 56.9 %all-to-all-start = ((bf16[32,192,128]{2,1,0:T(8,128)(2,1)}), bf16[32,192,128]{2,1,0:T(8,128)(2,1)S(1)}, u32[]{:S(2)}, u32[]{:S(2)}) async-start(bf16[32,192,128]{2,1,0:T(8,128)(2,1)} %shard_map.94), calls=%async_computation | async-start | bytes 3145728 | tf_op jit(solution)/shard_map/all_to_all | solution.py:261
  67.1 2.8 %copy-start.7 = (bf16[128,512]{1,0:T(8,128)(2,1)S(1)}, bf16[128,512]{1,0:T(8,128)(2,1)}, u32[]{:S(2)}) copy-start(bf16[128,512]{1,0:T(8,128)(2,1)} %grad_ref.1) | copy-start | bytes 393220
  77.3 47.5 %all-to-all-start.1 = ((bf16[32,192,128]{2,1,0:T(8,128)(2,1)}), bf16[32,192,128]{2,1,0:T(8,128)(2,1)S(1)}, u32[]{:S(2)}, u32[]{:S(2)}) async-start(bf16[32,192,128]{2,1,0:T(8,128)(2,1)} %get-tuple-element.18), calls=%async_computation.1 | async-start | bytes 3145728 | tf_op jit(solution)/shard_map/all_to_all | solution.py:287
  118.8 13.3 %copy-start.4 = (s32[2,4]{1,0:T(2,128)S(1)}, s32[2,4]{1,0:T(2,128)}, u32[]{:S(2)}) copy-start(s32[2,4]{1,0:T(2,128)} %gate_keep.3) | copy-start | bytes 100
  118.8 13.3 %copy-start.6 = (s32[2,4]{1,0:T(2,128)S(1)}, s32[2,4]{1,0:T(2,128)}, u32[]{:S(2)}) copy-start(s32[2,4]{1,0:T(2,128)} %up_keep.3) | copy-start | bytes 100
  125.0 12.3 %collective-permute-start.1 = (bf16[64,256]{1,0:T(8,128)(2,1)S(1)}, bf16[64,256]{1,0:T(8,128)(2,1)S(1)}, u32[]{:S(2)}, u32[]{:S(2)}) collective-permute-start(bf16[64,256]{1,0:T(8,128)(2,1)S(1)} %shard_map.96), channel_id=1, source_target_pairs={{0,0},{1,32},{2,64},{3,96},{4,128},{5,160},{6,192},{7,224},{8,256}... | collective-permute-start | bytes 98312 | tf_op jit(solution)/shard_map/ppermute | solution.py:292

commit v9 on v8

--- a/solution.py
+++ b/solution.py
@@ -11,7 +11,6 @@
 EXTRA = 16
 MARKS = 8
 PARTS = 4
-SPLIT = 64
 bf16 = jnp.bfloat16
 f16 = jnp.float16
 f32 = jnp.float32
@@ -48,12 +47,9 @@
         packed_ref[2 * BLOCK :, at] = jnp.where(line == 2, power, lines).astype(bf16)
 
 
-def spread(tokens_ref, block_ref, copies_ref, one, sems):
-    count = tokens_ref.shape[0]
-    one[:count] = tokens_ref[...]
-    one[count:] = block_ref[:SPLIT]
+def spread(tokens_ref, copies_ref, sems):
     copies = [
-        pltpu.make_async_copy(one, copies_ref.at[i], sems.at[i]) for i in range(copies_ref.shape[0])
+        pltpu.make_async_copy(tokens_ref, copies_ref.at[i], sems.at[i]) for i in range(copies_ref.shape[0])
     ]
     for copy in copies:
         copy.start()
@@ -137,8 +133,8 @@
         second = jnp.where(left, pltpu.roll(upper, half, 1), lower)
         share_ref[2 * g, :BLOCK, :] = first.astype(bf16)
         share_ref[2 * g + 1, :BLOCK, :] = second.astype(bf16)
-        share_ref[2 * g, BLOCK:, :] = block_ref[SPLIT:, :]
-        share_ref[2 * g + 1, BLOCK:, :] = block_ref[SPLIT:, :]
+        share_ref[2 * g, BLOCK:, :] = block_ref[...]
+        share_ref[2 * g + 1, BLOCK:, :] = block_ref[...]
         deliver(g).start()
         return carry
 
@@ -161,7 +157,7 @@
 
 
 def weight_gradients(
-    both_ref, got_ref, shares_ref, gate_keep, up_keep, gate_ref, up_ref, columns, both, total, sems, out_sems
+    both_ref, shares_ref, gate_keep, up_keep, gate_ref, up_ref, columns, both, total, sems, out_sems
 ):
     sources, units = both_ref.shape[0], gate_ref.shape[1]
     count = columns.shape[1] // sources
@@ -178,9 +174,7 @@
             fetch(c).wait()
             back = jnp.exp2(-both[c, 2 * count : 2 * count + 1, :BLOCK].astype(f32)).astype(bf16)
             for h in range(2):
-                tile = jnp.concatenate(
-                    [got_ref[2 * c + h, count:, :], shares_ref[2 * c + h, BLOCK:, :]], axis=0
-                )
+                tile = shares_ref[2 * c + h, BLOCK:, :]
                 columns[h * BLOCK : (h + 1) * BLOCK, c * count : (c + 1) * count] = (tile * back).T
         inner = slice(p * part * count, (p + 1) * part * count)
         for n in range(0, 2 * units, step):
@@ -241,8 +235,6 @@
     route = [
         (r * cols + c, (2 * c + r % 2) * cols + r // 2) for r in range(rows) for c in range(cols)
     ]
-    block = lax.ppermute(tokens, ("row", "col"), route)
-
     packed, same = kernel(
         pack,
         [((2 * BLOCK + EXTRA, units), bf16), ((count, width), bf16)],
@@ -255,9 +247,10 @@
     packed = packed[: 2 * BLOCK + MARKS].astype(f16)
 
     (copies,) = kernel(
-        spread, [((rows, count + SPLIT, width), bf16)], "vvh", [(count + SPLIT, width)], [rows], 48, 1
-    )(same, block)
-    copies, packed = lax.optimization_barrier((copies, packed))
+        spread, [((rows, count, width), bf16)], "vh", [], [rows], 48, 1
+    )(tokens)
+    packed, same = lax.optimization_barrier((packed, same))
+    block = lax.ppermute(same, ("row", "col"), route)
     got = lax.all_to_all(copies, "row", 0, 0, tiled=True)
 
     weights = lax.all_gather(packed, "col", axis=0).astype(bf16)
@@ -267,7 +260,7 @@
         [
             ((count, units), bf16),
             ((2 * count + EXTRA, units), bf16),
-            ((rows, BLOCK + count - SPLIT, count), bf16),
+            ((rows, BLOCK + count, count), bf16),
         ],
         "vhvvvvh",
         [
@@ -275,12 +268,12 @@
             (rows * width, 2 * units),
             (count, 2 * units),
             (cols, 2 * BLOCK + MARKS, units),
-            (rows, BLOCK + count - SPLIT, count),
+            (rows, BLOCK + count, count),
             (2 * units, count),
             (f32, count, 2 * units),
         ],
         [cols, cols],
-        48,
+        50,
         8 * count * rows * width * units,
     )(got, weights, cotangent, block)
 
@@ -294,12 +287,12 @@
     grad_gate, grad_up = kernel(
         weight_gradients,
         [((2 * BLOCK, units), f32)] * 2,
-        "hvvsshh",
+        "hvsshh",
         [(2 * BLOCK, cols * count), (cols, 2 * count + MARKS, units), (f32, 2 * BLOCK, 2 * units)],
         [cols, 4],
         48,
         8 * BLOCK * cols * count * units,
-    )(both_all, got, shares, gate_keep, up_keep)
+    )(both_all, shares, gate_keep, up_keep)
     return hidden, grad_tokens, grad_gate, grad_up
 
 

time: 139 us -> 149 us (1.072)
  waiting for transfers between devices: 3.13 us -> 12 us
  starting transfers between devices: 37.9 us -> 35 us
  blocking collectives: 70.8 us -> 72.9 us
    all_to_all x1, waiting for transfers between devices: 3.12 us -> 12 us  [shards(): shares = lax.all_to_all(share, 'row', 0, 0, tiled=True)]
    all_to_all x1, starting transfers between devices: 15.2 us -> 10.5 us  [shards(): got = lax.all_to_all(copies, 'row', 0, 0, tiled=True)]
    all_to_all x1, starting transfers between devices: 9.51 us -> 12.2 us  [shards(): shares = lax.all_to_all(share, 'row', 0, 0, tiled=True)]
    all_gather x1, blocking collectives: 31.9 us -> 33.5 us  [shards(): lax.all_gather(sent[:2 * count + MARKS].astype(f16), 'col', axis=0)]
    unnamed x17 -> x19, local copies, waits for them, and re-layouts: 4.64 us -> 5.39 us
where the time goes in v9:
time: 149 us; the launch traced here: 147 us
  blocking collectives  72.9 us (49%)
  starting transfers between devices  35 us (23%)
  Pallas kernels  14.8 us (10%)
  waiting for transfers between devices  12 us (8%)
  other arithmetic  5.74 us (4%)
  local copies, waits for them, and re-layouts  5.39 us (4%)
    all_gather x1, blocking collectives, shards(): weights = lax.all_gather(packed, 'col', axis=0).astype(bf16)  39.4 us
    all_gather x1, blocking collectives, shards(): lax.all_gather(sent[:2 * count + MARKS].astype(f16), 'col', axis=0)  33.5 us
    all_to_all x1, starting transfers between devices, shards(): shares = lax.all_to_all(share, 'row', 0, 0, tiled=True)  12.2 us
    all_to_all x1, waiting for transfers between devices, shards(): shares = lax.all_to_all(share, 'row', 0, 0, tiled=True)  12 us
    all_to_all x1, starting transfers between devices, shards(): got = lax.all_to_all(copies, 'row', 0, 0, tiled=True)  10.5 us
    pallas_call x1, Pallas kernels, shards(): kernel(forward, [((count, units), bf16), ((2 * count + EXTRA, units), bf1...  7.36 us
    ppermute x1, starting transfers between devices, shards(): grad_tokens = lax.ppermute(total, ('row', 'col'), route)  6.56 us
    ppermute x1, starting transfers between devices, shards(): block = lax.ppermute(same, ('row', 'col'), route)  5.76 us
  transfers between devices with their start and end apart: 4, of which 1 were waited for; matrix products, arithmetic and copies ran while one was open for 4% of the time, Pallas kernels for 4%

profile of v9, /device:TPU:1, one launch (start us, length us, event | category | flops | bytes accessed | tf_op | source)
XLA Modules:
  0.0 146.6 jit_solution(9258286165688389960)
XLA Ops:
  0.6 0.0 copy-start.2
  0.6 0.7 copy-done.2
  1.4 1.3 shard_map.93
  2.7 10.5 %all-to-all-start = ((bf16[32,128,128]{2,1,0:T(8,128)(2,1)}), bf16[32,128,128]{2,1,0:T(8,128)(2,1)S(1)}, u32[]{:S(2)}, u32[]{:S(2)}) async-start(bf16[32,128,128]{2,1,0:T(8,128)(2,1)} %shard_map.93), calls=%async_computation | async-start | bytes 2097152 | tf_op jit(solution)/shard_map/all_to_all | solution.py:254
  13.2 0.0 copy-start
  13.2 0.9 copy-done
  14.2 0.0 copy-start.1
  14.2 0.9 copy-done.1
  15.1 0.0 copy-start.3
  15.1 0.8 copy-done.3
  15.9 0.0 copy-start.4
  15.9 0.7 copy-done.4
  16.6 0.7 copy-done.6
  17.2 0.8 shard_map.94
  18.1 5.8 %collective-permute-start = (bf16[128,128]{1,0:T(8,128)(2,1)S(1)}, bf16[128,128]{1,0:T(8,128)(2,1)S(1)}, u32[]{:S(2)}, u32[]{:S(2)}) collective-permute-start(bf16[128,128]{1,0:T(8,128)(2,1)S(1)} %get-tuple-element.16), channel_id=1, source_target_pairs={{0,0},{1,32},{2,64},{3,96},{4,128},{5,160},{6,192},{7,224},{8,256}... | collective-permute-start | bytes 98312 | tf_op jit(solution)/shard_map/ppermute | solution.py:253
  23.8 39.4 %all-gather.4 = f16[4224,512]{1,0:T(8,128)(2,1)S(1)} all-gather(f16[264,512]{1,0:T(8,128)(2,1)S(1)} %slice_convert_fusion.1), channel_id=2, replica_groups=mesh['row'=32,'col'=16] {'col'}, dimensions={0}, use_global_device_ids=true | all-gather | bytes 4595712 | tf_op jit(solution)/shard_map/all_gather | solution.py:256
  63.2 2.8 %convert_element_type.16 = bf16[4224,512]{1,0:T(8,128)(2,1)} convert(f16[4224,512]{1,0:T(8,128)(2,1)S(1)} %all-gather.4) | non-fusion elementwise | flops 2162688 | bytes 8650752 | tf_op jit(solution)/shard_map/convert_element_type | solution.py:256
  66.0 0.0 collective-permute-done.block_ref
  66.0 0.0 all-to-all-done.got_ref
  66.0 0.0 copy-done.8
  66.0 7.4 %shard_map.95 = (bf16[128,512]{1,0:T(8,128)(2,1)}, bf16[272,512]{1,0:T(8,128)(2,1)S(1)}, bf16[32,256,128]{2,1,0:T(8,128)(2,1)}) custom-call(bf16[32,128,128]{2,1,0:T(8,128)(2,1)S(1)} %all-to-all-done.got_ref, bf16[16,264,512]{2,1,0:T(8,128)(2,1)} %bitcast.3, bf16[128,512]{1,0:T(8,128)(2,1)S(1)} %copy-done.8, bf16[128,128]{1,0:T(8,128)(2,1)S(1)} %collective-permute-done.block_ref), custom_call_target="tpu_custom_call" | custom-call | flops 2147483648 | bytes 4194304 | tf_op jit(solution)/shard_map/pallas_call | solution.py:258
  73.4 12.2 %all-to-all-start.1 = ((bf16[32,256,128]{2,1,0:T(8,128)(2,1)}), bf16[32,256,128]{2,1,0:T(8,128)(2,1)S(1)}, u32[]{:S(2)}, u32[]{:S(2)}) async-start(bf16[32,256,128]{2,1,0:T(8,128)(2,1)} %get-tuple-element.18), calls=%async_computation.1 | async-start | bytes 4194304 | tf_op jit(solution)/shard_map/all_to_all | solution.py:280
  85.6 33.5 %all-gather.5 = f16[4224,512]{1,0:T(8,128)(2,1)S(1)} all-gather(f16[264,512]{1,0:T(8,128)(2,1)S(1)} %slice_convert_fusion), channel_id=3, replica_groups=mesh['row'=32,'col'=16] {'col'}, dimensions={0}, use_global_device_ids=true | all-gather | bytes 4595712 | tf_op jit(solution)/shard_map/all_gather | solution.py:282
  119.2 2.8 %convert_element_type.17 = bf16[4224,512]{1,0:T(8,128)(2,1)} convert(f16[4224,512]{1,0:T(8,128)(2,1)S(1)} %all-gather.5) | non-fusion elementwise | flops 2162688 | bytes 8650752 | tf_op jit(solution)/shard_map/convert_element_type | solution.py:282
  122.0 12.0 %all-to-all-done.1.shares_ref = bf16[32,256,128]{2,1,0:T(8,128)(2,1)S(1)} async-done(((bf16[32,256,128]{2,1,0:T(8,128)(2,1)}), bf16[32,256,128]{2,1,0:T(8,128)(2,1)S(1)}, u32[]{:S(2)}, u32[]{:S(2)}) %all-to-all-start.1) | async-done | bytes 2097184 | tf_op jit(solution)/shard_map/all_to_all | solution.py:280
  134.0 0.2 shard_map.96
  134.2 6.6 %collective-permute-start.1 = (bf16[64,256]{1,0:T(8,128)(2,1)S(1)}, bf16[64,256]{1,0:T(8,128)(2,1)S(1)}, u32[]{:S(2)}, u32[]{:S(2)}) collective-permute-start(bf16[64,256]{1,0:T(8,128)(2,1)S(1)} %shard_map.96), channel_id=1, source_target_pairs={{0,0},{1,32},{2,64},{3,96},{4,128},{5,160},{6,192},{7,224},{8,256}... | collective-permute-start | bytes 98312 | tf_op jit(solution)/shard_map/ppermute | solution.py:285
  140.8 0.0 copy-done.5
  140.8 0.0 copy-done.7
  140.8 5.2 %shard_map.97 = (f32[256,512]{1,0:T(8,128)}, f32[256,512]{1,0:T(8,128)}) custom-call(bf16[16,264,512]{2,1,0:T(8,128)(2,1)} %bitcast.2, bf16[32,256,128]{2,1,0:T(8,128)(2,1)S(1)} %all-to-all-done.1.shares_ref, s32[2,4]{1,0:T(2,128)S(1)} %copy-done.5, s32[2,4]{1,0:T(2,128)S(1)} %copy-done.7), custom_call_target="tpu_custom_call" | custom-call | flops 1073741824 | bytes 4194304 | tf_op jit(solution)/shard_map/pallas_call | solution.py:287
  145.9 0.0 collective-permute-done.1
  146.0 0.6 copy.11
  (6 shorter events, 0.1 us)
Async XLA Ops:
  0.6 0.8 copy-start.2
  2.7 63.3 %all-to-all-start = ((bf16[32,128,128]{2,1,0:T(8,128)(2,1)}), bf16[32,128,128]{2,1,0:T(8,128)(2,1)S(1)}, u32[]{:S(2)}, u32[]{:S(2)}) async-start(bf16[32,128,128]{2,1,0:T(8,128)(2,1)} %shard_map.93), calls=%async_computation | async-start | bytes 2097152 | tf_op jit(solution)/shard_map/all_to_all | solution.py:254
  13.2 1.0 copy-start
  14.2 0.9 copy-start.1
  15.1 0.8 copy-start.3
  15.9 0.7 copy-start.4
  16.6 0.7 copy-start.6
  18.1 48.0 %collective-permute-start = (bf16[128,128]{1,0:T(8,128)(2,1)S(1)}, bf16[128,128]{1,0:T(8,128)(2,1)S(1)}, u32[]{:S(2)}, u32[]{:S(2)}) collective-permute-start(bf16[128,128]{1,0:T(8,128)(2,1)S(1)} %get-tuple-element.16), channel_id=1, source_target_pairs={{0,0},{1,32},{2,64},{3,96},{4,128},{5,160},{6,192},{7,224},{8,256}... | collective-permute-start | bytes 98312 | tf_op jit(solution)/shard_map/ppermute | solution.py:253
  63.2 2.8 %copy-start.8 = (bf16[128,512]{1,0:T(8,128)(2,1)S(1)}, bf16[128,512]{1,0:T(8,128)(2,1)}, u32[]{:S(2)}) copy-start(bf16[128,512]{1,0:T(8,128)(2,1)} %grad_ref.1) | copy-start | bytes 393220
  73.4 60.6 %all-to-all-start.1 = ((bf16[32,256,128]{2,1,0:T(8,128)(2,1)}), bf16[32,256,128]{2,1,0:T(8,128)(2,1)S(1)}, u32[]{:S(2)}, u32[]{:S(2)}) async-start(bf16[32,256,128]{2,1,0:T(8,128)(2,1)} %get-tuple-element.18), calls=%async_computation.1 | async-start | bytes 4194304 | tf_op jit(solution)/shard_map/all_to_all | solution.py:280
  119.1 21.6 %copy-start.5 = (s32[2,4]{1,0:T(2,128)S(1)}, s32[2,4]{1,0:T(2,128)}, u32[]{:S(2)}) copy-start(s32[2,4]{1,0:T(2,128)} %gate_keep.3) | copy-start | bytes 100
  119.2 21.6 %copy-start.7 = (s32[2,4]{1,0:T(2,128)S(1)}, s32[2,4]{1,0:T(2,128)}, u32[]{:S(2)}) copy-start(s32[2,4]{1,0:T(2,128)} %up_keep.3) | copy-start | bytes 100
  134.2 11.8 %collective-permute-start.1 = (bf16[64,256]{1,0:T(8,128)(2,1)S(1)}, bf16[64,256]{1,0:T(8,128)(2,1)S(1)}, u32[]{:S(2)}, u32[]{:S(2)}) collective-permute-start(bf16[64,256]{1,0:T(8,128)(2,1)S(1)} %shard_map.96), channel_id=1, source_target_pairs={{0,0},{1,32},{2,64},{3,96},{4,128},{5,160},{6,192},{7,224},{8,256}... | collective-permute-start | bytes 98312 | tf_op jit(solution)/shard_map/ppermute | solution.py:285

commit v10 on v7

--- a/solution.py
+++ b/solution.py
@@ -11,7 +11,7 @@
 EXTRA = 16
 MARKS = 8
 PARTS = 4
-SPLIT = 64
+SPLIT = 80
 bf16 = jnp.bfloat16
 f16 = jnp.float16
 f32 = jnp.float32

time: 139 us -> 140 us (level)
  the two profiles are of different devices: /device:TPU:1 before, /device:TPU:33 now
where the time goes in v10:
time: 140 us
  blocking collectives  73.2 us (52%)
  starting transfers between devices  32.7 us (23%)
  Pallas kernels  13.5 us (10%)
  waiting for transfers between devices  7.77 us (6%)
  local copies, waits for them, and re-layouts  5.78 us (4%)
  other arithmetic  5.74 us (4%)
    all_gather x1, blocking collectives, shards(): weights = lax.all_gather(packed, 'col', axis=0).astype(bf16)  39.1 us
    all_gather x1, blocking collectives, shards(): lax.all_gather(sent[:2 * count + MARKS].astype(f16), 'col', axis=0)  34.1 us
    ppermute x1, starting transfers between devices, shards(): block = lax.ppermute(tokens, ('row', 'col'), route)  13.2 us
    all_to_all x1, starting transfers between devices, shards(): shares = lax.all_to_all(share, 'row', 0, 0, tiled=True)  9.21 us
    ppermute x1, waiting for transfers between devices, shards(): grad_tokens = lax.ppermute(total, ('row', 'col'), route)  7.77 us
    all_to_all x1, starting transfers between devices, shards(): got = lax.all_to_all(copies, 'row', 0, 0, tiled=True)  6.85 us
    pallas_call x1, Pallas kernels, shards(): kernel(forward, [((count, units), bf16), ((2 * count + EXTRA, units), bf1...  5.93 us
    unnamed x19, local copies, waits for them, and re-layouts  5.78 us
  transfers between devices with their start and end apart: 4, of which 1 were waited for; matrix products, arithmetic and copies ran while one was open for 4% of the time, Pallas kernels for 4%

profile of v10, /device:TPU:33, one launch (start us, length us, event | category | flops | bytes accessed | tf_op | source)
XLA Modules:
  0.0 139.5 jit_solution(6983603622094690430)
XLA Ops:
  0.6 13.2 %collective-permute-start = (bf16[128,128]{1,0:T(8,128)(2,1)}, bf16[128,128]{1,0:T(8,128)(2,1)S(1)}, u32[]{:S(2)}, u32[]{:S(2)}) collective-permute-start(bf16[128,128]{1,0:T(8,128)(2,1)} %tokens_ref.1), channel_id=1, source_target_pairs={{0,0},{1,32},{2,64},{3,96},{4,128},{5,160},{6,192},{7,224},{8,256}... | collective-permute-start | bytes 98312 | tf_op jit(solution)/shard_map/ppermute | solution.py:231
  13.8 0.0 copy-start.1
  13.8 0.9 copy-done.1
  14.8 0.0 copy-start.2
  14.8 0.9 copy-done.2
  15.7 0.0 copy-start.3
  15.7 0.8 copy-done.3
  16.5 0.0 copy-start.4
  16.5 0.7 copy-done.4
  17.2 0.7 copy-done.6
  17.9 0.8 shard_map.93
  18.7 0.0 collective-permute-done.block_ref
  18.7 1.5 %shard_map.94 = bf16[32,208,128]{2,1,0:T(8,128)(2,1)} custom-call(bf16[128,128]{1,0:T(8,128)(2,1)S(1)} %get-tuple-element.13.tokens_ref, bf16[128,128]{1,0:T(8,128)(2,1)S(1)} %collective-permute-done.block_ref), custom_call_target="tpu_custom_call" | custom-call | flops 1 | bytes 4194304 | tf_op jit(solution)/shard_map/pallas_call | solution.py:244
  20.2 6.8 %all-to-all-start = ((bf16[32,208,128]{2,1,0:T(8,128)(2,1)}), bf16[32,208,128]{2,1,0:T(8,128)(2,1)S(1)}, u32[]{:S(2)}, u32[]{:S(2)}) async-start(bf16[32,208,128]{2,1,0:T(8,128)(2,1)} %shard_map.94), calls=%async_computation | async-start | bytes 3407872 | tf_op jit(solution)/shard_map/all_to_all | solution.py:248
  27.1 39.1 %all-gather.4 = f16[4224,512]{1,0:T(8,128)(2,1)S(1)} all-gather(f16[264,512]{1,0:T(8,128)(2,1)S(1)} %slice_convert_fusion.1), channel_id=2, replica_groups=mesh['row'=32,'col'=16] {'col'}, dimensions={0}, use_global_device_ids=true | all-gather | bytes 4595712 | tf_op jit(solution)/shard_map/all_gather | solution.py:250
  66.2 2.8 %convert_element_type.16 = bf16[4224,512]{1,0:T(8,128)(2,1)} convert(f16[4224,512]{1,0:T(8,128)(2,1)S(1)} %all-gather.4) | non-fusion elementwise | flops 2162688 | bytes 8650752 | tf_op jit(solution)/shard_map/convert_element_type | solution.py:250
  69.0 0.0 all-to-all-done.got_ref
  69.0 0.0 copy-done.8
  69.0 5.9 %shard_map.95 = (bf16[128,512]{1,0:T(8,128)(2,1)}, bf16[272,512]{1,0:T(8,128)(2,1)S(1)}, bf16[32,176,128]{2,1,0:T(8,128)(2,1)S(1)}) custom-call(bf16[32,208,128]{2,1,0:T(8,128)(2,1)S(1)} %all-to-all-done.got_ref, bf16[16,264,512]{2,1,0:T(8,128)(2,1)} %bitcast.3, bf16[128,512]{1,0:T(8,128)(2,1)S(1)} %copy-done.8, ...), custom_call_target="tpu_custom_call" | custom-call | flops 2147483648 | bytes 4194304 | tf_op jit(solution)/shard_map/pallas_call | solution.py:252
  75.0 0.0 copy-start
  75.0 1.1 copy-done
  76.1 9.2 %all-to-all-start.1 = ((bf16[32,176,128]{2,1,0:T(8,128)(2,1)}), bf16[32,176,128]{2,1,0:T(8,128)(2,1)S(1)}, u32[]{:S(2)}, u32[]{:S(2)}) async-start(bf16[32,176,128]{2,1,0:T(8,128)(2,1)} %copy-done), calls=%async_computation.1 | async-start | bytes 2883584 | tf_op jit(solution)/shard_map/all_to_all | solution.py:273
  85.4 34.1 %all-gather.5 = f16[4224,512]{1,0:T(8,128)(2,1)S(1)} all-gather(f16[264,512]{1,0:T(8,128)(2,1)S(1)} %slice_convert_fusion), channel_id=3, replica_groups=mesh['row'=32,'col'=16] {'col'}, dimensions={0}, use_global_device_ids=true | all-gather | bytes 4595712 | tf_op jit(solution)/shard_map/all_gather | solution.py:275
  119.5 2.8 %convert_element_type.17 = bf16[4224,512]{1,0:T(8,128)(2,1)} convert(f16[4224,512]{1,0:T(8,128)(2,1)S(1)} %all-gather.5) | non-fusion elementwise | flops 2162688 | bytes 8650752 | tf_op jit(solution)/shard_map/convert_element_type | solution.py:275
  122.3 0.0 all-to-all-done.1.shares_ref
  122.3 0.2 shard_map.96
  122.5 3.4 %collective-permute-start.1 = (bf16[64,256]{1,0:T(8,128)(2,1)S(1)}, bf16[64,256]{1,0:T(8,128)(2,1)S(1)}, u32[]{:S(2)}, u32[]{:S(2)}) collective-permute-start(bf16[64,256]{1,0:T(8,128)(2,1)S(1)} %shard_map.96), channel_id=1, source_target_pairs={{0,0},{1,32},{2,64},{3,96},{4,128},{5,160},{6,192},{7,224},{8,256}... | collective-permute-start | bytes 98312 | tf_op jit(solution)/shard_map/ppermute | solution.py:278
  126.0 0.0 copy-done.5
  126.0 0.0 copy-done.7
  126.0 5.1 %shard_map.97 = (f32[256,512]{1,0:T(8,128)}, f32[256,512]{1,0:T(8,128)}) custom-call(bf16[16,264,512]{2,1,0:T(8,128)(2,1)} %bitcast.2, bf16[32,208,128]{2,1,0:T(8,128)(2,1)S(1)} %all-to-all-done.got_ref, bf16[32,176,128]{2,1,0:T(8,128)(2,1)S(1)} %all-to-all-done.1.shares_ref, s32[2,4]{1,0:T(2,128)S(1)} %copy-done.5, s32[2,4]{1,0:T(2,128)S(1)} %copy-done.7), custom_call_target="tpu_custom_call" | custom-call | flops 1073741824 | bytes 4194304 | tf_op jit(solution)/shard_map/pallas_call | solution.py:280
  131.1 7.8 %collective-permute-done.1 = bf16[64,256]{1,0:T(8,128)(2,1)S(1)} collective-permute-done((bf16[64,256]{1,0:T(8,128)(2,1)S(1)}, bf16[64,256]{1,0:T(8,128)(2,1)S(1)}, u32[]{:S(2)}, u32[]{:S(2)}) %collective-permute-start.1) | collective-permute-done | bytes 32800 | tf_op jit(solution)/shard_map/ppermute | solution.py:278
  138.9 0.6 copy.11
  (6 shorter events, 0.1 us)
Async XLA Ops:
  0.6 18.1 %collective-permute-start = (bf16[128,128]{1,0:T(8,128)(2,1)}, bf16[128,128]{1,0:T(8,128)(2,1)S(1)}, u32[]{:S(2)}, u32[]{:S(2)}) collective-permute-start(bf16[128,128]{1,0:T(8,128)(2,1)} %tokens_ref.1), channel_id=1, source_target_pairs={{0,0},{1,32},{2,64},{3,96},{4,128},{5,160},{6,192},{7,224},{8,256}... | collective-permute-start | bytes 98312 | tf_op jit(solution)/shard_map/ppermute | solution.py:231
  13.8 1.0 copy-start.1
  14.8 0.9 copy-start.2
  15.7 0.8 copy-start.3
  16.5 0.7 copy-start.4
  17.2 0.7 copy-start.6
  20.2 48.8 %all-to-all-start = ((bf16[32,208,128]{2,1,0:T(8,128)(2,1)}), bf16[32,208,128]{2,1,0:T(8,128)(2,1)S(1)}, u32[]{:S(2)}, u32[]{:S(2)}) async-start(bf16[32,208,128]{2,1,0:T(8,128)(2,1)} %shard_map.94), calls=%async_computation | async-start | bytes 3407872 | tf_op jit(solution)/shard_map/all_to_all | solution.py:248
  66.2 2.8 %copy-start.8 = (bf16[128,512]{1,0:T(8,128)(2,1)S(1)}, bf16[128,512]{1,0:T(8,128)(2,1)}, u32[]{:S(2)}) copy-start(bf16[128,512]{1,0:T(8,128)(2,1)} %grad_ref.1) | copy-start | bytes 393220
  75.0 1.2 copy-start
  76.1 46.2 %all-to-all-start.1 = ((bf16[32,176,128]{2,1,0:T(8,128)(2,1)}), bf16[32,176,128]{2,1,0:T(8,128)(2,1)S(1)}, u32[]{:S(2)}, u32[]{:S(2)}) async-start(bf16[32,176,128]{2,1,0:T(8,128)(2,1)} %copy-done), calls=%async_computation.1 | async-start | bytes 2883584 | tf_op jit(solution)/shard_map/all_to_all | solution.py:273
  119.5 6.5 %copy-start.5 = (s32[2,4]{1,0:T(2,128)S(1)}, s32[2,4]{1,0:T(2,128)}, u32[]{:S(2)}) copy-start(s32[2,4]{1,0:T(2,128)} %gate_keep.3) | copy-start | bytes 100
  119.5 6.5 %copy-start.7 = (s32[2,4]{1,0:T(2,128)S(1)}, s32[2,4]{1,0:T(2,128)}, u32[]{:S(2)}) copy-start(s32[2,4]{1,0:T(2,128)} %up_keep.3) | copy-start | bytes 100
  122.5 16.4 %collective-permute-start.1 = (bf16[64,256]{1,0:T(8,128)(2,1)S(1)}, bf16[64,256]{1,0:T(8,128)(2,1)S(1)}, u32[]{:S(2)}, u32[]{:S(2)}) collective-permute-start(bf16[64,256]{1,0:T(8,128)(2,1)S(1)} %shard_map.96), channel_id=1, source_target_pairs={{0,0},{1,32},{2,64},{3,96},{4,128},{5,160},{6,192},{7,224},{8,256}... | collective-permute-start | bytes 98312 | tf_op jit(solution)/shard_map/ppermute | solution.py:278
